TPU v7x, 32 devices: a whole 2x2x4 slice. The times are simulated.
32 devices in a mesh: section: 2 (over x), dp: 16 (over z, y, core).
Axes of the slice: x: 2, y: 2, z: 4, core: 2. Of those that a mesh axis runs over, the one named last changes fastest.
Arguments:
- section_input: bfloat16 [2, 64, 128, 512], P('section', 'dp'), may hold values from -6 to 6
- top_grad: bfloat16 [64, 128, 512], P('dp'), may hold values from -6 to 6
- conv_weight: bfloat16 [2, 3, 512, 512], P('section'), may hold values from -0.15625 to 0.15625
- step_table: bfloat16 [2, 50, 512], P('section'), may hold values from -4 to 4
- timesteps: int32 [64], P('dp'), may hold values from 0 to 49
- dilations: int32 [2], P('section'), may hold values from 1 to 32, as said below
Outputs:
- input_grad: bfloat16 [2, 64, 128, 512], P('section', 'dp')
- weight_grad: bfloat16 [2, 3, 512, 512], P('section')
- table_grad: bfloat16 [2, 50, 512], P('section')
Inputs may be any that keep to these rules, and one draw needn't show every extreme that they name: `dilations`: each is a power of two; some section has dilation 32 and some other section dilation 1.
All inputs are finite; a program needn't handle non-finite values.
Results may differ from a plain program's by a relative error of at most 0.014.
Values may be sent and summed in bfloat16 or wider, within the bound.
No kernel may reach another device: no remote copies, remote signals or barrier semaphores. Data moves between devices by JAX's collectives and lax.ppermute only.
A program may use at most 64 MiB of HBM per device.

v0:
```python
import math

import jax
import jax.numpy as jnp
from jax import lax
from jax.sharding import PartitionSpec as P

DMAX = 32


def from_behind(value, axis, by):
    count = lax.axis_size(axis)
    pairs = [(i, i + by) for i in range(count) if 0 <= i + by < count]
    return lax.ppermute(value, axis, pairs)


def spread_taps(seq_rows, dilation, orientation):
    bins_count = seq_rows.shape[0]
    padded = jnp.pad(seq_rows, ((DMAX, DMAX), (0, 0)))
    pieces = []
    for tap_num in range(3):
        start = DMAX + orientation * (tap_num - 1) * dilation
        pieces.append(lax.dynamic_slice_in_dim(padded, start, bins_count, 0))
    return jnp.concatenate(pieces, axis=1)


def body(section_input, top_grad, conv_weight, step_table, timesteps, dilations):
    my_section = lax.axis_index("section")
    section_count = lax.axis_size("section")
    saved_input = section_input[0]
    conv_kernel = conv_weight[0]
    emb_table = step_table[0]
    dilation = dilations[0]
    micro_count, seq_bins, channels = saved_input.shape
    flat_weight = conv_kernel.reshape(3 * channels, channels)
    onehot = timesteps[:, None] == jnp.arange(emb_table.shape[0], dtype=jnp.int32)[None, :]
    onehot_float = onehot.astype(jnp.float32)
    step_embed = jnp.dot(onehot.astype(jnp.bfloat16), emb_table, preferred_element_type=jnp.float32)

    def advance(tick_num, state_in):
        received, grads_out, weight_acc, table_acc, stash_mixed, stash_delta = state_in
        micro_pos = tick_num - (section_count - 1 - my_section)
        active = (micro_pos >= 0) & (micro_pos < micro_count)
        micro_slot = jnp.clip(micro_pos, 0, micro_count - 1)
        top_rows = lax.dynamic_index_in_dim(top_grad, micro_slot, 0, keepdims=False)
        upstream = jnp.where(my_section == section_count - 1, top_rows, received)

        def run_layer(layer_state):
            grads_keep, weight_keep, table_keep, mixed_keep, delta_keep = layer_state
            input_rows = lax.dynamic_index_in_dim(saved_input, micro_slot, 0, keepdims=False)
            embed_row = lax.dynamic_index_in_dim(step_embed, micro_slot, 0, keepdims=True)
            mixed_rows = (input_rows.astype(jnp.float32) + embed_row).astype(jnp.bfloat16)
            fwd_taps = spread_taps(mixed_rows, dilation, 1)
            preact = jnp.dot(fwd_taps, flat_weight, preferred_element_type=jnp.float32)
            gate_value = jax.nn.sigmoid(preact)
            upstream_float = upstream.astype(jnp.float32)
            grad_pre = (upstream_float * gate_value * (1.0 + preact * (1.0 - gate_value))).astype(
                jnp.bfloat16
            )
            back_taps = spread_taps(grad_pre, dilation, -1).reshape(seq_bins, 3, channels)
            grad_mixed = jnp.einsum(
                "tko,kio->ti", back_taps, conv_kernel, preferred_element_type=jnp.float32
            )
            out_rows = (upstream_float + grad_mixed).astype(jnp.bfloat16)
            grads_keep = lax.dynamic_update_index_in_dim(grads_keep, out_rows, micro_slot, 0)
            step_row = lax.dynamic_index_in_dim(onehot_float, micro_slot, 0, keepdims=False)
            table_keep = table_keep + step_row[:, None] * jnp.sum(grad_mixed, axis=0)[None, :]
            mixed_keep = lax.dynamic_update_index_in_dim(mixed_keep, mixed_rows, micro_slot, 0)
            delta_keep = lax.dynamic_update_index_in_dim(delta_keep, grad_pre, micro_slot, 0)
            return (out_rows, grads_keep, weight_keep, table_keep, mixed_keep, delta_keep)

        def skip_layer(layer_state):
            return (jnp.zeros_like(received),) + layer_state

        out_rows, grads_out, weight_acc, table_acc, stash_mixed, stash_delta = lax.cond(
            active,
            run_layer,
            skip_layer,
            (grads_out, weight_acc, table_acc, stash_mixed, stash_delta),
        )
        received = from_behind(out_rows, "section", -1)
        return (received, grads_out, weight_acc, table_acc, stash_mixed, stash_delta)

    stash_shape = (micro_count, seq_bins, channels)
    start_state = (
        jnp.zeros((seq_bins, channels), jnp.bfloat16),
        jnp.zeros((micro_count, seq_bins, channels), jnp.bfloat16),
        jnp.zeros((3 * channels, channels), jnp.float32),
        jnp.zeros(emb_table.shape, jnp.float32),
        jnp.zeros(stash_shape, jnp.bfloat16),
        jnp.zeros(stash_shape, jnp.bfloat16),
    )
    final_state = lax.fori_loop(0, section_count + micro_count - 1, advance, start_state)
    received, grads_out, weight_acc, table_acc, stash_mixed, stash_delta = final_state
    all_taps = jax.vmap(lambda one_group: spread_taps(one_group, dilation, 1))(stash_mixed)
    all_taps = all_taps.reshape(micro_count * seq_bins, 3 * channels)
    weight_acc = lax.dot_general(
        all_taps,
        stash_delta.reshape(micro_count * seq_bins, channels),
        (((0,), (0,)), ((), ())),
        preferred_element_type=jnp.float32,
    )
    grad_scale = 1.0 / math.sqrt(micro_count * lax.axis_size("dp") * seq_bins)
    weight_block = weight_acc.reshape(3, channels, channels)
    weight_total, table_total = lax.psum((weight_block, table_acc), "dp")
    weight_out = (weight_total * grad_scale).astype(jnp.bfloat16)
    table_out = (table_total * grad_scale).astype(jnp.bfloat16)
    return (grads_out[None], weight_out[None], table_out[None])


def solution(mesh):
    placed = (
        P("section", "dp", None, None),
        P("dp", None, None),
        P("section", None, None, None),
        P("section", None, None),
        P("dp"),
        P("section"),
    )
    return jax.shard_map(
        body,
        mesh=mesh,
        in_specs=placed,
        out_specs=(
            P("section", "dp", None, None),
            P("section", None, None, None),
            P("section", None, None),
        ),
        check_vma=False,
    )
```

profile of v0, /device:TPU:0, one launch (start us, length us, event | category | flops | bytes accessed | tf_op | source)
XLA Modules:
  0.0 211.1 jit_solution(1455187457926156488)
XLA Ops:
  8.0 0.8 fusion.22
  9.0 0.8 broadcast.31.clone.1
  9.9 0.8 broadcast.31
  10.7 79.1 %while.26 = (s32[]{:T(128)}, bf16[128,512]{1,0:T(8,128)(2,1)S(1)}, bf16[4,128,512]{2,1,0:T(8,128)(2,1)}, f32[50,512]{1,0:T(8,128)S(1)}, bf16[4,128,512]{2,1,0:T(...) while((s32[]{:T(128)}, bf16[128,512]{1,0:T(8,128)(2,1)S(1)}, ...), condition=%wide.region_4.5_spmd.clone, body=%wide.region_0.4_spmd.clone.sunk | while | flops 406505376 | bytes 9133023 | solution.py:93
  10.8 1.3 collective-permute-start
  12.1 15.1 %collective-permute-done = bf16[128,512]{1,0:T(8,128)(2,1)S(1)} collective-permute-done((bf16[128,512]{1,0:T(8,128)(2,1)S(1)}, bf16[128,512]{1,0:T(8,128)(2,1)S(1)}, u32[]{:S(2)}, u32[]{:S(2)}) %collective-permute-start) | collective-permute-done | bytes 131104 | tf_op jit(solution)/shard_map/while/body/eval_jaxpr/ppermute | solution.py:14
  27.3 8.7 %conditional.3 = (bf16[128,512]{1,0:T(8,128)(2,1)S(1)}, bf16[4,128,512]{2,1,0:T(8,128)(2,1)}, f32[50,512]{1,0:T(8,128)S(1)}, bf16[4,128,512]{2,1,0:T(8,128)(2,1)S(1)}, bf16[4,128,512]{2,1,0:T(8,128)(2,1)}) conditional(s32[]{:T(128)} %convert_element_type.114, (bf16[4,128,512]{2,1,0:T(8,128)(2,1)}, f32[50,512]{1,0:T(8,128)S(1)}, ...), branch_computations={%region_1.1_spmd, %region_2.3_spmd} | conditional | flops 406504960 | bytes 8607532 | solution.py:75
  29.3 0.9 fusion.12
  30.2 0.1 pad_dynamic-slice_fusion.3
  30.3 2.0 bitcast_dynamic-update-slice_fusion
  32.5 0.2 copy.11
  32.7 0.9 fusion.16
  33.6 2.2 %bitcast_dynamic-update-slice_fusion.1 = (bf16[4,128,512]{2,1,0:T(8,128)(2,1)}, bf16[128,512]{1,0:T(8,128)(2,1)S(1)}, f32[128,512]{1,0:T(8,128)S(1)}) fusion(bf16[4,128,512]{2,1,0:T(8,128)(2,1)} %get-tuple-element.469, s32[]{:T(128)S(6)} %min.11, bf16[128,512]{1,0:T(8,128)(2,1)S(1)} %get-tuple-element.463, bf16[4,128,512]{2,1,0:T(8,128)(2,1)} %get-tuple-element.461, ...), kind=kOutput, calls=%fused_computation.25 | convolution fusion | flops 201588736 | bytes 2753028 | tf_op jit(solution)/shard_map/while/body/eval_jaxpr/cond/branch_1_fun/tko,kio->ti/dot_general | solution.py:61
  36.0 1.3 collective-permute-start
  37.3 5.6 %collective-permute-done = bf16[128,512]{1,0:T(8,128)(2,1)S(1)} collective-permute-done((bf16[128,512]{1,0:T(8,128)(2,1)S(1)}, bf16[128,512]{1,0:T(8,128)(2,1)S(1)}, u32[]{:S(2)}, u32[]{:S(2)}) %collective-permute-start) | collective-permute-done | bytes 131104 | tf_op jit(solution)/shard_map/while/body/eval_jaxpr/ppermute | solution.py:14
  42.9 8.7 %conditional.3 = (bf16[128,512]{1,0:T(8,128)(2,1)S(1)}, bf16[4,128,512]{2,1,0:T(8,128)(2,1)}, f32[50,512]{1,0:T(8,128)S(1)}, bf16[4,128,512]{2,1,0:T(8,128)(2,1)S(1)}, bf16[4,128,512]{2,1,0:T(8,128)(2,1)}) conditional(s32[]{:T(128)} %convert_element_type.114, (bf16[4,128,512]{2,1,0:T(8,128)(2,1)}, f32[50,512]{1,0:T(8,128)S(1)}, ...), branch_computations={%region_1.1_spmd, %region_2.3_spmd} | conditional | flops 406504960 | bytes 8607532 | solution.py:75
  44.9 0.9 fusion.12
  45.9 0.1 pad_dynamic-slice_fusion.3
  46.0 2.0 bitcast_dynamic-update-slice_fusion
  48.1 0.2 copy.11
  48.4 0.9 fusion.16
  49.3 2.2 %bitcast_dynamic-update-slice_fusion.1 = (bf16[4,128,512]{2,1,0:T(8,128)(2,1)}, bf16[128,512]{1,0:T(8,128)(2,1)S(1)}, f32[128,512]{1,0:T(8,128)S(1)}) fusion(bf16[4,128,512]{2,1,0:T(8,128)(2,1)} %get-tuple-element.469, s32[]{:T(128)S(6)} %min.11, bf16[128,512]{1,0:T(8,128)(2,1)S(1)} %get-tuple-element.463, bf16[4,128,512]{2,1,0:T(8,128)(2,1)} %get-tuple-element.461, ...), kind=kOutput, calls=%fused_computation.25 | convolution fusion | flops 201588736 | bytes 2753028 | tf_op jit(solution)/shard_map/while/body/eval_jaxpr/cond/branch_1_fun/tko,kio->ti/dot_general | solution.py:61
  51.7 1.3 collective-permute-start
  53.0 5.6 %collective-permute-done = bf16[128,512]{1,0:T(8,128)(2,1)S(1)} collective-permute-done((bf16[128,512]{1,0:T(8,128)(2,1)S(1)}, bf16[128,512]{1,0:T(8,128)(2,1)S(1)}, u32[]{:S(2)}, u32[]{:S(2)}) %collective-permute-start) | collective-permute-done | bytes 131104 | tf_op jit(solution)/shard_map/while/body/eval_jaxpr/ppermute | solution.py:14
  58.6 8.7 %conditional.3 = (bf16[128,512]{1,0:T(8,128)(2,1)S(1)}, bf16[4,128,512]{2,1,0:T(8,128)(2,1)}, f32[50,512]{1,0:T(8,128)S(1)}, bf16[4,128,512]{2,1,0:T(8,128)(2,1)S(1)}, bf16[4,128,512]{2,1,0:T(8,128)(2,1)}) conditional(s32[]{:T(128)} %convert_element_type.114, (bf16[4,128,512]{2,1,0:T(8,128)(2,1)}, f32[50,512]{1,0:T(8,128)S(1)}, ...), branch_computations={%region_1.1_spmd, %region_2.3_spmd} | conditional | flops 406504960 | bytes 8607532 | solution.py:75
  60.6 0.9 fusion.12
  61.6 2.0 bitcast_dynamic-update-slice_fusion
  63.8 0.2 copy.11
  64.0 0.9 fusion.16
  64.9 2.2 %bitcast_dynamic-update-slice_fusion.1 = (bf16[4,128,512]{2,1,0:T(8,128)(2,1)}, bf16[128,512]{1,0:T(8,128)(2,1)S(1)}, f32[128,512]{1,0:T(8,128)S(1)}) fusion(bf16[4,128,512]{2,1,0:T(8,128)(2,1)} %get-tuple-element.469, s32[]{:T(128)S(6)} %min.11, bf16[128,512]{1,0:T(8,128)(2,1)S(1)} %get-tuple-element.463, bf16[4,128,512]{2,1,0:T(8,128)(2,1)} %get-tuple-element.461, ...), kind=kOutput, calls=%fused_computation.25 | convolution fusion | flops 201588736 | bytes 2753028 | tf_op jit(solution)/shard_map/while/body/eval_jaxpr/cond/branch_1_fun/tko,kio->ti/dot_general | solution.py:61
  67.3 1.3 collective-permute-start
  68.6 5.6 %collective-permute-done = bf16[128,512]{1,0:T(8,128)(2,1)S(1)} collective-permute-done((bf16[128,512]{1,0:T(8,128)(2,1)S(1)}, bf16[128,512]{1,0:T(8,128)(2,1)S(1)}, u32[]{:S(2)}, u32[]{:S(2)}) %collective-permute-start) | collective-permute-done | bytes 131104 | tf_op jit(solution)/shard_map/while/body/eval_jaxpr/ppermute | solution.py:14
  74.2 8.7 %conditional.3 = (bf16[128,512]{1,0:T(8,128)(2,1)S(1)}, bf16[4,128,512]{2,1,0:T(8,128)(2,1)}, f32[50,512]{1,0:T(8,128)S(1)}, bf16[4,128,512]{2,1,0:T(8,128)(2,1)S(1)}, bf16[4,128,512]{2,1,0:T(8,128)(2,1)}) conditional(s32[]{:T(128)} %convert_element_type.114, (bf16[4,128,512]{2,1,0:T(8,128)(2,1)}, f32[50,512]{1,0:T(8,128)S(1)}, ...), branch_computations={%region_1.1_spmd, %region_2.3_spmd} | conditional | flops 406504960 | bytes 8607532 | solution.py:75
  76.2 0.9 fusion.12
  77.3 2.0 bitcast_dynamic-update-slice_fusion
  79.4 0.2 copy.11
  79.7 0.9 fusion.16
  80.6 2.2 %bitcast_dynamic-update-slice_fusion.1 = (bf16[4,128,512]{2,1,0:T(8,128)(2,1)}, bf16[128,512]{1,0:T(8,128)(2,1)S(1)}, f32[128,512]{1,0:T(8,128)S(1)}) fusion(bf16[4,128,512]{2,1,0:T(8,128)(2,1)} %get-tuple-element.469, s32[]{:T(128)S(6)} %min.11, bf16[128,512]{1,0:T(8,128)(2,1)S(1)} %get-tuple-element.463, bf16[4,128,512]{2,1,0:T(8,128)(2,1)} %get-tuple-element.461, ...), kind=kOutput, calls=%fused_computation.25 | convolution fusion | flops 201588736 | bytes 2753028 | tf_op jit(solution)/shard_map/while/body/eval_jaxpr/cond/branch_1_fun/tko,kio->ti/dot_general | solution.py:61
  83.0 1.3 collective-permute-start
  84.3 5.6 %collective-permute-done = bf16[128,512]{1,0:T(8,128)(2,1)S(1)} collective-permute-done((bf16[128,512]{1,0:T(8,128)(2,1)S(1)}, bf16[128,512]{1,0:T(8,128)(2,1)S(1)}, u32[]{:S(2)}, u32[]{:S(2)}) %collective-permute-start) | collective-permute-done | bytes 131104 | tf_op jit(solution)/shard_map/while/body/eval_jaxpr/ppermute | solution.py:14
  89.8 0.3 pad_dynamic-slice_fusion.5
  90.2 0.1 pad_maximum_fusion.1
  90.3 0.2 copy-done.2
  90.5 0.7 copy.13
  91.2 3.7 %fusion.28 = f32[3,512,512]{2,1,0:T(8,128)} fusion(bf16[3,512,512]{2,1,0:T(8,128)(2,1)S(1)} %bitcast.67, bf16[512,512,1]{1,0,2:T(8,128)(2,1)} %bitcast.69), kind=kOutput, calls=%fused_computation.49 | convolution fusion | flops 805306368 | bytes 5242880 | tf_op jit(solution)/shard_map/dot_general | solution.py:97
  94.9 105.2 %all-reduce.6.cloned.1.call-done = (f32[3,512,512]{2,1,0:T(8,128)}, f32[50,512]{1,0:T(8,128)}) async-done(((f32[3,512,512]{2,1,0:T(8,128)}, f32[50,512]{1,0:T(8,128)}), (f32[3,512,512]{2,1,0:T(8,128)}, f32[50,512]{1,0:T(8,128)})) %all-reduce.6.cloned.1.call-update) | async-done | bytes 3248144 | tf_op jit(solution)/shard_map/psum | solution.py:105
  200.1 3.5 %fusion.20 = bf16[1,3,512,512]{3,2,1,0:T(8,128)(2,1)} fusion(f32[3,512,512]{2,1,0:T(8,128)} %get-tuple-element.596), kind=kLoop, calls=%fused_computation.35 | loop fusion | flops 1572864 | bytes 4718592 | tf_op jit(solution)/shard_map/broadcast_in_dim | solution.py:108
  203.6 0.6 fusion.21
  (48 shorter events, 1.8 us)
Async XLA Ops:
  7.2 0.9 copy-start
  7.2 3.5 %copy-start.4 = (s32[4]{0:T(128)S(1)}, s32[4]{0:T(128)}, u32[]{:S(2)}) copy-start(s32[4]{0:T(128)} %param.14) | copy-start | bytes 52
  7.2 3.5 %copy-start.1 = (bf16[1,3,512,512]{3,2,1,0:T(8,128)(2,1)S(1)}, bf16[1,3,512,512]{3,2,1,0:T(8,128)(2,1)}, u32[]{:S(2)}) copy-start(bf16[1,3,512,512]{3,2,1,0:T(8,128)(2,1)} %param.12) | copy-start | bytes 4718596
  7.2 192.9 %all-reduce.6.cloned.1.call-start = ((), (), s32[]{:S(2)}) async-start(), calls=%async_computation | async-start | bytes 6520832 | tf_op jit(solution)/shard_map/psum | solution.py:105
  10.8 16.4 %collective-permute-start = (bf16[128,512]{1,0:T(8,128)(2,1)S(1)}, bf16[128,512]{1,0:T(8,128)(2,1)S(1)}, u32[]{:S(2)}, u32[]{:S(2)}) collective-permute-start(bf16[128,512]{1,0:T(8,128)(2,1)S(1)} %get-tuple-element.707), channel_id=1, source_target_pairs={{16,0},{17,1},{18,2},{19,3},{20,4},{21,5},{22,6},{23,7},{24,8},{25... | collective-permute-start | bytes 393224 | tf_op jit(solution)/shard_map/while/body/eval_jaxpr/ppermute | solution.py:14
  36.0 6.9 %collective-permute-start = (bf16[128,512]{1,0:T(8,128)(2,1)S(1)}, bf16[128,512]{1,0:T(8,128)(2,1)S(1)}, u32[]{:S(2)}, u32[]{:S(2)}) collective-permute-start(bf16[128,512]{1,0:T(8,128)(2,1)S(1)} %get-tuple-element.707), channel_id=1, source_target_pairs={{16,0},{17,1},{18,2},{19,3},{20,4},{21,5},{22,6},{23,7},{24,8},{25... | collective-permute-start | bytes 393224 | tf_op jit(solution)/shard_map/while/body/eval_jaxpr/ppermute | solution.py:14
  51.7 6.9 %collective-permute-start = (bf16[128,512]{1,0:T(8,128)(2,1)S(1)}, bf16[128,512]{1,0:T(8,128)(2,1)S(1)}, u32[]{:S(2)}, u32[]{:S(2)}) collective-permute-start(bf16[128,512]{1,0:T(8,128)(2,1)S(1)} %get-tuple-element.707), channel_id=1, source_target_pairs={{16,0},{17,1},{18,2},{19,3},{20,4},{21,5},{22,6},{23,7},{24,8},{25... | collective-permute-start | bytes 393224 | tf_op jit(solution)/shard_map/while/body/eval_jaxpr/ppermute | solution.py:14
  67.3 6.9 %collective-permute-start = (bf16[128,512]{1,0:T(8,128)(2,1)S(1)}, bf16[128,512]{1,0:T(8,128)(2,1)S(1)}, u32[]{:S(2)}, u32[]{:S(2)}) collective-permute-start(bf16[128,512]{1,0:T(8,128)(2,1)S(1)} %get-tuple-element.707), channel_id=1, source_target_pairs={{16,0},{17,1},{18,2},{19,3},{20,4},{21,5},{22,6},{23,7},{24,8},{25... | collective-permute-start | bytes 393224 | tf_op jit(solution)/shard_map/while/body/eval_jaxpr/ppermute | solution.py:14
  83.0 6.9 %collective-permute-start = (bf16[128,512]{1,0:T(8,128)(2,1)S(1)}, bf16[128,512]{1,0:T(8,128)(2,1)S(1)}, u32[]{:S(2)}, u32[]{:S(2)}) collective-permute-start(bf16[128,512]{1,0:T(8,128)(2,1)S(1)} %get-tuple-element.707), channel_id=1, source_target_pairs={{16,0},{17,1},{18,2},{19,3},{20,4},{21,5},{22,6},{23,7},{24,8},{25... | collective-permute-start | bytes 393224 | tf_op jit(solution)/shard_map/while/body/eval_jaxpr/ppermute | solution.py:14
  89.8 0.6 copy-start.2
  200.1 3.5 %copy-start.3 = (f32[50,512]{1,0:T(8,128)S(1)}, f32[50,512]{1,0:T(8,128)}, u32[]{:S(2)}) copy-start(f32[50,512]{1,0:T(8,128)} %get-tuple-element.597) | copy-start | bytes 307204
Sparse Core Ops, SparseCore 0:
  95.0 105.0 all-reduce.5
where the time goes:
time: 212 us; the launch traced here: 211 us
  waiting for transfers between devices  143 us (67%)
  matrix products  21.6 us (10%)
  between operations  14.9 us (7%)
  other arithmetic  12.7 us (6%)
  loops' own time  8.18 us (4%)
  starting transfers between devices  6.5 us (3%)
  local copies, waits for them, and re-layouts  4.68 us (2%)
    psum x1, waiting for transfers between devices, body(): weight_total, table_total = lax.psum((weight_block, table_acc), 'dp')  105 us
    ppermute x5, waiting for transfers between devices, from_behind(): return lax.ppermute(value, axis, pairs)  37.3 us
    dot_general x4, matrix products, run_layer(): jnp.einsum('tko,kio->ti', back_taps, conv_kernel, preferred_element_type=...  8.89 us
    dot_general x4, matrix products, run_layer(): preact = jnp.dot(fwd_taps, flat_weight, preferred_element_type=jnp.float32)  8.12 us
    another operation x5, loops' own time, advance(): lax.cond(active, run_layer, skip_layer, (grads_out, weight_acc, table_acc...  8.08 us
    ppermute x5, starting transfers between devices, from_behind(): return lax.ppermute(value, axis, pairs)  6.46 us
  transfers between devices with their start and end apart: 6, of which 6 were waited for; matrix products, arithmetic and copies ran while one was open for 0% of the time, Pallas kernels for 0%

commit v1 on v0

v1 whole, which is shorter than its diff:
```python
import functools
import math

import jax
import jax.numpy as jnp
from jax import lax
from jax.experimental import pallas as pl
from jax.experimental.pallas import tpu as pltpu
from jax.sharding import PartitionSpec as P

CHUNKS = 2
F32 = jnp.float32
BF16 = jnp.bfloat16
VMEM = pl.BlockSpec(memory_space=pltpu.VMEM)
SMEM = pl.BlockSpec(memory_space=pltpu.SMEM)
NT = (((1,), (1,)), ((), ()))


def call(kernel, out_shape, args, smem=0, scratch=(), flops=0, aliases=None):
    specs = [SMEM] * smem + [VMEM] * (len(args) - smem)
    moved = sum(a.size * a.dtype.itemsize for a in args)
    moved += sum(math.prod(o.shape) * o.dtype.itemsize for o in out_shape)
    return pl.pallas_call(
        kernel,
        out_shape=out_shape,
        in_specs=specs,
        out_specs=[VMEM] * len(out_shape),
        scratch_shapes=list(scratch),
        input_output_aliases=aliases or {},
        compiler_params=pltpu.CompilerParams(vmem_limit_bytes=48 * 2**20),
        cost_estimate=pl.CostEstimate(flops=flops, bytes_accessed=moved, transcendentals=0),
    )(*args)


def like(shape, dtype):
    return jax.ShapeDtypeStruct(shape, dtype)


def put_taps(values, taps, bins, dilation, orientation):
    rows, cols = values.shape
    place = lax.broadcasted_iota(jnp.int32, (bins, cols), 0)
    taps[:, cols : 2 * cols] = values
    for b in range(rows // bins):
        at = slice(b * bins, (b + 1) * bins)
        group = values[at].astype(F32)
        later = pltpu.roll(group, bins - dilation, 0)
        later = jnp.where(place < bins - dilation, later, 0.0).astype(BF16)
        earlier = pltpu.roll(group, dilation, 0)
        earlier = jnp.where(place >= dilation, earlier, 0.0).astype(BF16)
        first, third = (earlier, later) if orientation == 1 else (later, earlier)
        taps[at, 0:cols] = first
        taps[at, 2 * cols : 3 * cols] = third


def back_product(taps, weight, cols):
    total = None
    for k in range(3):
        part = lax.dot_general(
            taps[:, k * cols : (k + 1) * cols], weight[k], NT, preferred_element_type=F32
        )
        total = part if total is None else total + part
    return total


def first_kernel(ts, dil, x, table, weight, top, slope, h_t, *rest):
    g_out, (taps, tab) = rest[:-2], rest[-2:]
    groups, bins, chans = x.shape
    dilation = dil[0]
    tab[...] = table[...].astype(F32)
    mixed = [
        (x[b].astype(F32) + tab[pl.ds(ts[b], 1), :]).astype(BF16) for b in range(groups)
    ]
    mixed = jnp.concatenate(mixed, axis=0)
    put_taps(mixed, taps, bins, dilation, 1)
    flat = weight[...].reshape(3 * chans, chans)
    y = jnp.dot(taps[...], flat, preferred_element_type=F32)
    gate = jax.nn.sigmoid(y)
    slope[...] = gate * (1.0 + y * (1.0 - gate))
    g = top[...].reshape(groups * bins, chans).astype(F32)
    delta = (g * slope[...]).astype(BF16)
    put_taps(delta, taps, bins, dilation, -1)
    out = (g + back_product(taps, weight, chans)).astype(BF16)
    width = chans // len(g_out)
    for j, ref in enumerate(g_out):
        ref[...] = out[:, j * width : (j + 1) * width]
    h_t[...] = mixed.T


def layer_kernel(bins, dil, slope, weight, g_in, *rest):
    g_out, taps = rest[:-1], rest[-1]
    chans = slope.shape[1]
    g = g_in[...].astype(F32)
    delta = (g * slope[...]).astype(BF16)
    put_taps(delta, taps, bins, dil[0], -1)
    out = (g + back_product(taps, weight, chans)).astype(BF16)
    width = chans // len(g_out)
    for j, ref in enumerate(g_out):
        ref[...] = out[:, j * width : (j + 1) * width]


def weight_kernel(col, scale, flags, dil, top, recv, slope, h_t, g_used, taps, send, keep):
    rows, width = recv.shape
    bins = top.shape[1]
    at_top = flags[0] == 1
    bit = flags[1]
    fresh = top[...].reshape(rows, top.shape[-1])[:, col : col + width]
    g = jnp.where(at_top, fresh.astype(F32), recv[...].astype(F32))
    g_used[...] = g.astype(BF16)
    delta = (g * slope[:, col : col + width]).astype(BF16)
    put_taps(delta, taps, bins, dil[0], -1)
    half = h_t.shape[0] // 2
    for ref, part in ((send, 1 - bit), (keep, bit)):
        left = h_t[pl.ds(pl.multiple_of(part * half, half), half), :]
        prod = jnp.dot(left, taps[...], preferred_element_type=F32)
        ref[:, 0 : 3 * width] = (prod * scale).astype(BF16)


def back_kernel(col, taps, weight, acc):
    width = taps.shape[1] // 3
    acc[...] = back_product(taps, weight[:, :, col : col + width], width)


def last_kernel(
    col, scale, flags, dil, ts, top, recv, slope, h_t, weight, *rest
):
    prior = (len(rest) - 4) // 2
    g_prior, acc = rest[:prior], rest[prior : 2 * prior]
    send, keep, grad, taps = rest[2 * prior :]
    rows, width = recv.shape
    groups, bins, chans = grad.shape
    at_top = flags[0] == 1
    bit = flags[1]
    fresh = top[...].reshape(rows, chans)[:, col : col + width]
    g = jnp.where(at_top, fresh.astype(F32), recv[...].astype(F32))
    delta = (g * slope[:, col : col + width]).astype(BF16)
    put_taps(delta, taps, bins, dil[0], -1)
    dh = back_product(taps, weight[:, :, col : col + width], width)
    for ref in acc:
        dh = dh + ref[...]
    whole = jnp.concatenate([ref[...].astype(F32) for ref in g_prior] + [g], axis=1)
    grad[...] = (whole + dh).astype(BF16).reshape(groups, bins, chans)
    steps = lax.broadcasted_iota(jnp.int32, (128, chans), 0)
    table = jnp.zeros((128, chans), F32)
    for b in range(groups):
        total = jnp.sum(dh[b * bins : (b + 1) * bins], axis=0, keepdims=True)
        table = table + jnp.where(steps == ts[b], total * scale, 0.0)
    table_t = table.T.astype(BF16)
    half = h_t.shape[0] // 2
    for ref, part in ((send, 1 - bit), (keep, bit)):
        left = h_t[pl.ds(pl.multiple_of(part * half, half), half), :]
        prod = jnp.dot(left, taps[...], preferred_element_type=F32)
        ref[:, 0 : 3 * width] = (prod * scale).astype(BF16)
    for ref, part in ((send, 1 - bit), (keep, bit)):
        first = table_t[0:half]
        second = table_t[half : 2 * half]
        ref[:, 3 * width :] = jnp.where(part == 0, first, second)


def fold_kernel(flags, pos, keep, recv, send_out, keep_out):
    half = keep.shape[0] // 2
    for ref, part in ((send_out, 1 - flags[pos]), (keep_out, flags[pos])):
        at = pl.ds(pl.multiple_of(part * half, half), half)
        ref[...] = (keep[at, :].astype(F32) + recv[at, :].astype(F32)).astype(BF16)


def swap(value, bit_num):
    count = lax.axis_size("dp")
    return lax.ppermute(value, "dp", [(i, i ^ (1 << bit_num)) for i in range(count)])


def body(section_input, top_grad, conv_weight, step_table, timesteps, dilations):
    my_section = lax.axis_index("section")
    section_count = lax.axis_size("section")
    dp_count = lax.axis_size("dp")
    dp_bits = dp_count.bit_length() - 1
    me = lax.axis_index("dp")
    x = section_input[0]
    weight = conv_weight[0]
    table = step_table[0]
    groups, bins, chans = x.shape
    rows = groups * bins
    width = chans // CHUNKS
    scale = 1.0 / math.sqrt(groups * dp_count * bins)
    is_top = (my_section == section_count - 1).astype(jnp.int32)
    flags = jnp.stack([is_top] + [(me >> n) & 1 for n in range(dp_bits)]).astype(jnp.int32)
    unit = 2 * rows * chans * chans * 3

    slices = [like((rows, width), BF16)] * CHUNKS
    whole = [like((rows, chans), BF16)]
    ticks = section_count - 1
    slope, h_t, *sent = call(
        first_kernel,
        [like((rows, chans), F32), like((chans, rows), BF16)] + (slices if ticks <= 1 else whole),
        (timesteps, dilations, x, table, weight, top_grad),
        smem=2,
        scratch=[
            pltpu.VMEM((rows, 3 * chans), BF16),
            pltpu.VMEM(table.shape, F32),
        ],
        flops=2 * unit,
    )

    def below(value):
        return lax.ppermute(value, "section", [(i, i - 1) for i in range(1, section_count)])

    for tick in range(1, ticks):
        got = jnp.where(is_top == 1, top_grad.reshape(rows, chans), below(sent[0]))
        sent = call(
            functools.partial(layer_kernel, bins),
            slices if tick == ticks - 1 else whole,
            (dilations, slope, weight, got),
            smem=1,
            scratch=[pltpu.VMEM((rows, 3 * chans), BF16)],
            flops=unit,
        )
    got = [below(value) for value in sent]

    halves = []
    g_used = []
    accs = []
    for c in range(CHUNKS):
        if c < CHUNKS - 1:
            used, taps, send, keep = call(
                functools.partial(weight_kernel, c * width, scale),
                [like((rows, width), BF16), like((rows, 3 * width), BF16)]
                + [like((chans // 2, 3 * width), BF16)] * 2,
                (flags, dilations, top_grad, got[c], slope, h_t),
                smem=2,
                flops=unit // CHUNKS,
            )
            acc = call(
                functools.partial(back_kernel, c * width),
                [like((rows, chans), F32)],
                (taps, weight),
                flops=unit // CHUNKS,
            )[0]
            g_used.append(used)
            accs.append(acc)
        else:
            send, keep, grad = call(
                functools.partial(last_kernel, c * width, scale),
                [like((chans // 2, 3 * width + 128), BF16)] * 2 + [like(x.shape, BF16)],
                (flags, dilations, timesteps, top_grad, got[c], slope, h_t, weight)
                + tuple(g_used)
                + tuple(accs),
                smem=3,
                scratch=[pltpu.VMEM((rows, 3 * width), BF16)],
                flops=2 * unit // CHUNKS,
            )
        halves.append((send, keep))

    order = None
    counts = []
    pieces = []
    for send, keep in halves:
        cols = keep.shape[1]
        for n in range(1, dp_bits - 1):
            recv = swap(send, n - 1)
            half = [like((keep.shape[0] // 2, cols), BF16)] * 2
            fold = lambda flags_ref, *refs, pos=1 + n: fold_kernel(flags_ref, pos, *refs)
            send, keep = call(fold, half, (flags, keep, recv), smem=1)
        keep = (keep.astype(F32) + swap(send, dp_bits - 2).astype(F32)).astype(BF16)
        own = (keep.astype(F32) + swap(keep, dp_bits - 1).astype(F32)).astype(BF16)
        held = [(own, [0])]
        for n in range(dp_bits - 2, 0, -1):
            message = jnp.concatenate([v for v, _ in held], axis=0) if len(held) > 1 else held[0][0]
            offsets = [o for _, offs in held for o in offs]
            held.append((swap(message, n), [o ^ (1 << n) for o in offsets]))
        held = held + [(swap(v, 0), [o ^ 1 for o in offs]) for v, offs in held]
        pieces += [v for v, _ in held]
        order = [offs for _, offs in held]
        counts.append(len(held))

    weight_out, table_t = call(
        lambda flags_ref, *refs: assemble_kernel(order, counts, dp_bits, flags_ref, *refs),
        [like(weight.shape, BF16), like((chans, 128), BF16)],
        (flags,) + tuple(pieces),
        smem=1,
    )
    table_out = table_t.T[: table.shape[0]]
    return (grad[None], weight_out[None], table_out[None])


def assemble_kernel(order, counts, dp_bits, flags, *refs):
    weight_out, table_out = refs[-2], refs[-1]
    pieces = refs[:-2]
    chans = weight_out.shape[1]
    width = chans // len(counts)
    at = 0
    for c, count in enumerate(counts):
        for n in range(count):
            ref = pieces[at]
            at += 1
            size = ref.shape[0] // len(order[n])
            for slot, offset in enumerate(order[n]):
                block = 0
                for bit_num in range(dp_bits - 1):
                    bit = flags[1 + bit_num]
                    block = block * 2 + (1 - bit if (offset >> bit_num) & 1 else bit)
                row = pl.ds(pl.multiple_of(block * size, size), size)
                here = slice(slot * size, (slot + 1) * size)
                for k in range(3):
                    weight_out[k, row, c * width : (c + 1) * width] = ref[
                        here, k * width : (k + 1) * width
                    ]
                if ref.shape[1] > 3 * width:
                    table_out[row, :] = ref[here, 3 * width :]


def solution(mesh):
    placed = (
        P("section", "dp", None, None),
        P("dp", None, None),
        P("section", None, None, None),
        P("section", None, None),
        P("dp"),
        P("section"),
    )
    return jax.shard_map(
        body,
        mesh=mesh,
        in_specs=placed,
        out_specs=(
            P("section", "dp", None, None),
            P("section", None, None, None),
            P("section", None, None),
        ),
        check_vma=False,
    )
```

time: 212 us -> 76.4 us (0.36)
  waiting for transfers between devices: 143 us -> 32.7 us
  matrix products: 21.6 us -> 0 us
  starting transfers between devices: 6.5 us -> 20.5 us
  Pallas kernels: 0 us -> 13.6 us
  between operations: 14.9 us -> 1.44 us
  other arithmetic: 12.7 us -> 0.15 us
  loops' own time: 8.18 us -> 0 us
  local copies, waits for them, and re-layouts: 4.68 us -> 7.66 us
    psum x1 -> x0, waiting for transfers between devices: 105 us -> none  [body(): weight_total, table_total = lax.psum((weight_block, table_acc), 'dp')]
    dot_general x10 -> x0, matrix products: 21.6 us -> none  [the longest x4 8.89 us: run_layer(): jnp.einsum('tko,kio->ti', back_taps, conv_kernel, preferred_element_type=...]
    ppermute x5 -> x20, starting transfers between devices: 6.46 us -> 20.5 us  [the longest x18 17.8 us: swap(): lax.ppermute(value, 'dp', [(i, i ^ 1 << bit_num) for i in range(count)])]
    pallas_call x0 -> x9, Pallas kernels: none -> 13.6 us  [call(): pl.pallas_call(kernel, out_shape=out_shape, in_specs=specs, out_specs=[VM...]
    another operation x6 -> x0, loops' own time: 8.18 us -> none  [the longest x5 8.08 us: advance(): lax.cond(active, run_layer, skip_layer, (grads_out, weight_acc, table_acc...]
    unnamed x10 -> x23, local copies, waits for them, and re-layouts: 0.19 us -> 7.56 us
    ppermute x5 -> x20, waiting for transfers between devices: 37.3 us -> 32.7 us  [the longest x18 22.6 us: swap(): lax.ppermute(value, 'dp', [(i, i ^ 1 << bit_num) for i in range(count)])]
    broadcast_in_dim x2 -> x0, other arithmetic: 4.13 us -> none  [body(): return (grads_out[None], weight_out[None], table_out[None])]
  transfers between devices with their start and end apart: 6 -> 20, of which waited for: 6 -> 12; matrix products, arithmetic and copies ran while one was open for 0% -> 0% of each run, Pallas kernels for 0% -> 7%
where the time goes in v1:
time: 76.4 us; the launch traced here: 76 us
  waiting for transfers between devices  32.7 us (43%)
  starting transfers between devices  20.5 us (27%)
  Pallas kernels  13.6 us (18%)
  local copies, waits for them, and re-layouts  7.66 us (10%)
  between operations  1.44 us (2%)
    ppermute x18, waiting for transfers between devices, swap(): lax.ppermute(value, 'dp', [(i, i ^ 1 << bit_num) for i in range(count)])  22.6 us
    ppermute x18, starting transfers between devices, swap(): lax.ppermute(value, 'dp', [(i, i ^ 1 << bit_num) for i in range(count)])  17.8 us
    pallas_call x9, Pallas kernels, call(): pl.pallas_call(kernel, out_shape=out_shape, in_specs=specs, out_specs=[VM...  13.6 us
    ppermute x2, waiting for transfers between devices, below(): lax.ppermute(value, 'section', [(i, i - 1) for i in range(1, section_coun...  10 us
    unnamed x23, local copies, waits for them, and re-layouts  7.56 us
    ppermute x2, starting transfers between devices, below(): lax.ppermute(value, 'section', [(i, i - 1) for i in range(1, section_coun...  2.7 us
  transfers between devices with their start and end apart: 20, of which 12 were waited for; matrix products, arithmetic and copies ran while one was open for 0% of the time, Pallas kernels for 7%

profile of v1, /device:TPU:0, one launch (start us, length us, event | category | flops | bytes accessed | tf_op | source)
XLA Modules:
  0.0 76.0 jit_solution(12112940684044191157)
XLA Ops:
  1.3 0.0 copy-start
  1.3 1.4 %copy-done = bf16[1,3,512,512]{3,2,1,0:T(8,128)(2,1)S(1)} copy-done((bf16[1,3,512,512]{3,2,1,0:T(8,128)(2,1)S(1)}, bf16[1,3,512,512]{3,2,1,0:T(8,128)(2,1)}, u32[]{:S(2)}) %copy-start) | copy-done | bytes 1572888
  2.7 1.0 %copy-done.2 = bf16[4,128,512]{2,1,0:T(8,128)(2,1)S(1)} copy-done((bf16[4,128,512]{2,1,0:T(8,128)(2,1)S(1)}, bf16[4,128,512]{2,1,0:T(8,128)(2,1)}, u32[]{:S(2)}) %copy-start.2) | copy-done | bytes 524312
  3.7 0.7 copy-done.7
  4.4 1.0 %copy-done.9 = bf16[1,4,128,512]{3,2,1,0:T(8,128)(2,1)S(1)} copy-done((bf16[1,4,128,512]{3,2,1,0:T(8,128)(2,1)S(1)}, bf16[1,4,128,512]{3,2,1,0:T(8,128)(2,1)}, u32[]{:S(2)}) %copy-start.9) | copy-done | bytes 524312
  5.4 0.8 %copy-done.10 = bf16[1,50,512]{2,1,0:T(8,128)(2,1)S(1)} copy-done((bf16[1,50,512]{2,1,0:T(8,128)(2,1)S(1)}, bf16[1,50,512]{2,1,0:T(8,128)(2,1)}, u32[]{:S(2)}) %copy-start.10) | copy-done | bytes 51224
  6.3 4.6 %shard_map.85 = (f32[512,512]{1,0:T(8,128)S(1)}, bf16[512,512]{1,0:T(8,128)(2,1)S(1)}, bf16[512,256]{1,0:T(8,128)(2,1)}, bf16[512,256]{1,0:T(8,128)(2,1)}) custom-call(s32[4]{0:T(128)S(1)} %copy-done.7, s32[1]{0:T(128)S(6)} %copy.10.dil, bf16[4,128,512]{2,1,0:T(8,128)(2,1)S(1)} %bitcast.17, bf16[50,512]{1,0:T(8,128)(2,1)S(1)} %bitcast.18, ...), custom_call_target="tpu_custom_call" | custom-call | flops 1610612736 | bytes 4769812 | tf_op jit(solution)/shard_map/pallas_call | solution.py:23
  10.8 0.8 %copy-done.4 = bf16[512,512]{1,0:T(8,128)(2,1)} copy-done((bf16[512,512]{1,0:T(8,128)(2,1)}, bf16[512,512]{1,0:T(8,128)(2,1)S(1)}, u32[]{:S(2)}) %copy-start.4) | copy-done | bytes 524312
  11.6 1.4 %collective-permute-start.1 = (bf16[512,256]{1,0:T(8,128)(2,1)}, bf16[512,256]{1,0:T(8,128)(2,1)}, u32[]{:S(2)}, u32[]{:S(2)}) collective-permute-start(bf16[512,256]{1,0:T(8,128)(2,1)} %get-tuple-element.27), channel_id=1, source_target_pairs={{16,0},{17,1},{18,2},{19,3},{20,4},{21,5},{22,6},{23,7},{24,8},{25... | collective-permute-start | bytes 786440 | tf_op jit(solution)/shard_map/ppermute | solution.py:204
  13.0 1.3 %collective-permute-start = (bf16[512,256]{1,0:T(8,128)(2,1)}, bf16[512,256]{1,0:T(8,128)(2,1)S(1)}, u32[]{:S(2)}, u32[]{:S(2)}) collective-permute-start(bf16[512,256]{1,0:T(8,128)(2,1)} %get-tuple-element.24), channel_id=1, source_target_pairs={{16,0},{17,1},{18,2},{19,3},{20,4},{21,5},{22,6},{23,7},{24,8},{25... | collective-permute-start | bytes 786440 | tf_op jit(solution)/shard_map/ppermute | solution.py:204
  14.3 0.1 stack.27.flags.flags_ref
  14.4 8.9 %collective-permute-done.1.recv = bf16[512,256]{1,0:T(8,128)(2,1)} collective-permute-done((bf16[512,256]{1,0:T(8,128)(2,1)}, bf16[512,256]{1,0:T(8,128)(2,1)}, u32[]{:S(2)}, u32[]{:S(2)}) %collective-permute-start.1) | collective-permute-done | bytes 262176 | tf_op jit(solution)/shard_map/ppermute | solution.py:204
  23.4 1.0 %copy-done.5 = bf16[512,512]{1,0:T(8,128)(2,1)S(1)} copy-done((bf16[512,512]{1,0:T(8,128)(2,1)S(1)}, bf16[512,512]{1,0:T(8,128)(2,1)}, u32[]{:S(2)}) %copy-start.5) | copy-done | bytes 524312
  24.4 2.0 %shard_map.86 = (bf16[512,256]{1,0:T(8,128)(2,1)S(1)}, bf16[512,768]{1,0:T(8,128)(2,1)S(1)}, bf16[256,768]{1,0:T(8,128)(2,1)S(1)}, bf16[256,768]{1,0:T(8,128)(2,1)S(1)}) custom-call(s32[5]{0:T(128)S(1)} %stack.27.flags.flags_ref, s32[1]{0:T(128)S(6)} %copy.10.dil, bf16[4,128,512]{2,1,0:T(8,128)(2,1)S(1)} %copy-done.3, ...), custom_call_target="tpu_custom_call" | custom-call | flops 402653184 | bytes 4194328 | tf_op jit(solution)/shard_map/pallas_call | solution.py:23
  26.4 0.0 copy-start.6
  26.4 0.6 shard_map.87.rest_1_
  27.0 1.1 %collective-permute-done.recv = bf16[512,256]{1,0:T(8,128)(2,1)S(1)} collective-permute-done((bf16[512,256]{1,0:T(8,128)(2,1)}, bf16[512,256]{1,0:T(8,128)(2,1)S(1)}, u32[]{:S(2)}, u32[]{:S(2)}) %collective-permute-start) | collective-permute-done | bytes 262176 | tf_op jit(solution)/shard_map/ppermute | solution.py:204
  28.1 2.1 %shard_map.88 = (bf16[256,896]{1,0:T(8,128)(2,1)S(1)}, bf16[256,896]{1,0:T(8,128)(2,1)S(1)}, bf16[4,128,512]{2,1,0:T(8,128)(2,1)}) custom-call(s32[5]{0:T(128)S(1)} %stack.27.flags.flags_ref, s32[1]{0:T(128)S(6)} %copy.10.dil, s32[4]{0:T(128)S(1)} %copy-done.8, bf16[4,128,512]{2,1,0:T(8,128)(2,1)S(1)} %copy-done.3, ...), custom_call_target="tpu_custom_call" | custom-call | flops 805306368 | bytes 6684712 | tf_op jit(solution)/shard_map/pallas_call | solution.py:23
  30.2 0.5 collective-permute-start.2
  30.8 1.3 %collective-permute-done.11.refs_1_ = bf16[256,896]{1,0:T(8,128)(2,1)S(1)} collective-permute-done((bf16[256,896]{1,0:T(8,128)(2,1)S(1)}, bf16[256,896]{1,0:T(8,128)(2,1)S(1)}, u32[]{:S(2)}, u32[]{:S(2)}) %collective-permute-start.11) | collective-permute-done | bytes 458784 | tf_op jit(solution)/shard_map/ppermute | solution.py:168
  32.1 0.7 shard_map.91
  32.7 2.4 %collective-permute-start.12 = (bf16[128,896]{1,0:T(8,128)(2,1)S(1)}, bf16[128,896]{1,0:T(8,128)(2,1)S(1)}, u32[]{:S(2)}, u32[]{:S(2)}) collective-permute-start(bf16[128,896]{1,0:T(8,128)(2,1)S(1)} %get-tuple-element.40), channel_id=1, source_target_pairs={{0,2},{1,3},{2,0},{3,1},{4,6},{5,7},{6,4},{7,5},{8,10},{9,11},{10,... | collective-permute-start | bytes 688136 | tf_op jit(solution)/shard_map/ppermute | solution.py:168
  35.1 0.7 shard_map.89
  35.8 0.1 collective-permute-start.3
  35.9 5.6 %collective-permute-done.12.refs_1_ = bf16[128,896]{1,0:T(8,128)(2,1)S(1)} collective-permute-done((bf16[128,896]{1,0:T(8,128)(2,1)S(1)}, bf16[128,896]{1,0:T(8,128)(2,1)S(1)}, u32[]{:S(2)}, u32[]{:S(2)}) %collective-permute-start.12) | collective-permute-done | bytes 229408 | tf_op jit(solution)/shard_map/ppermute | solution.py:168
  41.5 0.6 shard_map.92
  42.1 2.2 %collective-permute-start.13 = (bf16[64,896]{1,0:T(8,128)(2,1)S(1)}, bf16[64,896]{1,0:T(8,128)(2,1)S(1)}, u32[]{:S(2)}, u32[]{:S(2)}) collective-permute-start(bf16[64,896]{1,0:T(8,128)(2,1)S(1)} %get-tuple-element.42), channel_id=1, source_target_pairs={{0,4},{1,5},{2,6},{3,7},{4,0},{5,1},{6,2},{7,3},{8,12},{9,13},{10,... | collective-permute-start | bytes 344072 | tf_op jit(solution)/shard_map/ppermute | solution.py:168
  44.3 0.9 %collective-permute-done.3.refs_1_ = bf16[128,768]{1,0:T(8,128)(2,1)S(1)} collective-permute-done((bf16[128,768]{1,0:T(8,128)(2,1)S(1)}, bf16[128,768]{1,0:T(8,128)(2,1)S(1)}, u32[]{:S(2)}, u32[]{:S(2)}) %collective-permute-start.3) | collective-permute-done | bytes 196640 | tf_op jit(solution)/shard_map/ppermute | solution.py:168
  45.3 0.6 shard_map.90
  45.9 1.9 %collective-permute-start.4 = (bf16[64,768]{1,0:T(8,128)(2,1)S(1)}, bf16[64,768]{1,0:T(8,128)(2,1)S(1)}, u32[]{:S(2)}, u32[]{:S(2)}) collective-permute-start(bf16[64,768]{1,0:T(8,128)(2,1)S(1)} %get-tuple-element.36), channel_id=1, source_target_pairs={{0,4},{1,5},{2,6},{3,7},{4,0},{5,1},{6,2},{7,3},{8,12},{9,13},{10,... | collective-permute-start | bytes 294920 | tf_op jit(solution)/shard_map/ppermute | solution.py:168
  47.7 2.6 %collective-permute-start.14 = (bf16[64,896]{1,0:T(8,128)(2,1)S(1)}, bf16[64,896]{1,0:T(8,128)(2,1)S(1)}, u32[]{:S(2)}, u32[]{:S(2)}) collective-permute-start(bf16[64,896]{1,0:T(8,128)(2,1)S(1)} %add_convert_fusion.1), channel_id=1, source_target_pairs={{0,8},{1,9},{2,10},{3,11},{4,12},{5,13},{6,14},{7,15},{8,0},{9,1},... | collective-permute-start | bytes 344072 | tf_op jit(solution)/shard_map/ppermute | solution.py:168
  50.4 1.0 %collective-permute-done.4 = bf16[64,768]{1,0:T(8,128)(2,1)S(1)} collective-permute-done((bf16[64,768]{1,0:T(8,128)(2,1)S(1)}, bf16[64,768]{1,0:T(8,128)(2,1)S(1)}, u32[]{:S(2)}, u32[]{:S(2)}) %collective-permute-start.4) | collective-permute-done | bytes 98336 | tf_op jit(solution)/shard_map/ppermute | solution.py:168
  51.4 2.6 %collective-permute-start.5 = (bf16[64,768]{1,0:T(8,128)(2,1)S(1)}, bf16[64,768]{1,0:T(8,128)(2,1)S(1)}, u32[]{:S(2)}, u32[]{:S(2)}) collective-permute-start(bf16[64,768]{1,0:T(8,128)(2,1)S(1)} %add_convert_fusion.3), channel_id=1, source_target_pairs={{0,8},{1,9},{2,10},{3,11},{4,12},{5,13},{6,14},{7,15},{8,0},{9,1},... | collective-permute-start | bytes 294920 | tf_op jit(solution)/shard_map/ppermute | solution.py:168
  54.1 4.0 %collective-permute-done.14 = bf16[64,896]{1,0:T(8,128)(2,1)S(1)} collective-permute-done((bf16[64,896]{1,0:T(8,128)(2,1)S(1)}, bf16[64,896]{1,0:T(8,128)(2,1)S(1)}, u32[]{:S(2)}, u32[]{:S(2)}) %collective-permute-start.14) | collective-permute-done | bytes 114720 | tf_op jit(solution)/shard_map/ppermute | solution.py:168
  58.1 0.5 collective-permute-start.15
  58.6 1.0 %collective-permute-done.5 = bf16[64,768]{1,0:T(8,128)(2,1)S(1)} collective-permute-done((bf16[64,768]{1,0:T(8,128)(2,1)S(1)}, bf16[64,768]{1,0:T(8,128)(2,1)S(1)}, u32[]{:S(2)}, u32[]{:S(2)}) %collective-permute-start.5) | collective-permute-done | bytes 98336 | tf_op jit(solution)/shard_map/ppermute | solution.py:168
  59.6 0.7 collective-permute-start.6
  60.3 2.8 %collective-permute-done.15.refs_7_ = bf16[64,896]{1,0:T(8,128)(2,1)S(1)} collective-permute-done((bf16[64,896]{1,0:T(8,128)(2,1)S(1)}, bf16[64,896]{1,0:T(8,128)(2,1)S(1)}, u32[]{:S(2)}, u32[]{:S(2)}) %collective-permute-start.15) | collective-permute-done | bytes 114720 | tf_op jit(solution)/shard_map/ppermute | solution.py:168
  63.1 1.6 %collective-permute-start.16 = (bf16[128,896]{1,0:T(8,128)(2,1)S(1)}, bf16[128,896]{1,0:T(8,128)(2,1)S(1)}, u32[]{:S(2)}, u32[]{:S(2)}) collective-permute-start(bf16[128,896]{1,0:T(8,128)(2,1)S(1)} %pad_maximum_fusion), channel_id=1, source_target_pairs={{0,2},{1,3},{2,0},{3,1},{4,6},{5,7},{6,4},{7,5},{8,10},{9,11},{10,... | collective-permute-start | bytes 688136 | tf_op jit(solution)/shard_map/ppermute | solution.py:168
  64.6 1.2 %collective-permute-start.7 = (bf16[128,768]{1,0:T(8,128)(2,1)S(1)}, bf16[128,768]{1,0:T(8,128)(2,1)S(1)}, u32[]{:S(2)}, u32[]{:S(2)}) collective-permute-start(bf16[128,768]{1,0:T(8,128)(2,1)S(1)} %pad_maximum_fusion.1), channel_id=1, source_target_pairs={{0,2},{1,3},{2,0},{3,1},{4,6},{5,7},{6,4},{7,5},{8,10},{9,11},{10,... | collective-permute-start | bytes 589832 | tf_op jit(solution)/shard_map/ppermute | solution.py:168
  65.9 3.4 %collective-permute-done.16.refs_8_ = bf16[128,896]{1,0:T(8,128)(2,1)S(1)} collective-permute-done((bf16[128,896]{1,0:T(8,128)(2,1)S(1)}, bf16[128,896]{1,0:T(8,128)(2,1)S(1)}, u32[]{:S(2)}, u32[]{:S(2)}) %collective-permute-start.16) | collective-permute-done | bytes 229408 | tf_op jit(solution)/shard_map/ppermute | solution.py:168
  69.3 0.5 collective-permute-start.8
  69.8 1.6 %collective-permute-done.7.refs_2_ = bf16[128,768]{1,0:T(8,128)(2,1)S(1)} collective-permute-done((bf16[128,768]{1,0:T(8,128)(2,1)S(1)}, bf16[128,768]{1,0:T(8,128)(2,1)S(1)}, u32[]{:S(2)}, u32[]{:S(2)}) %collective-permute-start.7) | collective-permute-done | bytes 196640 | tf_op jit(solution)/shard_map/ppermute | solution.py:168
  71.4 0.5 collective-permute-start.17
  71.9 0.5 collective-permute-start.9
  72.4 1.0 %collective-permute-done.9.refs_4_ = bf16[64,768]{1,0:T(8,128)(2,1)S(1)} collective-permute-done((bf16[64,768]{1,0:T(8,128)(2,1)S(1)}, bf16[64,768]{1,0:T(8,128)(2,1)S(1)}, u32[]{:S(2)}, u32[]{:S(2)}) %collective-permute-start.9) | collective-permute-done | bytes 98336 | tf_op jit(solution)/shard_map/ppermute | solution.py:168
  73.4 1.8 %shard_map.93 = (bf16[3,512,512]{2,1,0:T(8,128)(2,1)}, bf16[512,128]{1,0:T(8,128)(2,1)S(1)}) custom-call(s32[5]{0:T(128)S(1)} %stack.27.flags.flags_ref, bf16[64,768]{1,0:T(8,128)(2,1)S(1)} %add_convert_fusion.2.refs_0_, bf16[64,768]{1,0:T(8,128)(2,1)S(1)} %collective-permute-done.6.refs_1_, bf16[128,768]{1,0:T(8,128)(2,1)S(1)} %collective-permute-done.7.refs_2_, ...), custom_call_target="tpu_custom_call" | custom-call | bytes 3407892 | tf_op jit(solution)/shard_map/pallas_call | solution.py:23
  75.2 0.7 copy.9
  (32 shorter events, 0.2 us)
Async XLA Ops:
  1.3 1.4 %copy-start = (bf16[1,3,512,512]{3,2,1,0:T(8,128)(2,1)S(1)}, bf16[1,3,512,512]{3,2,1,0:T(8,128)(2,1)}, u32[]{:S(2)}) copy-start(bf16[1,3,512,512]{3,2,1,0:T(8,128)(2,1)} %param.8) | copy-start | bytes 4718596
  2.7 1.0 %copy-start.2 = (bf16[4,128,512]{2,1,0:T(8,128)(2,1)S(1)}, bf16[4,128,512]{2,1,0:T(8,128)(2,1)}, u32[]{:S(2)}) copy-start(bf16[4,128,512]{2,1,0:T(8,128)(2,1)} %top.5) | copy-start | bytes 1572868
  3.7 0.7 copy-start.7
  4.4 1.0 %copy-start.9 = (bf16[1,4,128,512]{3,2,1,0:T(8,128)(2,1)S(1)}, bf16[1,4,128,512]{3,2,1,0:T(8,128)(2,1)}, u32[]{:S(2)}) copy-start(bf16[1,4,128,512]{3,2,1,0:T(8,128)(2,1)} %param.6) | copy-start | bytes 1572868
  5.4 0.8 %copy-start.10 = (bf16[1,50,512]{2,1,0:T(8,128)(2,1)S(1)}, bf16[1,50,512]{2,1,0:T(8,128)(2,1)}, u32[]{:S(2)}) copy-start(bf16[1,50,512]{2,1,0:T(8,128)(2,1)} %param.9) | copy-start | bytes 153604
  6.2 17.1 %copy-start.3 = (bf16[4,128,512]{2,1,0:T(8,128)(2,1)S(1)}, bf16[4,128,512]{2,1,0:T(8,128)(2,1)}, u32[]{:S(2)}) copy-start(bf16[4,128,512]{2,1,0:T(8,128)(2,1)} %top.5) | copy-start | bytes 1572868
  10.8 0.8 %copy-start.4 = (bf16[512,512]{1,0:T(8,128)(2,1)}, bf16[512,512]{1,0:T(8,128)(2,1)S(1)}, u32[]{:S(2)}) copy-start(bf16[512,512]{1,0:T(8,128)(2,1)S(1)} %get-tuple-element.26.h_t) | copy-start | bytes 1572868
  11.6 14.8 %copy-start.1 = (bf16[1,3,512,512]{3,2,1,0:T(8,128)(2,1)S(1)}, bf16[1,3,512,512]{3,2,1,0:T(8,128)(2,1)}, u32[]{:S(2)}) copy-start(bf16[1,3,512,512]{3,2,1,0:T(8,128)(2,1)} %param.8) | copy-start | bytes 4718596
  11.6 11.8 %collective-permute-start.1 = (bf16[512,256]{1,0:T(8,128)(2,1)}, bf16[512,256]{1,0:T(8,128)(2,1)}, u32[]{:S(2)}, u32[]{:S(2)}) collective-permute-start(bf16[512,256]{1,0:T(8,128)(2,1)} %get-tuple-element.27), channel_id=1, source_target_pairs={{16,0},{17,1},{18,2},{19,3},{20,4},{21,5},{22,6},{23,7},{24,8},{25... | collective-permute-start | bytes 786440 | tf_op jit(solution)/shard_map/ppermute | solution.py:204
  13.0 15.1 %collective-permute-start = (bf16[512,256]{1,0:T(8,128)(2,1)}, bf16[512,256]{1,0:T(8,128)(2,1)S(1)}, u32[]{:S(2)}, u32[]{:S(2)}) collective-permute-start(bf16[512,256]{1,0:T(8,128)(2,1)} %get-tuple-element.24), channel_id=1, source_target_pairs={{16,0},{17,1},{18,2},{19,3},{20,4},{21,5},{22,6},{23,7},{24,8},{25... | collective-permute-start | bytes 786440 | tf_op jit(solution)/shard_map/ppermute | solution.py:204
  23.4 1.0 %copy-start.5 = (bf16[512,512]{1,0:T(8,128)(2,1)S(1)}, bf16[512,512]{1,0:T(8,128)(2,1)}, u32[]{:S(2)}) copy-start(bf16[512,512]{1,0:T(8,128)(2,1)} %copy-done.4) | copy-start | bytes 1572868
  26.4 1.7 %copy-start.6 = (bf16[512,512]{1,0:T(8,128)(2,1)S(1)}, bf16[512,512]{1,0:T(8,128)(2,1)}, u32[]{:S(2)}) copy-start(bf16[512,512]{1,0:T(8,128)(2,1)} %copy-done.4) | copy-start | bytes 1572868
  26.4 1.7 %copy-start.8 = (s32[4]{0:T(128)S(1)}, s32[4]{0:T(128)}, u32[]{:S(2)}) copy-start(s32[4]{0:T(128)} %ts.3) | copy-start | bytes 52
  30.2 1.8 %collective-permute-start.11 = (bf16[256,896]{1,0:T(8,128)(2,1)S(1)}, bf16[256,896]{1,0:T(8,128)(2,1)S(1)}, u32[]{:S(2)}, u32[]{:S(2)}) collective-permute-start(bf16[256,896]{1,0:T(8,128)(2,1)S(1)} %get-tuple-element.38), channel_id=1, source_target_pairs={{0,1},{1,0},{2,3},{3,2},{4,5},{5,4},{6,7},{7,6},{8,9},{9,8},{10,11... | collective-permute-start | bytes 1376264 | tf_op jit(solution)/shard_map/ppermute | solution.py:168
  30.2 4.9 %collective-permute-start.2 = (bf16[256,768]{1,0:T(8,128)(2,1)S(1)}, bf16[256,768]{1,0:T(8,128)(2,1)S(1)}, u32[]{:S(2)}, u32[]{:S(2)}) collective-permute-start(bf16[256,768]{1,0:T(8,128)(2,1)S(1)} %get-tuple-element.32), channel_id=1, source_target_pairs={{0,1},{1,0},{2,3},{3,2},{4,5},{5,4},{6,7},{7,6},{8,9},{9,8},{10,11... | collective-permute-start | bytes 1179656 | tf_op jit(solution)/shard_map/ppermute | solution.py:168
  32.7 8.8 %collective-permute-start.12 = (bf16[128,896]{1,0:T(8,128)(2,1)S(1)}, bf16[128,896]{1,0:T(8,128)(2,1)S(1)}, u32[]{:S(2)}, u32[]{:S(2)}) collective-permute-start(bf16[128,896]{1,0:T(8,128)(2,1)S(1)} %get-tuple-element.40), channel_id=1, source_target_pairs={{0,2},{1,3},{2,0},{3,1},{4,6},{5,7},{6,4},{7,5},{8,10},{9,11},{10,... | collective-permute-start | bytes 688136 | tf_op jit(solution)/shard_map/ppermute | solution.py:168
  35.8 9.5 %collective-permute-start.3 = (bf16[128,768]{1,0:T(8,128)(2,1)S(1)}, bf16[128,768]{1,0:T(8,128)(2,1)S(1)}, u32[]{:S(2)}, u32[]{:S(2)}) collective-permute-start(bf16[128,768]{1,0:T(8,128)(2,1)S(1)} %get-tuple-element.34), channel_id=1, source_target_pairs={{0,2},{1,3},{2,0},{3,1},{4,6},{5,7},{6,4},{7,5},{8,10},{9,11},{10,... | collective-permute-start | bytes 589832 | tf_op jit(solution)/shard_map/ppermute | solution.py:168
  42.1 5.6 %collective-permute-start.13 = (bf16[64,896]{1,0:T(8,128)(2,1)S(1)}, bf16[64,896]{1,0:T(8,128)(2,1)S(1)}, u32[]{:S(2)}, u32[]{:S(2)}) collective-permute-start(bf16[64,896]{1,0:T(8,128)(2,1)S(1)} %get-tuple-element.42), channel_id=1, source_target_pairs={{0,4},{1,5},{2,6},{3,7},{4,0},{5,1},{6,2},{7,3},{8,12},{9,13},{10,... | collective-permute-start | bytes 344072 | tf_op jit(solution)/shard_map/ppermute | solution.py:168
  45.9 5.6 %collective-permute-start.4 = (bf16[64,768]{1,0:T(8,128)(2,1)S(1)}, bf16[64,768]{1,0:T(8,128)(2,1)S(1)}, u32[]{:S(2)}, u32[]{:S(2)}) collective-permute-start(bf16[64,768]{1,0:T(8,128)(2,1)S(1)} %get-tuple-element.36), channel_id=1, source_target_pairs={{0,4},{1,5},{2,6},{3,7},{4,0},{5,1},{6,2},{7,3},{8,12},{9,13},{10,... | collective-permute-start | bytes 294920 | tf_op jit(solution)/shard_map/ppermute | solution.py:168
  47.7 10.3 %collective-permute-start.14 = (bf16[64,896]{1,0:T(8,128)(2,1)S(1)}, bf16[64,896]{1,0:T(8,128)(2,1)S(1)}, u32[]{:S(2)}, u32[]{:S(2)}) collective-permute-start(bf16[64,896]{1,0:T(8,128)(2,1)S(1)} %add_convert_fusion.1), channel_id=1, source_target_pairs={{0,8},{1,9},{2,10},{3,11},{4,12},{5,13},{6,14},{7,15},{8,0},{9,1},... | collective-permute-start | bytes 344072 | tf_op jit(solution)/shard_map/ppermute | solution.py:168
  51.4 8.1 %collective-permute-start.5 = (bf16[64,768]{1,0:T(8,128)(2,1)S(1)}, bf16[64,768]{1,0:T(8,128)(2,1)S(1)}, u32[]{:S(2)}, u32[]{:S(2)}) collective-permute-start(bf16[64,768]{1,0:T(8,128)(2,1)S(1)} %add_convert_fusion.3), channel_id=1, source_target_pairs={{0,8},{1,9},{2,10},{3,11},{4,12},{5,13},{6,14},{7,15},{8,0},{9,1},... | collective-permute-start | bytes 294920 | tf_op jit(solution)/shard_map/ppermute | solution.py:168
  58.1 5.0 %collective-permute-start.15 = (bf16[64,896]{1,0:T(8,128)(2,1)S(1)}, bf16[64,896]{1,0:T(8,128)(2,1)S(1)}, u32[]{:S(2)}, u32[]{:S(2)}) collective-permute-start(bf16[64,896]{1,0:T(8,128)(2,1)S(1)} %add_convert_fusion.refs_6_), channel_id=1, source_target_pairs={{0,4},{1,5},{2,6},{3,7},{4,0},{5,1},{6,2},{7,3},{8,12},{9,13},{10,... | collective-permute-start | bytes 344072 | tf_op jit(solution)/shard_map/ppermute | solution.py:168
  59.6 5.1 %collective-permute-start.6 = (bf16[64,768]{1,0:T(8,128)(2,1)S(1)}, bf16[64,768]{1,0:T(8,128)(2,1)S(1)}, u32[]{:S(2)}, u32[]{:S(2)}) collective-permute-start(bf16[64,768]{1,0:T(8,128)(2,1)S(1)} %add_convert_fusion.2.refs_0_), channel_id=1, source_target_pairs={{0,4},{1,5},{2,6},{3,7},{4,0},{5,1},{6,2},{7,3},{8,12},{9,13},{10,... | collective-permute-start | bytes 294920 | tf_op jit(solution)/shard_map/ppermute | solution.py:168
  63.1 6.2 %collective-permute-start.16 = (bf16[128,896]{1,0:T(8,128)(2,1)S(1)}, bf16[128,896]{1,0:T(8,128)(2,1)S(1)}, u32[]{:S(2)}, u32[]{:S(2)}) collective-permute-start(bf16[128,896]{1,0:T(8,128)(2,1)S(1)} %pad_maximum_fusion), channel_id=1, source_target_pairs={{0,2},{1,3},{2,0},{3,1},{4,6},{5,7},{6,4},{7,5},{8,10},{9,11},{10,... | collective-permute-start | bytes 688136 | tf_op jit(solution)/shard_map/ppermute | solution.py:168
  64.6 6.8 %collective-permute-start.7 = (bf16[128,768]{1,0:T(8,128)(2,1)S(1)}, bf16[128,768]{1,0:T(8,128)(2,1)S(1)}, u32[]{:S(2)}, u32[]{:S(2)}) collective-permute-start(bf16[128,768]{1,0:T(8,128)(2,1)S(1)} %pad_maximum_fusion.1), channel_id=1, source_target_pairs={{0,2},{1,3},{2,0},{3,1},{4,6},{5,7},{6,4},{7,5},{8,10},{9,11},{10,... | collective-permute-start | bytes 589832 | tf_op jit(solution)/shard_map/ppermute | solution.py:168
  69.3 4.1 %collective-permute-start.19 = (bf16[128,896]{1,0:T(8,128)(2,1)S(1)}, bf16[128,896]{1,0:T(8,128)(2,1)S(1)}, u32[]{:S(2)}, u32[]{:S(2)}) collective-permute-start(bf16[128,896]{1,0:T(8,128)(2,1)S(1)} %collective-permute-done.16.refs_8_), channel_id=1, source_target_pairs={{0,1},{1,0},{2,3},{3,2},{4,5},{5,4},{6,7},{7,6},{8,9},{9,8},{10,11... | collective-permute-start | bytes 688136 | tf_op jit(solution)/shard_map/ppermute | solution.py:168
  69.3 2.6 %collective-permute-start.8 = (bf16[64,768]{1,0:T(8,128)(2,1)S(1)}, bf16[64,768]{1,0:T(8,128)(2,1)S(1)}, u32[]{:S(2)}, u32[]{:S(2)}) collective-permute-start(bf16[64,768]{1,0:T(8,128)(2,1)S(1)} %add_convert_fusion.2.refs_0_), channel_id=1, source_target_pairs={{0,1},{1,0},{2,3},{3,2},{4,5},{5,4},{6,7},{7,6},{8,9},{9,8},{10,11... | collective-permute-start | bytes 294920 | tf_op jit(solution)/shard_map/ppermute | solution.py:168
  71.4 2.0 %collective-permute-start.10 = (bf16[128,768]{1,0:T(8,128)(2,1)S(1)}, bf16[128,768]{1,0:T(8,128)(2,1)S(1)}, u32[]{:S(2)}, u32[]{:S(2)}) collective-permute-start(bf16[128,768]{1,0:T(8,128)(2,1)S(1)} %collective-permute-done.7.refs_2_), channel_id=1, source_target_pairs={{0,1},{1,0},{2,3},{3,2},{4,5},{5,4},{6,7},{7,6},{8,9},{9,8},{10,11... | collective-permute-start | bytes 589832 | tf_op jit(solution)/shard_map/ppermute | solution.py:168
  71.4 2.0 %collective-permute-start.17 = (bf16[64,896]{1,0:T(8,128)(2,1)S(1)}, bf16[64,896]{1,0:T(8,128)(2,1)S(1)}, u32[]{:S(2)}, u32[]{:S(2)}) collective-permute-start(bf16[64,896]{1,0:T(8,128)(2,1)S(1)} %add_convert_fusion.refs_6_), channel_id=1, source_target_pairs={{0,1},{1,0},{2,3},{3,2},{4,5},{5,4},{6,7},{7,6},{8,9},{9,8},{10,11... | collective-permute-start | bytes 344072 | tf_op jit(solution)/shard_map/ppermute | solution.py:168
  71.9 1.5 %collective-permute-start.18 = (bf16[64,896]{1,0:T(8,128)(2,1)S(1)}, bf16[64,896]{1,0:T(8,128)(2,1)S(1)}, u32[]{:S(2)}, u32[]{:S(2)}) collective-permute-start(bf16[64,896]{1,0:T(8,128)(2,1)S(1)} %collective-permute-done.15.refs_7_), channel_id=1, source_target_pairs={{0,1},{1,0},{2,3},{3,2},{4,5},{5,4},{6,7},{7,6},{8,9},{9,8},{10,11... | collective-permute-start | bytes 344072 | tf_op jit(solution)/shard_map/ppermute | solution.py:168
  71.9 1.5 %collective-permute-start.9 = (bf16[64,768]{1,0:T(8,128)(2,1)S(1)}, bf16[64,768]{1,0:T(8,128)(2,1)S(1)}, u32[]{:S(2)}, u32[]{:S(2)}) collective-permute-start(bf16[64,768]{1,0:T(8,128)(2,1)S(1)} %collective-permute-done.6.refs_1_), channel_id=1, source_target_pairs={{0,1},{1,0},{2,3},{3,2},{4,5},{5,4},{6,7},{7,6},{8,9},{9,8},{10,11... | collective-permute-start | bytes 294920 | tf_op jit(solution)/shard_map/ppermute | solution.py:168

commit v2 on v1

v2 whole, which is shorter than its diff:
```python
import functools
import math

import jax
import jax.numpy as jnp
from jax import lax
from jax.experimental import pallas as pl
from jax.experimental.pallas import tpu as pltpu
from jax.sharding import PartitionSpec as P

CHUNKS = 2
F32 = jnp.float32
BF16 = jnp.bfloat16
VMEM = pl.BlockSpec(memory_space=pltpu.VMEM)
SMEM = pl.BlockSpec(memory_space=pltpu.SMEM)
HBM = pl.BlockSpec(memory_space=pltpu.HBM)
NT = (((1,), (1,)), ((), ()))


def call(kernel, out_shape, args, smem=0, far=0, scratch=(), flops=0):
    specs = [SMEM] * smem + [HBM] * far + [VMEM] * (len(args) - smem - far)
    moved = sum(a.size * a.dtype.itemsize for a in args)
    moved += sum(math.prod(o.shape) * o.dtype.itemsize for o in out_shape)
    return pl.pallas_call(
        kernel,
        out_shape=out_shape,
        in_specs=specs,
        out_specs=[VMEM] * len(out_shape),
        scratch_shapes=list(scratch),
        compiler_params=pltpu.CompilerParams(vmem_limit_bytes=48 * 2**20),
        cost_estimate=pl.CostEstimate(flops=flops, bytes_accessed=moved, transcendentals=0),
    )(*args)


def is_top():
    return lax.axis_index("section") == lax.axis_size("section") - 1


def dp_bit(n):
    return lax.rem(lax.div(lax.axis_index("dp"), 1 << n), 2)


def like(shape, dtype):
    return jax.ShapeDtypeStruct(shape, dtype)


def put_taps(values, taps, bins, dilation, orientation):
    rows, cols = values.shape
    place = lax.broadcasted_iota(jnp.int32, (bins, cols), 0)
    taps[:, cols : 2 * cols] = values
    for b in range(rows // bins):
        at = slice(b * bins, (b + 1) * bins)
        group = values[at].astype(F32)
        later = pltpu.roll(group, bins - dilation, 0)
        later = jnp.where(place < bins - dilation, later, 0.0).astype(BF16)
        earlier = pltpu.roll(group, dilation, 0)
        earlier = jnp.where(place >= dilation, earlier, 0.0).astype(BF16)
        first, third = (earlier, later) if orientation == 1 else (later, earlier)
        taps[at, 0:cols] = first
        taps[at, 2 * cols : 3 * cols] = third


def back_product(taps, weight, cols):
    total = None
    for k in range(3):
        part = lax.dot_general(
            taps[:, k * cols : (k + 1) * cols], weight[k], NT, preferred_element_type=F32
        )
        total = part if total is None else total + part
    return total


def first_kernel(
    dil, ts, x, table, weight, top, slope, mixed, taps, weight_v, top_v, hot, g_out, *scratch
):
    ts_s, x_v, table_v, tab, sems = scratch
    pairs = ((ts, ts_s), (x, x_v), (table, table_v), (weight, weight_v), (top, top_v))
    copies = [pltpu.make_async_copy(a, b, sems.at[n]) for n, (a, b) in enumerate(pairs)]
    for copy in copies:
        copy.start()
    groups, bins, chans = x.shape
    for copy in copies[:3]:
        copy.wait()
    tab[...] = table_v[...].astype(F32)
    for b in range(groups):
        row = x_v[b].astype(F32) + tab[pl.ds(ts_s[b], 1), :]
        mixed[b * bins : (b + 1) * bins, :] = row.astype(BF16)
    put_taps(mixed[...], taps, bins, dil[0], 1)
    steps = lax.broadcasted_iota(jnp.int32, hot.shape, 0)
    lanes = lax.broadcasted_iota(jnp.int32, hot.shape, 1)
    marks = jnp.zeros(hot.shape, F32)
    for b in range(groups):
        marks = jnp.where((lanes == b) & (steps == ts_s[b]), 1.0, marks)
    hot[...] = marks
    copies[3].wait()
    flat = weight_v[...].reshape(3 * chans, chans)
    y = jnp.dot(taps[...], flat, preferred_element_type=F32)
    gate = jax.nn.sigmoid(y)
    slope[...] = gate * (1.0 + y * (1.0 - gate))
    copies[4].wait()
    g = top_v[...].reshape(groups * bins, chans).astype(F32)
    delta = (g * slope[...]).astype(BF16)
    put_taps(delta, taps, bins, dil[0], -1)
    width = g_out.shape[1]
    dh = back_product(taps, weight_v[:, 0:width, :], chans)
    g_out[...] = (g[:, 0:width] + dh).astype(BF16)


def second_kernel(start, mixed, taps, weight, top, g_out, h_t):
    width = g_out.shape[1]
    chans = mixed.shape[1]
    dh = back_product(taps, weight[:, start : start + width, :], chans)
    g = top[...].reshape(mixed.shape)[:, start : start + width]
    g_out[...] = (g.astype(F32) + dh).astype(BF16)
    h_t[...] = mixed[...].T


def layer_kernel(bins, dil, slope, weight, top, *rest):
    g_in, g_out, taps = rest[:CHUNKS], rest[CHUNKS:-1], rest[-1]
    chans = slope.shape[1]
    got = jnp.concatenate([ref[...] for ref in g_in], axis=1)
    fresh = top[...].reshape(got.shape)
    g = jnp.where(is_top(), fresh.astype(F32), got.astype(F32))
    delta = (g * slope[...]).astype(BF16)
    put_taps(delta, taps, bins, dil[0], -1)
    out = (g + back_product(taps, weight, chans)).astype(BF16)
    at = 0
    for ref in g_out:
        ref[...] = out[:, at : at + ref.shape[1]]
        at += ref.shape[1]


def weight_halves(h_t, taps, scale, send, keep, cols):
    half = h_t.shape[0] // 2
    bit = dp_bit(0)
    for ref, part in ((send, 1 - bit), (keep, bit)):
        left = h_t[pl.ds(pl.multiple_of(part * half, half), half), :]
        prod = jnp.dot(left, taps[...], preferred_element_type=F32)
        ref[:, 0:cols] = (prod * scale).astype(BF16)


def weight_kernel(col, scale, dil, top, recv, slope, h_t, g_used, taps, send, keep):
    rows, width = recv.shape
    fresh = top[...].reshape(rows, top.shape[-1])[:, col : col + width]
    g = jnp.where(is_top(), fresh.astype(F32), recv[...].astype(F32))
    g_used[...] = g.astype(BF16)
    delta = (g * slope[:, col : col + width]).astype(BF16)
    put_taps(delta, taps, top.shape[1], dil[0], -1)
    weight_halves(h_t, taps, scale, send, keep, 3 * width)


def back_kernel(col, taps, weight, acc):
    width = taps.shape[1] // 3
    acc[...] = back_product(taps, weight[:, :, col : col + width], width)


def last_kernel(col, scale, dil, top, recv, slope, h_t, weight, hot, *rest):
    prior = (len(rest) - 4) // 2
    g_prior, acc = rest[:prior], rest[prior : 2 * prior]
    send, keep, grad, taps = rest[2 * prior :]
    rows, width = recv.shape
    groups, bins, chans = grad.shape
    fresh = top[...].reshape(rows, chans)[:, col : col + width]
    g = jnp.where(is_top(), fresh.astype(F32), recv[...].astype(F32))
    delta = (g * slope[:, col : col + width]).astype(BF16)
    put_taps(delta, taps, bins, dil[0], -1)
    dh = back_product(taps, weight[:, :, col : col + width], width)
    for ref in acc:
        dh = dh + ref[...]
    whole = jnp.concatenate([ref[...].astype(F32) for ref in g_prior] + [g], axis=1)
    grad[...] = (whole + dh).astype(BF16).reshape(groups, bins, chans)
    table = jnp.zeros((hot.shape[0], chans), F32)
    for b in range(groups):
        total = jnp.sum(dh[b * bins : (b + 1) * bins], axis=0, keepdims=True)
        table = table + hot[:, b : b + 1] * (total * scale)
    table_t = table.T.astype(BF16)
    weight_halves(h_t, taps, scale, send, keep, 3 * width)
    half = chans // 2
    bit = dp_bit(0)
    for ref, part in ((send, 1 - bit), (keep, bit)):
        ref[:, 3 * width :] = jnp.where(part == 0, table_t[0:half], table_t[half:])


def fold_kernel(bit_num, keep, recv, send_out, keep_out):
    half = keep.shape[0] // 2
    bit = dp_bit(bit_num)
    for ref, part in ((send_out, 1 - bit), (keep_out, bit)):
        at = pl.ds(pl.multiple_of(part * half, half), half)
        ref[...] = (keep[at, :].astype(F32) + recv[at, :].astype(F32)).astype(BF16)


def assemble_kernel(plans, *refs):
    weight_out, table_out, table_t = refs[-3:]
    pieces = list(refs[:-3])
    col = 0
    for halvings, lists in plans:
        for offsets in lists:
            ref = pieces.pop(0)
            size = ref.shape[0] // len(offsets)
            for slot, offset in enumerate(offsets):
                block = 0
                for n in halvings:
                    bit = dp_bit(n)
                    block = block * 2 + (1 - bit if (offset >> n) & 1 else bit)
                row = pl.ds(pl.multiple_of(block * size, size), size)
                here = slice(slot * size, (slot + 1) * size)
                width = ref.shape[1] // 3 // 128 * 128
                for k in range(3):
                    weight_out[k, row, col : col + width] = ref[here, k * width : (k + 1) * width]
                if ref.shape[1] > 3 * width:
                    table_t[row, :] = ref[here, 3 * width :].astype(F32)
        col += width
    table_out[...] = table_t[...].T[: table_out.shape[0]].astype(BF16)


def swap(value, bit_num):
    count = lax.axis_size("dp")
    return lax.ppermute(value, "dp", [(i, i ^ (1 << bit_num)) for i in range(count)])


def body(section_input, top_grad, conv_weight, step_table, timesteps, dilations):
    section_count = lax.axis_size("section")
    dp_count = lax.axis_size("dp")
    dp_bits = dp_count.bit_length() - 1
    x = section_input[0]
    weight = conv_weight[0]
    table = step_table[0]
    groups, bins, chans = x.shape
    rows = groups * bins
    width = chans // CHUNKS
    scale = 1.0 / math.sqrt(groups * dp_count * bins)
    unit = 2 * rows * chans * chans * 3

    slope, mixed, taps, weight, top, hot, first = call(
        first_kernel,
        [
            like((rows, chans), F32),
            like((rows, chans), BF16),
            like((rows, 3 * chans), BF16),
            like(weight.shape, BF16),
            like(x.shape, BF16),
            like((128, 128), F32),
            like((rows, width), BF16),
        ],
        (dilations, timesteps, x, table, weight, top_grad),
        smem=1,
        far=5,
        scratch=[
            pltpu.SMEM(timesteps.shape, jnp.int32),
            pltpu.VMEM(x.shape, BF16),
            pltpu.VMEM(table.shape, BF16),
            pltpu.VMEM(table.shape, F32),
            pltpu.SemaphoreType.DMA((5,)),
        ],
        flops=3 * unit // 2,
    )

    def below(value):
        return lax.ppermute(value, "section", [(i, i - 1) for i in range(1, section_count)])

    second, h_t = call(
        functools.partial(second_kernel, width),
        [like((rows, chans - width), BF16), like((chans, rows), BF16)],
        (mixed, taps, weight, top),
        flops=unit // 2,
    )
    got = [below(first), below(second)]
    for _ in range(section_count - 2):
        sent = call(
            functools.partial(layer_kernel, bins),
            [like(v.shape, BF16) for v in got],
            (dilations, slope, weight, top) + tuple(got),
            smem=1,
            scratch=[pltpu.VMEM((rows, 3 * chans), BF16)],
            flops=unit,
        )
        got = [below(value) for value in sent]

    used, taps, send, keep = call(
        functools.partial(weight_kernel, 0, scale),
        [like((rows, width), BF16), like((rows, 3 * width), BF16)]
        + [like((chans // 2, 3 * width), BF16)] * 2,
        (dilations, top, got[0], slope, h_t),
        smem=1,
        flops=unit // 2,
    )
    acc = call(
        functools.partial(back_kernel, 0),
        [like((rows, chans), F32)],
        (taps, weight),
        flops=unit // 2,
    )[0]
    send_2, keep_2, grad = call(
        functools.partial(last_kernel, width, scale),
        [like((chans // 2, 3 * width + 128), BF16)] * 2 + [like(x.shape, BF16)],
        (dilations, top, got[1], slope, h_t, weight, hot, used, acc),
        smem=1,
        scratch=[pltpu.VMEM((rows, 3 * width), BF16)],
        flops=unit,
    )

    inner = list(range(1, dp_bits - 1))
    plans = []
    pieces = []
    for send, keep, order in ((send, keep, inner), (send_2, keep_2, inner[::-1])):
        cols = keep.shape[1]
        at = 0
        for n in order:
            half = [like((keep.shape[0] // 2, cols), BF16)] * 2
            send, keep = call(functools.partial(fold_kernel, n), half, (keep, swap(send, at)))
            at = n
        keep = (keep.astype(F32) + swap(send, at).astype(F32)).astype(BF16)
        own = (keep.astype(F32) + swap(keep, dp_bits - 1).astype(F32)).astype(BF16)
        held = [(own, [0])]
        for n in order[::-1]:
            message = jnp.concatenate([v for v, _ in held], axis=0) if len(held) > 1 else own
            offsets = [o for _, offs in held for o in offs]
            held.append((swap(message, n), [o ^ (1 << n) for o in offsets]))
        held = held + [(swap(v, 0), [o ^ 1 for o in offs]) for v, offs in held]
        pieces += [v for v, _ in held]
        plans.append(([0] + order, [offs for _, offs in held]))

    weight_out, table_out = call(
        functools.partial(assemble_kernel, plans),
        [like(weight.shape, BF16), like(table.shape, BF16)],
        tuple(pieces),
        scratch=[pltpu.VMEM((chans, 128), F32)],
    )
    return (grad[None], weight_out[None], table_out[None])


def solution(mesh):
    placed = (
        P("section", "dp", None, None),
        P("dp", None, None),
        P("section", None, None, None),
        P("section", None, None),
        P("dp"),
        P("section"),
    )
    return jax.shard_map(
        body,
        mesh=mesh,
        in_specs=placed,
        out_specs=(
            P("section", "dp", None, None),
            P("section", None, None, None),
            P("section", None, None),
        ),
        check_vma=False,
    )
```

time: 76.4 us -> 70 us (0.916)
  Pallas kernels: 13.6 us -> 10.8 us
  local copies, waits for them, and re-layouts: 7.66 us -> 4.96 us
  starting transfers between devices: 20.5 us -> 19.6 us
    pallas_call x9 -> x10, Pallas kernels: 13.6 us -> 10.8 us  [call(): pl.pallas_call(kernel, out_shape=out_shape, in_specs=specs, out_specs=[VM...]
    unnamed x23 -> x12, local copies, waits for them, and re-layouts: 7.56 us -> 4.96 us
    ppermute x18, starting transfers between devices: 17.8 us -> 16.9 us  [swap(): lax.ppermute(value, 'dp', [(i, i ^ 1 << bit_num) for i in range(count)])]
  transfers between devices with their start and end apart: 20 -> 20, of which waited for: 12 -> 11; matrix products, arithmetic and copies ran while one was open for 0% -> 0% of each run, Pallas kernels for 7% -> 4%
where the time goes in v2:
time: 70 us; the launch traced here: 69.7 us
  waiting for transfers between devices  32.8 us (47%)
  starting transfers between devices  19.6 us (28%)
  Pallas kernels  10.8 us (15%)
  local copies, waits for them, and re-layouts  4.96 us (7%)
  between operations  1.43 us (2%)
    ppermute x18, waiting for transfers between devices, swap(): lax.ppermute(value, 'dp', [(i, i ^ 1 << bit_num) for i in range(count)])  23 us
    ppermute x18, starting transfers between devices, swap(): lax.ppermute(value, 'dp', [(i, i ^ 1 << bit_num) for i in range(count)])  16.9 us
    pallas_call x10, Pallas kernels, call(): pl.pallas_call(kernel, out_shape=out_shape, in_specs=specs, out_specs=[VM...  10.8 us
    ppermute x2, waiting for transfers between devices, below(): lax.ppermute(value, 'section', [(i, i - 1) for i in range(1, section_coun...  9.77 us
    unnamed x12, local copies, waits for them, and re-layouts  4.96 us
    ppermute x2, starting transfers between devices, below(): lax.ppermute(value, 'section', [(i, i - 1) for i in range(1, section_coun...  2.72 us
  transfers between devices with their start and end apart: 20, of which 11 were waited for; matrix products, arithmetic and copies ran while one was open for 0% of the time, Pallas kernels for 4%

profile of v2, /device:TPU:0, one launch (start us, length us, event | category | flops | bytes accessed | tf_op | source)
XLA Modules:
  0.0 69.7 jit_solution(7399020941053455676)
XLA Ops:
  1.3 1.0 %copy-done.2 = bf16[1,4,128,512]{3,2,1,0:T(8,128)(2,1)S(1)} copy-done((bf16[1,4,128,512]{3,2,1,0:T(8,128)(2,1)S(1)}, bf16[1,4,128,512]{3,2,1,0:T(8,128)(2,1)}, u32[]{:S(2)}) %copy-start.2) | copy-done | bytes 524312
  2.3 1.0 %copy-done.3 = bf16[4,128,512]{2,1,0:T(8,128)(2,1)S(1)} copy-done((bf16[4,128,512]{2,1,0:T(8,128)(2,1)S(1)}, bf16[4,128,512]{2,1,0:T(8,128)(2,1)}, u32[]{:S(2)}) %copy-start.3) | copy-done | bytes 524312
  3.4 0.8 %copy-done.4 = bf16[1,50,512]{2,1,0:T(8,128)(2,1)S(1)} copy-done((bf16[1,50,512]{2,1,0:T(8,128)(2,1)S(1)}, bf16[1,50,512]{2,1,0:T(8,128)(2,1)}, u32[]{:S(2)}) %copy-start.4) | copy-done | bytes 51224
  4.2 0.7 copy-done.5
  4.8 5.3 %shard_map.85 = (f32[512,512]{1,0:T(8,128)S(1)}, bf16[512,512]{1,0:T(8,128)(2,1)S(1)}, bf16[512,1536]{1,0:T(8,128)(2,1)S(1)}, bf16[3,512,512]{2,1,0:T(8,128)(2,1...) custom-call(s32[1]{0:T(128)S(6)} %copy.9.dil, s32[4]{0:T(128)S(1)} %copy-done.5, ...), custom_call_target="tpu_custom_call" | custom-call | flops 1207959552 | bytes 8243220 | tf_op jit(solution)/shard_map/pallas_call | solution.py:24
  10.1 1.3 %collective-permute-start.1 = (bf16[512,256]{1,0:T(8,128)(2,1)S(1)}, bf16[512,256]{1,0:T(8,128)(2,1)S(1)}, u32[]{:S(2)}, u32[]{:S(2)}) collective-permute-start(bf16[512,256]{1,0:T(8,128)(2,1)S(1)} %get-tuple-element.37), channel_id=1, source_target_pairs={{16,0},{17,1},{18,2},{19,3},{20,4},{21,5},{22,6},{23,7},{24,8},{25... | collective-permute-start | bytes 786440 | tf_op jit(solution)/shard_map/ppermute | solution.py:259
  11.4 0.0 copy-start
  11.4 1.4 %copy-done = bf16[3,512,512]{2,1,0:T(8,128)(2,1)S(1)} copy-done((bf16[3,512,512]{2,1,0:T(8,128)(2,1)S(1)}, bf16[3,512,512]{2,1,0:T(8,128)(2,1)}, u32[]{:S(2)}) %copy-start) | copy-done | bytes 1572888
  12.8 0.6 shard_map.86
  13.4 0.0 copy-start.1
  13.5 1.4 %collective-permute-start = (bf16[512,256]{1,0:T(8,128)(2,1)S(1)}, bf16[512,256]{1,0:T(8,128)(2,1)S(1)}, u32[]{:S(2)}, u32[]{:S(2)}) collective-permute-start(bf16[512,256]{1,0:T(8,128)(2,1)S(1)} %get-tuple-element.33), channel_id=1, source_target_pairs={{16,0},{17,1},{18,2},{19,3},{20,4},{21,5},{22,6},{23,7},{24,8},{25... | collective-permute-start | bytes 786440 | tf_op jit(solution)/shard_map/ppermute | solution.py:259
  14.9 6.6 %collective-permute-done.1.recv = bf16[512,256]{1,0:T(8,128)(2,1)S(1)} collective-permute-done((bf16[512,256]{1,0:T(8,128)(2,1)S(1)}, bf16[512,256]{1,0:T(8,128)(2,1)S(1)}, u32[]{:S(2)}, u32[]{:S(2)}) %collective-permute-start.1) | collective-permute-done | bytes 262176 | tf_op jit(solution)/shard_map/ppermute | solution.py:259
  21.5 1.0 %shard_map.87 = (bf16[512,256]{1,0:T(8,128)(2,1)S(1)}, bf16[512,768]{1,0:T(8,128)(2,1)S(1)}, bf16[256,768]{1,0:T(8,128)(2,1)S(1)}, bf16[256,768]{1,0:T(8,128)(2,1)S(1)}) custom-call(s32[1]{0:T(128)S(6)} %copy.9.dil, bf16[4,128,512]{2,1,0:T(8,128)(2,1)S(1)} %get-tuple-element.29.top, bf16[512,256]{1,0:T(8,128)(2,1)S(1)} %collective-permute-done.1.recv, ...), custom_call_target="tpu_custom_call" | custom-call | flops 402653184 | bytes 4194308 | tf_op jit(solution)/shard_map/pallas_call | solution.py:24
  22.5 0.6 shard_map.88.rest_1_
  23.1 3.2 %collective-permute-done.recv = bf16[512,256]{1,0:T(8,128)(2,1)S(1)} collective-permute-done((bf16[512,256]{1,0:T(8,128)(2,1)S(1)}, bf16[512,256]{1,0:T(8,128)(2,1)S(1)}, u32[]{:S(2)}, u32[]{:S(2)}) %collective-permute-start) | collective-permute-done | bytes 262176 | tf_op jit(solution)/shard_map/ppermute | solution.py:259
  26.3 1.6 %shard_map.89 = (bf16[256,896]{1,0:T(8,128)(2,1)S(1)}, bf16[256,896]{1,0:T(8,128)(2,1)S(1)}, bf16[4,128,512]{2,1,0:T(8,128)(2,1)}) custom-call(s32[1]{0:T(128)S(6)} %copy.9.dil, bf16[4,128,512]{2,1,0:T(8,128)(2,1)S(1)} %get-tuple-element.29.top, bf16[512,256]{1,0:T(8,128)(2,1)S(1)} %collective-permute-done.recv, f32[512,512]{1,0:T(8,128)S(1)} %get-tuple-element.34.slope, ...), custom_call_target="tpu_custom_call" | custom-call | flops 805306368 | bytes 6750212 | tf_op jit(solution)/shard_map/pallas_call | solution.py:24
  27.9 0.5 collective-permute-start.2
  28.4 1.3 %collective-permute-done.11.recv = bf16[256,896]{1,0:T(8,128)(2,1)S(1)} collective-permute-done((bf16[256,896]{1,0:T(8,128)(2,1)S(1)}, bf16[256,896]{1,0:T(8,128)(2,1)S(1)}, u32[]{:S(2)}, u32[]{:S(2)}) %collective-permute-start.11) | collective-permute-done | bytes 458784 | tf_op jit(solution)/shard_map/ppermute | solution.py:218
  29.7 0.1 shard_map.92
  29.8 2.5 %collective-permute-start.12 = (bf16[128,896]{1,0:T(8,128)(2,1)S(1)}, bf16[128,896]{1,0:T(8,128)(2,1)S(1)}, u32[]{:S(2)}, u32[]{:S(2)}) collective-permute-start(bf16[128,896]{1,0:T(8,128)(2,1)S(1)} %get-tuple-element.50), channel_id=1, source_target_pairs={{0,4},{1,5},{2,6},{3,7},{4,0},{5,1},{6,2},{7,3},{8,12},{9,13},{10,... | collective-permute-start | bytes 688136 | tf_op jit(solution)/shard_map/ppermute | solution.py:218
  32.3 0.0 collective-permute-done.2.recv
  32.3 0.1 shard_map.90
  32.4 1.6 %collective-permute-start.3 = (bf16[128,768]{1,0:T(8,128)(2,1)S(1)}, bf16[128,768]{1,0:T(8,128)(2,1)S(1)}, u32[]{:S(2)}, u32[]{:S(2)}) collective-permute-start(bf16[128,768]{1,0:T(8,128)(2,1)S(1)} %get-tuple-element.44), channel_id=1, source_target_pairs={{0,2},{1,3},{2,0},{3,1},{4,6},{5,7},{6,4},{7,5},{8,10},{9,11},{10,... | collective-permute-start | bytes 589832 | tf_op jit(solution)/shard_map/ppermute | solution.py:218
  34.0 4.2 %collective-permute-done.12.recv = bf16[128,896]{1,0:T(8,128)(2,1)S(1)} collective-permute-done((bf16[128,896]{1,0:T(8,128)(2,1)S(1)}, bf16[128,896]{1,0:T(8,128)(2,1)S(1)}, u32[]{:S(2)}, u32[]{:S(2)}) %collective-permute-start.12) | collective-permute-done | bytes 229408 | tf_op jit(solution)/shard_map/ppermute | solution.py:218
  38.2 0.1 shard_map.93
  38.3 1.7 %collective-permute-start.13 = (bf16[64,896]{1,0:T(8,128)(2,1)S(1)}, bf16[64,896]{1,0:T(8,128)(2,1)S(1)}, u32[]{:S(2)}, u32[]{:S(2)}) collective-permute-start(bf16[64,896]{1,0:T(8,128)(2,1)S(1)} %get-tuple-element.52), channel_id=1, source_target_pairs={{0,2},{1,3},{2,0},{3,1},{4,6},{5,7},{6,4},{7,5},{8,10},{9,11},{10,... | collective-permute-start | bytes 344072 | tf_op jit(solution)/shard_map/ppermute | solution.py:218
  40.0 0.0 collective-permute-done.3.recv
  40.1 1.6 %collective-permute-start.4 = (bf16[64,768]{1,0:T(8,128)(2,1)S(1)}, bf16[64,768]{1,0:T(8,128)(2,1)S(1)}, u32[]{:S(2)}, u32[]{:S(2)}) collective-permute-start(bf16[64,768]{1,0:T(8,128)(2,1)S(1)} %get-tuple-element.46), channel_id=1, source_target_pairs={{0,4},{1,5},{2,6},{3,7},{4,0},{5,1},{6,2},{7,3},{8,12},{9,13},{10,... | collective-permute-start | bytes 294920 | tf_op jit(solution)/shard_map/ppermute | solution.py:218
  41.7 1.4 %collective-permute-done.13 = bf16[64,896]{1,0:T(8,128)(2,1)S(1)} collective-permute-done((bf16[64,896]{1,0:T(8,128)(2,1)S(1)}, bf16[64,896]{1,0:T(8,128)(2,1)S(1)}, u32[]{:S(2)}, u32[]{:S(2)}) %collective-permute-start.13) | collective-permute-done | bytes 114720 | tf_op jit(solution)/shard_map/ppermute | solution.py:218
  43.2 2.8 %collective-permute-start.14 = (bf16[64,896]{1,0:T(8,128)(2,1)S(1)}, bf16[64,896]{1,0:T(8,128)(2,1)S(1)}, u32[]{:S(2)}, u32[]{:S(2)}) collective-permute-start(bf16[64,896]{1,0:T(8,128)(2,1)S(1)} %add_convert_fusion.1), channel_id=1, source_target_pairs={{0,8},{1,9},{2,10},{3,11},{4,12},{5,13},{6,14},{7,15},{8,0},{9,1},... | collective-permute-start | bytes 344072 | tf_op jit(solution)/shard_map/ppermute | solution.py:218
  46.0 2.2 %collective-permute-start.5 = (bf16[64,768]{1,0:T(8,128)(2,1)S(1)}, bf16[64,768]{1,0:T(8,128)(2,1)S(1)}, u32[]{:S(2)}, u32[]{:S(2)}) collective-permute-start(bf16[64,768]{1,0:T(8,128)(2,1)S(1)} %add_convert_fusion.3), channel_id=1, source_target_pairs={{0,8},{1,9},{2,10},{3,11},{4,12},{5,13},{6,14},{7,15},{8,0},{9,1},... | collective-permute-start | bytes 294920 | tf_op jit(solution)/shard_map/ppermute | solution.py:218
  48.2 5.4 %collective-permute-done.14 = bf16[64,896]{1,0:T(8,128)(2,1)S(1)} collective-permute-done((bf16[64,896]{1,0:T(8,128)(2,1)S(1)}, bf16[64,896]{1,0:T(8,128)(2,1)S(1)}, u32[]{:S(2)}, u32[]{:S(2)}) %collective-permute-start.14) | collective-permute-done | bytes 114720 | tf_op jit(solution)/shard_map/ppermute | solution.py:218
  53.6 1.1 %collective-permute-start.15 = (bf16[64,896]{1,0:T(8,128)(2,1)S(1)}, bf16[64,896]{1,0:T(8,128)(2,1)S(1)}, u32[]{:S(2)}, u32[]{:S(2)}) collective-permute-start(bf16[64,896]{1,0:T(8,128)(2,1)S(1)} %add_convert_fusion.refs_6_), channel_id=1, source_target_pairs={{0,2},{1,3},{2,0},{3,1},{4,6},{5,7},{6,4},{7,5},{8,10},{9,11},{10,... | collective-permute-start | bytes 344072 | tf_op jit(solution)/shard_map/ppermute | solution.py:218
  54.7 0.0 collective-permute-done.5
  54.8 0.3 collective-permute-start.6
  55.0 3.4 %collective-permute-done.15.refs_7_ = bf16[64,896]{1,0:T(8,128)(2,1)S(1)} collective-permute-done((bf16[64,896]{1,0:T(8,128)(2,1)S(1)}, bf16[64,896]{1,0:T(8,128)(2,1)S(1)}, u32[]{:S(2)}, u32[]{:S(2)}) %collective-permute-start.15) | collective-permute-done | bytes 114720 | tf_op jit(solution)/shard_map/ppermute | solution.py:218
  58.5 0.1 collective-permute-start.16
  58.6 2.0 %collective-permute-done.6.refs_1_ = bf16[64,768]{1,0:T(8,128)(2,1)S(1)} collective-permute-done((bf16[64,768]{1,0:T(8,128)(2,1)S(1)}, bf16[64,768]{1,0:T(8,128)(2,1)S(1)}, u32[]{:S(2)}, u32[]{:S(2)}) %collective-permute-start.6) | collective-permute-done | bytes 98336 | tf_op jit(solution)/shard_map/ppermute | solution.py:218
  60.6 1.0 %collective-permute-start.7 = (bf16[128,768]{1,0:T(8,128)(2,1)S(1)}, bf16[128,768]{1,0:T(8,128)(2,1)S(1)}, u32[]{:S(2)}, u32[]{:S(2)}) collective-permute-start(bf16[128,768]{1,0:T(8,128)(2,1)S(1)} %pad_maximum_fusion.1), channel_id=1, source_target_pairs={{0,2},{1,3},{2,0},{3,1},{4,6},{5,7},{6,4},{7,5},{8,10},{9,11},{10,... | collective-permute-start | bytes 589832 | tf_op jit(solution)/shard_map/ppermute | solution.py:218
  61.6 3.0 %collective-permute-done.16.refs_8_ = bf16[128,896]{1,0:T(8,128)(2,1)S(1)} collective-permute-done((bf16[128,896]{1,0:T(8,128)(2,1)S(1)}, bf16[128,896]{1,0:T(8,128)(2,1)S(1)}, u32[]{:S(2)}, u32[]{:S(2)}) %collective-permute-start.16) | collective-permute-done | bytes 229408 | tf_op jit(solution)/shard_map/ppermute | solution.py:218
  64.6 0.5 collective-permute-start.8
  65.1 1.2 %collective-permute-done.7.refs_2_ = bf16[128,768]{1,0:T(8,128)(2,1)S(1)} collective-permute-done((bf16[128,768]{1,0:T(8,128)(2,1)S(1)}, bf16[128,768]{1,0:T(8,128)(2,1)S(1)}, u32[]{:S(2)}, u32[]{:S(2)}) %collective-permute-start.7) | collective-permute-done | bytes 196640 | tf_op jit(solution)/shard_map/ppermute | solution.py:218
  66.3 0.5 collective-permute-start.17
  66.8 0.0 collective-permute-start.18
  66.8 0.0 collective-permute-done.8.refs_3_
  66.8 0.5 collective-permute-start.9
  67.3 1.0 %collective-permute-done.9.refs_4_ = bf16[64,768]{1,0:T(8,128)(2,1)S(1)} collective-permute-done((bf16[64,768]{1,0:T(8,128)(2,1)S(1)}, bf16[64,768]{1,0:T(8,128)(2,1)S(1)}, u32[]{:S(2)}, u32[]{:S(2)}) %collective-permute-start.9) | collective-permute-done | bytes 98336 | tf_op jit(solution)/shard_map/ppermute | solution.py:218
  68.3 1.3 %shard_map.94 = (bf16[3,512,512]{2,1,0:T(8,128)(2,1)}, bf16[50,512]{1,0:T(8,128)(2,1)}) custom-call(bf16[64,768]{1,0:T(8,128)(2,1)S(1)} %add_convert_fusion.2.refs_0_, bf16[64,768]{1,0:T(8,128)(2,1)S(1)} %collective-permute-done.6.refs_1_, bf16[128,768]{1,0:T(8,128)(2,1)S(1)} %collective-permute-done.7.refs_2_, ...), custom_call_target="tpu_custom_call" | custom-call | bytes 3328000 | tf_op jit(solution)/shard_map/pallas_call | solution.py:24
  (20 shorter events, 0.2 us)
Async XLA Ops:
  1.3 1.0 %copy-start.2 = (bf16[1,4,128,512]{3,2,1,0:T(8,128)(2,1)S(1)}, bf16[1,4,128,512]{3,2,1,0:T(8,128)(2,1)}, u32[]{:S(2)}) copy-start(bf16[1,4,128,512]{3,2,1,0:T(8,128)(2,1)} %param.6) | copy-start | bytes 1572868
  2.3 1.0 %copy-start.3 = (bf16[4,128,512]{2,1,0:T(8,128)(2,1)S(1)}, bf16[4,128,512]{2,1,0:T(8,128)(2,1)}, u32[]{:S(2)}) copy-start(bf16[4,128,512]{2,1,0:T(8,128)(2,1)} %top.1) | copy-start | bytes 1572868
  3.4 0.8 %copy-start.4 = (bf16[1,50,512]{2,1,0:T(8,128)(2,1)S(1)}, bf16[1,50,512]{2,1,0:T(8,128)(2,1)}, u32[]{:S(2)}) copy-start(bf16[1,50,512]{2,1,0:T(8,128)(2,1)} %param.9) | copy-start | bytes 153604
  4.2 0.7 copy-start.5
  10.1 11.3 %collective-permute-start.1 = (bf16[512,256]{1,0:T(8,128)(2,1)S(1)}, bf16[512,256]{1,0:T(8,128)(2,1)S(1)}, u32[]{:S(2)}, u32[]{:S(2)}) collective-permute-start(bf16[512,256]{1,0:T(8,128)(2,1)S(1)} %get-tuple-element.37), channel_id=1, source_target_pairs={{16,0},{17,1},{18,2},{19,3},{20,4},{21,5},{22,6},{23,7},{24,8},{25... | collective-permute-start | bytes 786440 | tf_op jit(solution)/shard_map/ppermute | solution.py:259
  11.4 1.4 %copy-start = (bf16[3,512,512]{2,1,0:T(8,128)(2,1)S(1)}, bf16[3,512,512]{2,1,0:T(8,128)(2,1)}, u32[]{:S(2)}) copy-start(bf16[3,512,512]{2,1,0:T(8,128)(2,1)} %get-tuple-element.32.weight) | copy-start | bytes 4718596
  13.4 9.0 %copy-start.1 = (bf16[3,512,512]{2,1,0:T(8,128)(2,1)S(1)}, bf16[3,512,512]{2,1,0:T(8,128)(2,1)}, u32[]{:S(2)}) copy-start(bf16[3,512,512]{2,1,0:T(8,128)(2,1)} %get-tuple-element.32.weight) | copy-start | bytes 4718596
  13.5 12.8 %collective-permute-start = (bf16[512,256]{1,0:T(8,128)(2,1)S(1)}, bf16[512,256]{1,0:T(8,128)(2,1)S(1)}, u32[]{:S(2)}, u32[]{:S(2)}) collective-permute-start(bf16[512,256]{1,0:T(8,128)(2,1)S(1)} %get-tuple-element.33), channel_id=1, source_target_pairs={{16,0},{17,1},{18,2},{19,3},{20,4},{21,5},{22,6},{23,7},{24,8},{25... | collective-permute-start | bytes 786440 | tf_op jit(solution)/shard_map/ppermute | solution.py:259
  27.9 1.8 %collective-permute-start.11 = (bf16[256,896]{1,0:T(8,128)(2,1)S(1)}, bf16[256,896]{1,0:T(8,128)(2,1)S(1)}, u32[]{:S(2)}, u32[]{:S(2)}) collective-permute-start(bf16[256,896]{1,0:T(8,128)(2,1)S(1)} %get-tuple-element.48), channel_id=1, source_target_pairs={{0,1},{1,0},{2,3},{3,2},{4,5},{5,4},{6,7},{7,6},{8,9},{9,8},{10,11... | collective-permute-start | bytes 1376264 | tf_op jit(solution)/shard_map/ppermute | solution.py:218
  27.9 4.4 %collective-permute-start.2 = (bf16[256,768]{1,0:T(8,128)(2,1)S(1)}, bf16[256,768]{1,0:T(8,128)(2,1)S(1)}, u32[]{:S(2)}, u32[]{:S(2)}) collective-permute-start(bf16[256,768]{1,0:T(8,128)(2,1)S(1)} %get-tuple-element.42), channel_id=1, source_target_pairs={{0,1},{1,0},{2,3},{3,2},{4,5},{5,4},{6,7},{7,6},{8,9},{9,8},{10,11... | collective-permute-start | bytes 1179656 | tf_op jit(solution)/shard_map/ppermute | solution.py:218
  29.8 8.4 %collective-permute-start.12 = (bf16[128,896]{1,0:T(8,128)(2,1)S(1)}, bf16[128,896]{1,0:T(8,128)(2,1)S(1)}, u32[]{:S(2)}, u32[]{:S(2)}) collective-permute-start(bf16[128,896]{1,0:T(8,128)(2,1)S(1)} %get-tuple-element.50), channel_id=1, source_target_pairs={{0,4},{1,5},{2,6},{3,7},{4,0},{5,1},{6,2},{7,3},{8,12},{9,13},{10,... | collective-permute-start | bytes 688136 | tf_op jit(solution)/shard_map/ppermute | solution.py:218
  32.4 7.6 %collective-permute-start.3 = (bf16[128,768]{1,0:T(8,128)(2,1)S(1)}, bf16[128,768]{1,0:T(8,128)(2,1)S(1)}, u32[]{:S(2)}, u32[]{:S(2)}) collective-permute-start(bf16[128,768]{1,0:T(8,128)(2,1)S(1)} %get-tuple-element.44), channel_id=1, source_target_pairs={{0,2},{1,3},{2,0},{3,1},{4,6},{5,7},{6,4},{7,5},{8,10},{9,11},{10,... | collective-permute-start | bytes 589832 | tf_op jit(solution)/shard_map/ppermute | solution.py:218
  38.3 4.9 %collective-permute-start.13 = (bf16[64,896]{1,0:T(8,128)(2,1)S(1)}, bf16[64,896]{1,0:T(8,128)(2,1)S(1)}, u32[]{:S(2)}, u32[]{:S(2)}) collective-permute-start(bf16[64,896]{1,0:T(8,128)(2,1)S(1)} %get-tuple-element.52), channel_id=1, source_target_pairs={{0,2},{1,3},{2,0},{3,1},{4,6},{5,7},{6,4},{7,5},{8,10},{9,11},{10,... | collective-permute-start | bytes 344072 | tf_op jit(solution)/shard_map/ppermute | solution.py:218
  40.1 5.9 %collective-permute-start.4 = (bf16[64,768]{1,0:T(8,128)(2,1)S(1)}, bf16[64,768]{1,0:T(8,128)(2,1)S(1)}, u32[]{:S(2)}, u32[]{:S(2)}) collective-permute-start(bf16[64,768]{1,0:T(8,128)(2,1)S(1)} %get-tuple-element.46), channel_id=1, source_target_pairs={{0,4},{1,5},{2,6},{3,7},{4,0},{5,1},{6,2},{7,3},{8,12},{9,13},{10,... | collective-permute-start | bytes 294920 | tf_op jit(solution)/shard_map/ppermute | solution.py:218
  43.2 10.4 %collective-permute-start.14 = (bf16[64,896]{1,0:T(8,128)(2,1)S(1)}, bf16[64,896]{1,0:T(8,128)(2,1)S(1)}, u32[]{:S(2)}, u32[]{:S(2)}) collective-permute-start(bf16[64,896]{1,0:T(8,128)(2,1)S(1)} %add_convert_fusion.1), channel_id=1, source_target_pairs={{0,8},{1,9},{2,10},{3,11},{4,12},{5,13},{6,14},{7,15},{8,0},{9,1},... | collective-permute-start | bytes 344072 | tf_op jit(solution)/shard_map/ppermute | solution.py:218
  46.0 8.7 %collective-permute-start.5 = (bf16[64,768]{1,0:T(8,128)(2,1)S(1)}, bf16[64,768]{1,0:T(8,128)(2,1)S(1)}, u32[]{:S(2)}, u32[]{:S(2)}) collective-permute-start(bf16[64,768]{1,0:T(8,128)(2,1)S(1)} %add_convert_fusion.3), channel_id=1, source_target_pairs={{0,8},{1,9},{2,10},{3,11},{4,12},{5,13},{6,14},{7,15},{8,0},{9,1},... | collective-permute-start | bytes 294920 | tf_op jit(solution)/shard_map/ppermute | solution.py:218
  53.6 4.9 %collective-permute-start.15 = (bf16[64,896]{1,0:T(8,128)(2,1)S(1)}, bf16[64,896]{1,0:T(8,128)(2,1)S(1)}, u32[]{:S(2)}, u32[]{:S(2)}) collective-permute-start(bf16[64,896]{1,0:T(8,128)(2,1)S(1)} %add_convert_fusion.refs_6_), channel_id=1, source_target_pairs={{0,2},{1,3},{2,0},{3,1},{4,6},{5,7},{6,4},{7,5},{8,10},{9,11},{10,... | collective-permute-start | bytes 344072 | tf_op jit(solution)/shard_map/ppermute | solution.py:218
  54.8 5.8 %collective-permute-start.6 = (bf16[64,768]{1,0:T(8,128)(2,1)S(1)}, bf16[64,768]{1,0:T(8,128)(2,1)S(1)}, u32[]{:S(2)}, u32[]{:S(2)}) collective-permute-start(bf16[64,768]{1,0:T(8,128)(2,1)S(1)} %add_convert_fusion.2.refs_0_), channel_id=1, source_target_pairs={{0,4},{1,5},{2,6},{3,7},{4,0},{5,1},{6,2},{7,3},{8,12},{9,13},{10,... | collective-permute-start | bytes 294920 | tf_op jit(solution)/shard_map/ppermute | solution.py:218
  58.5 6.1 %collective-permute-start.16 = (bf16[128,896]{1,0:T(8,128)(2,1)S(1)}, bf16[128,896]{1,0:T(8,128)(2,1)S(1)}, u32[]{:S(2)}, u32[]{:S(2)}) collective-permute-start(bf16[128,896]{1,0:T(8,128)(2,1)S(1)} %pad_maximum_fusion), channel_id=1, source_target_pairs={{0,4},{1,5},{2,6},{3,7},{4,0},{5,1},{6,2},{7,3},{8,12},{9,13},{10,... | collective-permute-start | bytes 688136 | tf_op jit(solution)/shard_map/ppermute | solution.py:218
  60.6 5.7 %collective-permute-start.7 = (bf16[128,768]{1,0:T(8,128)(2,1)S(1)}, bf16[128,768]{1,0:T(8,128)(2,1)S(1)}, u32[]{:S(2)}, u32[]{:S(2)}) collective-permute-start(bf16[128,768]{1,0:T(8,128)(2,1)S(1)} %pad_maximum_fusion.1), channel_id=1, source_target_pairs={{0,2},{1,3},{2,0},{3,1},{4,6},{5,7},{6,4},{7,5},{8,10},{9,11},{10,... | collective-permute-start | bytes 589832 | tf_op jit(solution)/shard_map/ppermute | solution.py:218
  64.6 3.7 %collective-permute-start.19 = (bf16[128,896]{1,0:T(8,128)(2,1)S(1)}, bf16[128,896]{1,0:T(8,128)(2,1)S(1)}, u32[]{:S(2)}, u32[]{:S(2)}) collective-permute-start(bf16[128,896]{1,0:T(8,128)(2,1)S(1)} %collective-permute-done.16.refs_8_), channel_id=1, source_target_pairs={{0,1},{1,0},{2,3},{3,2},{4,5},{5,4},{6,7},{7,6},{8,9},{9,8},{10,11... | collective-permute-start | bytes 688136 | tf_op jit(solution)/shard_map/ppermute | solution.py:218
  64.6 2.2 %collective-permute-start.8 = (bf16[64,768]{1,0:T(8,128)(2,1)S(1)}, bf16[64,768]{1,0:T(8,128)(2,1)S(1)}, u32[]{:S(2)}, u32[]{:S(2)}) collective-permute-start(bf16[64,768]{1,0:T(8,128)(2,1)S(1)} %add_convert_fusion.2.refs_0_), channel_id=1, source_target_pairs={{0,1},{1,0},{2,3},{3,2},{4,5},{5,4},{6,7},{7,6},{8,9},{9,8},{10,11... | collective-permute-start | bytes 294920 | tf_op jit(solution)/shard_map/ppermute | solution.py:218
  66.3 2.0 %collective-permute-start.10 = (bf16[128,768]{1,0:T(8,128)(2,1)S(1)}, bf16[128,768]{1,0:T(8,128)(2,1)S(1)}, u32[]{:S(2)}, u32[]{:S(2)}) collective-permute-start(bf16[128,768]{1,0:T(8,128)(2,1)S(1)} %collective-permute-done.7.refs_2_), channel_id=1, source_target_pairs={{0,1},{1,0},{2,3},{3,2},{4,5},{5,4},{6,7},{7,6},{8,9},{9,8},{10,11... | collective-permute-start | bytes 589832 | tf_op jit(solution)/shard_map/ppermute | solution.py:218
  66.3 2.0 %collective-permute-start.17 = (bf16[64,896]{1,0:T(8,128)(2,1)S(1)}, bf16[64,896]{1,0:T(8,128)(2,1)S(1)}, u32[]{:S(2)}, u32[]{:S(2)}) collective-permute-start(bf16[64,896]{1,0:T(8,128)(2,1)S(1)} %add_convert_fusion.refs_6_), channel_id=1, source_target_pairs={{0,1},{1,0},{2,3},{3,2},{4,5},{5,4},{6,7},{7,6},{8,9},{9,8},{10,11... | collective-permute-start | bytes 344072 | tf_op jit(solution)/shard_map/ppermute | solution.py:218
  66.8 1.5 %collective-permute-start.18 = (bf16[64,896]{1,0:T(8,128)(2,1)S(1)}, bf16[64,896]{1,0:T(8,128)(2,1)S(1)}, u32[]{:S(2)}, u32[]{:S(2)}) collective-permute-start(bf16[64,896]{1,0:T(8,128)(2,1)S(1)} %collective-permute-done.15.refs_7_), channel_id=1, source_target_pairs={{0,1},{1,0},{2,3},{3,2},{4,5},{5,4},{6,7},{7,6},{8,9},{9,8},{10,11... | collective-permute-start | bytes 344072 | tf_op jit(solution)/shard_map/ppermute | solution.py:218
  66.8 1.5 %collective-permute-start.9 = (bf16[64,768]{1,0:T(8,128)(2,1)S(1)}, bf16[64,768]{1,0:T(8,128)(2,1)S(1)}, u32[]{:S(2)}, u32[]{:S(2)}) collective-permute-start(bf16[64,768]{1,0:T(8,128)(2,1)S(1)} %collective-permute-done.6.refs_1_), channel_id=1, source_target_pairs={{0,1},{1,0},{2,3},{3,2},{4,5},{5,4},{6,7},{7,6},{8,9},{9,8},{10,11... | collective-permute-start | bytes 294920 | tf_op jit(solution)/shard_map/ppermute | solution.py:218

commit v3 on v2

--- a/solution.py
+++ b/solution.py
@@ -242,7 +242,7 @@
             like((128, 128), F32),
             like((rows, width), BF16),
         ],
-        (dilations, timesteps, x, table, weight, top_grad),
+        (dilations,) + tuple(pltpu.with_memory_space_constraint(v, pltpu.HBM) for v in (timesteps, x, table, weight, top_grad)),
         smem=1,
         far=5,
         scratch=[

time: 70 us -> 66.4 us (0.949)
  local copies, waits for them, and re-layouts: 4.96 us -> 0 us
  waiting for transfers between devices: 32.8 us -> 34.3 us
    unnamed x12 -> x0, local copies, waits for them, and re-layouts: 4.96 us -> none
    ppermute x2, waiting for transfers between devices: 9.77 us -> 11.3 us  [below(): lax.ppermute(value, 'section', [(i, i - 1) for i in range(1, section_coun...]
where the time goes in v3:
time: 66.4 us; the launch traced here: 66.2 us
  waiting for transfers between devices  34.3 us (52%)
  starting transfers between devices  19.5 us (29%)
  Pallas kernels  10.9 us (16%)
  between operations  1.39 us (2%)
    ppermute x18, waiting for transfers between devices, swap(): lax.ppermute(value, 'dp', [(i, i ^ 1 << bit_num) for i in range(count)])  23 us
    ppermute x18, starting transfers between devices, swap(): lax.ppermute(value, 'dp', [(i, i ^ 1 << bit_num) for i in range(count)])  16.9 us
    ppermute x2, waiting for transfers between devices, below(): lax.ppermute(value, 'section', [(i, i - 1) for i in range(1, section_coun...  11.3 us
    pallas_call x10, Pallas kernels, call(): pl.pallas_call(kernel, out_shape=out_shape, in_specs=specs, out_specs=[VM...  10.9 us
    ppermute x2, starting transfers between devices, below(): lax.ppermute(value, 'section', [(i, i - 1) for i in range(1, section_coun...  2.58 us
  transfers between devices with their start and end apart: 20, of which 11 were waited for; matrix products, arithmetic and copies ran while one was open for 0% of the time, Pallas kernels for 4%

profile of v3, /device:TPU:0, one launch (start us, length us, event | category | flops | bytes accessed | tf_op | source)
XLA Modules:
  0.0 66.2 jit_solution(3199978349174596766)
XLA Ops:
  1.3 5.4 %shard_map.85 = (f32[512,512]{1,0:T(8,128)S(1)}, bf16[512,512]{1,0:T(8,128)(2,1)S(1)}, bf16[512,1536]{1,0:T(8,128)(2,1)S(1)}, bf16[3,512,512]{2,1,0:T(8,128)(2,1...) custom-call(s32[1]{0:T(128)S(6)} %copy.9.dil, s32[4]{0:T(128)} %ts.1, ...), custom_call_target="tpu_custom_call" | custom-call | flops 1207959552 | bytes 8243220 | tf_op jit(solution)/shard_map/pallas_call | solution.py:24
  6.7 1.3 %collective-permute-start.1 = (bf16[512,256]{1,0:T(8,128)(2,1)S(1)}, bf16[512,256]{1,0:T(8,128)(2,1)S(1)}, u32[]{:S(2)}, u32[]{:S(2)}) collective-permute-start(bf16[512,256]{1,0:T(8,128)(2,1)S(1)} %get-tuple-element.37), channel_id=1, source_target_pairs={{16,0},{17,1},{18,2},{19,3},{20,4},{21,5},{22,6},{23,7},{24,8},{25... | collective-permute-start | bytes 786440 | tf_op jit(solution)/shard_map/ppermute | solution.py:259
  8.0 0.6 shard_map.86
  8.6 1.3 %collective-permute-start = (bf16[512,256]{1,0:T(8,128)(2,1)S(1)}, bf16[512,256]{1,0:T(8,128)(2,1)S(1)}, u32[]{:S(2)}, u32[]{:S(2)}) collective-permute-start(bf16[512,256]{1,0:T(8,128)(2,1)S(1)} %get-tuple-element.33), channel_id=1, source_target_pairs={{16,0},{17,1},{18,2},{19,3},{20,4},{21,5},{22,6},{23,7},{24,8},{25... | collective-permute-start | bytes 786440 | tf_op jit(solution)/shard_map/ppermute | solution.py:259
  9.9 8.1 %collective-permute-done.1.recv = bf16[512,256]{1,0:T(8,128)(2,1)S(1)} collective-permute-done((bf16[512,256]{1,0:T(8,128)(2,1)S(1)}, bf16[512,256]{1,0:T(8,128)(2,1)S(1)}, u32[]{:S(2)}, u32[]{:S(2)}) %collective-permute-start.1) | collective-permute-done | bytes 262176 | tf_op jit(solution)/shard_map/ppermute | solution.py:259
  18.0 1.0 %shard_map.87 = (bf16[512,256]{1,0:T(8,128)(2,1)S(1)}, bf16[512,768]{1,0:T(8,128)(2,1)S(1)}, bf16[256,768]{1,0:T(8,128)(2,1)S(1)}, bf16[256,768]{1,0:T(8,128)(2,1)S(1)}) custom-call(s32[1]{0:T(128)S(6)} %copy.9.dil, bf16[4,128,512]{2,1,0:T(8,128)(2,1)S(1)} %get-tuple-element.29.top, bf16[512,256]{1,0:T(8,128)(2,1)S(1)} %collective-permute-done.1.recv, ...), custom_call_target="tpu_custom_call" | custom-call | flops 402653184 | bytes 4194308 | tf_op jit(solution)/shard_map/pallas_call | solution.py:24
  19.1 0.6 shard_map.88.rest_1_
  19.7 3.2 %collective-permute-done.recv = bf16[512,256]{1,0:T(8,128)(2,1)S(1)} collective-permute-done((bf16[512,256]{1,0:T(8,128)(2,1)S(1)}, bf16[512,256]{1,0:T(8,128)(2,1)S(1)}, u32[]{:S(2)}, u32[]{:S(2)}) %collective-permute-start) | collective-permute-done | bytes 262176 | tf_op jit(solution)/shard_map/ppermute | solution.py:259
  22.9 1.6 %shard_map.89 = (bf16[256,896]{1,0:T(8,128)(2,1)S(1)}, bf16[256,896]{1,0:T(8,128)(2,1)S(1)}, bf16[4,128,512]{2,1,0:T(8,128)(2,1)}) custom-call(s32[1]{0:T(128)S(6)} %copy.9.dil, bf16[4,128,512]{2,1,0:T(8,128)(2,1)S(1)} %get-tuple-element.29.top, bf16[512,256]{1,0:T(8,128)(2,1)S(1)} %collective-permute-done.recv, f32[512,512]{1,0:T(8,128)S(1)} %get-tuple-element.34.slope, ...), custom_call_target="tpu_custom_call" | custom-call | flops 805306368 | bytes 6750212 | tf_op jit(solution)/shard_map/pallas_call | solution.py:24
  24.5 0.0 collective-permute-start.11
  24.5 0.5 collective-permute-start.2
  25.0 1.3 %collective-permute-done.11.recv = bf16[256,896]{1,0:T(8,128)(2,1)S(1)} collective-permute-done((bf16[256,896]{1,0:T(8,128)(2,1)S(1)}, bf16[256,896]{1,0:T(8,128)(2,1)S(1)}, u32[]{:S(2)}, u32[]{:S(2)}) %collective-permute-start.11) | collective-permute-done | bytes 458784 | tf_op jit(solution)/shard_map/ppermute | solution.py:218
  26.3 0.1 shard_map.92
  26.4 2.5 %collective-permute-start.12 = (bf16[128,896]{1,0:T(8,128)(2,1)S(1)}, bf16[128,896]{1,0:T(8,128)(2,1)S(1)}, u32[]{:S(2)}, u32[]{:S(2)}) collective-permute-start(bf16[128,896]{1,0:T(8,128)(2,1)S(1)} %get-tuple-element.50), channel_id=1, source_target_pairs={{0,4},{1,5},{2,6},{3,7},{4,0},{5,1},{6,2},{7,3},{8,12},{9,13},{10,... | collective-permute-start | bytes 688136 | tf_op jit(solution)/shard_map/ppermute | solution.py:218
  28.9 0.0 collective-permute-done.2.recv
  28.9 0.1 shard_map.90
  29.0 1.6 %collective-permute-start.3 = (bf16[128,768]{1,0:T(8,128)(2,1)S(1)}, bf16[128,768]{1,0:T(8,128)(2,1)S(1)}, u32[]{:S(2)}, u32[]{:S(2)}) collective-permute-start(bf16[128,768]{1,0:T(8,128)(2,1)S(1)} %get-tuple-element.44), channel_id=1, source_target_pairs={{0,2},{1,3},{2,0},{3,1},{4,6},{5,7},{6,4},{7,5},{8,10},{9,11},{10,... | collective-permute-start | bytes 589832 | tf_op jit(solution)/shard_map/ppermute | solution.py:218
  30.6 4.2 %collective-permute-done.12.recv = bf16[128,896]{1,0:T(8,128)(2,1)S(1)} collective-permute-done((bf16[128,896]{1,0:T(8,128)(2,1)S(1)}, bf16[128,896]{1,0:T(8,128)(2,1)S(1)}, u32[]{:S(2)}, u32[]{:S(2)}) %collective-permute-start.12) | collective-permute-done | bytes 229408 | tf_op jit(solution)/shard_map/ppermute | solution.py:218
  34.8 0.1 shard_map.93
  34.9 1.7 %collective-permute-start.13 = (bf16[64,896]{1,0:T(8,128)(2,1)S(1)}, bf16[64,896]{1,0:T(8,128)(2,1)S(1)}, u32[]{:S(2)}, u32[]{:S(2)}) collective-permute-start(bf16[64,896]{1,0:T(8,128)(2,1)S(1)} %get-tuple-element.52), channel_id=1, source_target_pairs={{0,2},{1,3},{2,0},{3,1},{4,6},{5,7},{6,4},{7,5},{8,10},{9,11},{10,... | collective-permute-start | bytes 344072 | tf_op jit(solution)/shard_map/ppermute | solution.py:218
  36.6 0.0 collective-permute-done.3.recv
  36.7 1.6 %collective-permute-start.4 = (bf16[64,768]{1,0:T(8,128)(2,1)S(1)}, bf16[64,768]{1,0:T(8,128)(2,1)S(1)}, u32[]{:S(2)}, u32[]{:S(2)}) collective-permute-start(bf16[64,768]{1,0:T(8,128)(2,1)S(1)} %get-tuple-element.46), channel_id=1, source_target_pairs={{0,4},{1,5},{2,6},{3,7},{4,0},{5,1},{6,2},{7,3},{8,12},{9,13},{10,... | collective-permute-start | bytes 294920 | tf_op jit(solution)/shard_map/ppermute | solution.py:218
  38.3 1.4 %collective-permute-done.13 = bf16[64,896]{1,0:T(8,128)(2,1)S(1)} collective-permute-done((bf16[64,896]{1,0:T(8,128)(2,1)S(1)}, bf16[64,896]{1,0:T(8,128)(2,1)S(1)}, u32[]{:S(2)}, u32[]{:S(2)}) %collective-permute-start.13) | collective-permute-done | bytes 114720 | tf_op jit(solution)/shard_map/ppermute | solution.py:218
  39.7 2.8 %collective-permute-start.14 = (bf16[64,896]{1,0:T(8,128)(2,1)S(1)}, bf16[64,896]{1,0:T(8,128)(2,1)S(1)}, u32[]{:S(2)}, u32[]{:S(2)}) collective-permute-start(bf16[64,896]{1,0:T(8,128)(2,1)S(1)} %add_convert_fusion.1), channel_id=1, source_target_pairs={{0,8},{1,9},{2,10},{3,11},{4,12},{5,13},{6,14},{7,15},{8,0},{9,1},... | collective-permute-start | bytes 344072 | tf_op jit(solution)/shard_map/ppermute | solution.py:218
  42.6 0.0 collective-permute-done.4
  42.6 2.2 %collective-permute-start.5 = (bf16[64,768]{1,0:T(8,128)(2,1)S(1)}, bf16[64,768]{1,0:T(8,128)(2,1)S(1)}, u32[]{:S(2)}, u32[]{:S(2)}) collective-permute-start(bf16[64,768]{1,0:T(8,128)(2,1)S(1)} %add_convert_fusion.3), channel_id=1, source_target_pairs={{0,8},{1,9},{2,10},{3,11},{4,12},{5,13},{6,14},{7,15},{8,0},{9,1},... | collective-permute-start | bytes 294920 | tf_op jit(solution)/shard_map/ppermute | solution.py:218
  44.8 5.4 %collective-permute-done.14 = bf16[64,896]{1,0:T(8,128)(2,1)S(1)} collective-permute-done((bf16[64,896]{1,0:T(8,128)(2,1)S(1)}, bf16[64,896]{1,0:T(8,128)(2,1)S(1)}, u32[]{:S(2)}, u32[]{:S(2)}) %collective-permute-start.14) | collective-permute-done | bytes 114720 | tf_op jit(solution)/shard_map/ppermute | solution.py:218
  50.2 1.1 %collective-permute-start.15 = (bf16[64,896]{1,0:T(8,128)(2,1)S(1)}, bf16[64,896]{1,0:T(8,128)(2,1)S(1)}, u32[]{:S(2)}, u32[]{:S(2)}) collective-permute-start(bf16[64,896]{1,0:T(8,128)(2,1)S(1)} %add_convert_fusion.refs_6_), channel_id=1, source_target_pairs={{0,2},{1,3},{2,0},{3,1},{4,6},{5,7},{6,4},{7,5},{8,10},{9,11},{10,... | collective-permute-start | bytes 344072 | tf_op jit(solution)/shard_map/ppermute | solution.py:218
  51.3 0.0 collective-permute-done.5
  51.4 0.3 collective-permute-start.6
  51.6 3.4 %collective-permute-done.15.refs_7_ = bf16[64,896]{1,0:T(8,128)(2,1)S(1)} collective-permute-done((bf16[64,896]{1,0:T(8,128)(2,1)S(1)}, bf16[64,896]{1,0:T(8,128)(2,1)S(1)}, u32[]{:S(2)}, u32[]{:S(2)}) %collective-permute-start.15) | collective-permute-done | bytes 114720 | tf_op jit(solution)/shard_map/ppermute | solution.py:218
  55.1 0.1 collective-permute-start.16
  55.2 2.0 %collective-permute-done.6.refs_1_ = bf16[64,768]{1,0:T(8,128)(2,1)S(1)} collective-permute-done((bf16[64,768]{1,0:T(8,128)(2,1)S(1)}, bf16[64,768]{1,0:T(8,128)(2,1)S(1)}, u32[]{:S(2)}, u32[]{:S(2)}) %collective-permute-start.6) | collective-permute-done | bytes 98336 | tf_op jit(solution)/shard_map/ppermute | solution.py:218
  57.2 1.0 %collective-permute-start.7 = (bf16[128,768]{1,0:T(8,128)(2,1)S(1)}, bf16[128,768]{1,0:T(8,128)(2,1)S(1)}, u32[]{:S(2)}, u32[]{:S(2)}) collective-permute-start(bf16[128,768]{1,0:T(8,128)(2,1)S(1)} %pad_maximum_fusion.1), channel_id=1, source_target_pairs={{0,2},{1,3},{2,0},{3,1},{4,6},{5,7},{6,4},{7,5},{8,10},{9,11},{10,... | collective-permute-start | bytes 589832 | tf_op jit(solution)/shard_map/ppermute | solution.py:218
  58.2 3.0 %collective-permute-done.16.refs_8_ = bf16[128,896]{1,0:T(8,128)(2,1)S(1)} collective-permute-done((bf16[128,896]{1,0:T(8,128)(2,1)S(1)}, bf16[128,896]{1,0:T(8,128)(2,1)S(1)}, u32[]{:S(2)}, u32[]{:S(2)}) %collective-permute-start.16) | collective-permute-done | bytes 229408 | tf_op jit(solution)/shard_map/ppermute | solution.py:218
  61.2 0.0 collective-permute-start.19
  61.2 0.5 collective-permute-start.8
  61.7 1.2 %collective-permute-done.7.refs_2_ = bf16[128,768]{1,0:T(8,128)(2,1)S(1)} collective-permute-done((bf16[128,768]{1,0:T(8,128)(2,1)S(1)}, bf16[128,768]{1,0:T(8,128)(2,1)S(1)}, u32[]{:S(2)}, u32[]{:S(2)}) %collective-permute-start.7) | collective-permute-done | bytes 196640 | tf_op jit(solution)/shard_map/ppermute | solution.py:218
  62.9 0.0 collective-permute-start.10
  62.9 0.5 collective-permute-start.17
  63.4 0.0 collective-permute-start.18
  63.4 0.0 collective-permute-done.8.refs_3_
  63.4 0.5 collective-permute-start.9
  63.9 1.0 %collective-permute-done.9.refs_4_ = bf16[64,768]{1,0:T(8,128)(2,1)S(1)} collective-permute-done((bf16[64,768]{1,0:T(8,128)(2,1)S(1)}, bf16[64,768]{1,0:T(8,128)(2,1)S(1)}, u32[]{:S(2)}, u32[]{:S(2)}) %collective-permute-start.9) | collective-permute-done | bytes 98336 | tf_op jit(solution)/shard_map/ppermute | solution.py:218
  64.9 0.0 collective-permute-done.18.refs_10_
  64.9 0.0 collective-permute-done.10.refs_5_
  64.9 0.0 collective-permute-done.19.refs_11_
  64.9 1.3 %shard_map.94 = (bf16[3,512,512]{2,1,0:T(8,128)(2,1)}, bf16[50,512]{1,0:T(8,128)(2,1)}) custom-call(bf16[64,768]{1,0:T(8,128)(2,1)S(1)} %add_convert_fusion.2.refs_0_, bf16[64,768]{1,0:T(8,128)(2,1)S(1)} %collective-permute-done.6.refs_1_, bf16[128,768]{1,0:T(8,128)(2,1)S(1)} %collective-permute-done.7.refs_2_, ...), custom_call_target="tpu_custom_call" | custom-call | bytes 3328000 | tf_op jit(solution)/shard_map/pallas_call | solution.py:24
  (8 shorter events, 0.2 us)
Async XLA Ops:
  6.7 11.3 %collective-permute-start.1 = (bf16[512,256]{1,0:T(8,128)(2,1)S(1)}, bf16[512,256]{1,0:T(8,128)(2,1)S(1)}, u32[]{:S(2)}, u32[]{:S(2)}) collective-permute-start(bf16[512,256]{1,0:T(8,128)(2,1)S(1)} %get-tuple-element.37), channel_id=1, source_target_pairs={{16,0},{17,1},{18,2},{19,3},{20,4},{21,5},{22,6},{23,7},{24,8},{25... | collective-permute-start | bytes 786440 | tf_op jit(solution)/shard_map/ppermute | solution.py:259
  8.6 14.3 %collective-permute-start = (bf16[512,256]{1,0:T(8,128)(2,1)S(1)}, bf16[512,256]{1,0:T(8,128)(2,1)S(1)}, u32[]{:S(2)}, u32[]{:S(2)}) collective-permute-start(bf16[512,256]{1,0:T(8,128)(2,1)S(1)} %get-tuple-element.33), channel_id=1, source_target_pairs={{16,0},{17,1},{18,2},{19,3},{20,4},{21,5},{22,6},{23,7},{24,8},{25... | collective-permute-start | bytes 786440 | tf_op jit(solution)/shard_map/ppermute | solution.py:259
  24.5 1.8 %collective-permute-start.11 = (bf16[256,896]{1,0:T(8,128)(2,1)S(1)}, bf16[256,896]{1,0:T(8,128)(2,1)S(1)}, u32[]{:S(2)}, u32[]{:S(2)}) collective-permute-start(bf16[256,896]{1,0:T(8,128)(2,1)S(1)} %get-tuple-element.48), channel_id=1, source_target_pairs={{0,1},{1,0},{2,3},{3,2},{4,5},{5,4},{6,7},{7,6},{8,9},{9,8},{10,11... | collective-permute-start | bytes 1376264 | tf_op jit(solution)/shard_map/ppermute | solution.py:218
  24.5 4.4 %collective-permute-start.2 = (bf16[256,768]{1,0:T(8,128)(2,1)S(1)}, bf16[256,768]{1,0:T(8,128)(2,1)S(1)}, u32[]{:S(2)}, u32[]{:S(2)}) collective-permute-start(bf16[256,768]{1,0:T(8,128)(2,1)S(1)} %get-tuple-element.42), channel_id=1, source_target_pairs={{0,1},{1,0},{2,3},{3,2},{4,5},{5,4},{6,7},{7,6},{8,9},{9,8},{10,11... | collective-permute-start | bytes 1179656 | tf_op jit(solution)/shard_map/ppermute | solution.py:218
  26.4 8.4 %collective-permute-start.12 = (bf16[128,896]{1,0:T(8,128)(2,1)S(1)}, bf16[128,896]{1,0:T(8,128)(2,1)S(1)}, u32[]{:S(2)}, u32[]{:S(2)}) collective-permute-start(bf16[128,896]{1,0:T(8,128)(2,1)S(1)} %get-tuple-element.50), channel_id=1, source_target_pairs={{0,4},{1,5},{2,6},{3,7},{4,0},{5,1},{6,2},{7,3},{8,12},{9,13},{10,... | collective-permute-start | bytes 688136 | tf_op jit(solution)/shard_map/ppermute | solution.py:218
  29.0 7.6 %collective-permute-start.3 = (bf16[128,768]{1,0:T(8,128)(2,1)S(1)}, bf16[128,768]{1,0:T(8,128)(2,1)S(1)}, u32[]{:S(2)}, u32[]{:S(2)}) collective-permute-start(bf16[128,768]{1,0:T(8,128)(2,1)S(1)} %get-tuple-element.44), channel_id=1, source_target_pairs={{0,2},{1,3},{2,0},{3,1},{4,6},{5,7},{6,4},{7,5},{8,10},{9,11},{10,... | collective-permute-start | bytes 589832 | tf_op jit(solution)/shard_map/ppermute | solution.py:218
  34.9 4.9 %collective-permute-start.13 = (bf16[64,896]{1,0:T(8,128)(2,1)S(1)}, bf16[64,896]{1,0:T(8,128)(2,1)S(1)}, u32[]{:S(2)}, u32[]{:S(2)}) collective-permute-start(bf16[64,896]{1,0:T(8,128)(2,1)S(1)} %get-tuple-element.52), channel_id=1, source_target_pairs={{0,2},{1,3},{2,0},{3,1},{4,6},{5,7},{6,4},{7,5},{8,10},{9,11},{10,... | collective-permute-start | bytes 344072 | tf_op jit(solution)/shard_map/ppermute | solution.py:218
  36.7 5.9 %collective-permute-start.4 = (bf16[64,768]{1,0:T(8,128)(2,1)S(1)}, bf16[64,768]{1,0:T(8,128)(2,1)S(1)}, u32[]{:S(2)}, u32[]{:S(2)}) collective-permute-start(bf16[64,768]{1,0:T(8,128)(2,1)S(1)} %get-tuple-element.46), channel_id=1, source_target_pairs={{0,4},{1,5},{2,6},{3,7},{4,0},{5,1},{6,2},{7,3},{8,12},{9,13},{10,... | collective-permute-start | bytes 294920 | tf_op jit(solution)/shard_map/ppermute | solution.py:218
  39.7 10.4 %collective-permute-start.14 = (bf16[64,896]{1,0:T(8,128)(2,1)S(1)}, bf16[64,896]{1,0:T(8,128)(2,1)S(1)}, u32[]{:S(2)}, u32[]{:S(2)}) collective-permute-start(bf16[64,896]{1,0:T(8,128)(2,1)S(1)} %add_convert_fusion.1), channel_id=1, source_target_pairs={{0,8},{1,9},{2,10},{3,11},{4,12},{5,13},{6,14},{7,15},{8,0},{9,1},... | collective-permute-start | bytes 344072 | tf_op jit(solution)/shard_map/ppermute | solution.py:218
  42.6 8.7 %collective-permute-start.5 = (bf16[64,768]{1,0:T(8,128)(2,1)S(1)}, bf16[64,768]{1,0:T(8,128)(2,1)S(1)}, u32[]{:S(2)}, u32[]{:S(2)}) collective-permute-start(bf16[64,768]{1,0:T(8,128)(2,1)S(1)} %add_convert_fusion.3), channel_id=1, source_target_pairs={{0,8},{1,9},{2,10},{3,11},{4,12},{5,13},{6,14},{7,15},{8,0},{9,1},... | collective-permute-start | bytes 294920 | tf_op jit(solution)/shard_map/ppermute | solution.py:218
  50.2 4.9 %collective-permute-start.15 = (bf16[64,896]{1,0:T(8,128)(2,1)S(1)}, bf16[64,896]{1,0:T(8,128)(2,1)S(1)}, u32[]{:S(2)}, u32[]{:S(2)}) collective-permute-start(bf16[64,896]{1,0:T(8,128)(2,1)S(1)} %add_convert_fusion.refs_6_), channel_id=1, source_target_pairs={{0,2},{1,3},{2,0},{3,1},{4,6},{5,7},{6,4},{7,5},{8,10},{9,11},{10,... | collective-permute-start | bytes 344072 | tf_op jit(solution)/shard_map/ppermute | solution.py:218
  51.4 5.8 %collective-permute-start.6 = (bf16[64,768]{1,0:T(8,128)(2,1)S(1)}, bf16[64,768]{1,0:T(8,128)(2,1)S(1)}, u32[]{:S(2)}, u32[]{:S(2)}) collective-permute-start(bf16[64,768]{1,0:T(8,128)(2,1)S(1)} %add_convert_fusion.2.refs_0_), channel_id=1, source_target_pairs={{0,4},{1,5},{2,6},{3,7},{4,0},{5,1},{6,2},{7,3},{8,12},{9,13},{10,... | collective-permute-start | bytes 294920 | tf_op jit(solution)/shard_map/ppermute | solution.py:218
  55.1 6.1 %collective-permute-start.16 = (bf16[128,896]{1,0:T(8,128)(2,1)S(1)}, bf16[128,896]{1,0:T(8,128)(2,1)S(1)}, u32[]{:S(2)}, u32[]{:S(2)}) collective-permute-start(bf16[128,896]{1,0:T(8,128)(2,1)S(1)} %pad_maximum_fusion), channel_id=1, source_target_pairs={{0,4},{1,5},{2,6},{3,7},{4,0},{5,1},{6,2},{7,3},{8,12},{9,13},{10,... | collective-permute-start | bytes 688136 | tf_op jit(solution)/shard_map/ppermute | solution.py:218
  57.2 5.7 %collective-permute-start.7 = (bf16[128,768]{1,0:T(8,128)(2,1)S(1)}, bf16[128,768]{1,0:T(8,128)(2,1)S(1)}, u32[]{:S(2)}, u32[]{:S(2)}) collective-permute-start(bf16[128,768]{1,0:T(8,128)(2,1)S(1)} %pad_maximum_fusion.1), channel_id=1, source_target_pairs={{0,2},{1,3},{2,0},{3,1},{4,6},{5,7},{6,4},{7,5},{8,10},{9,11},{10,... | collective-permute-start | bytes 589832 | tf_op jit(solution)/shard_map/ppermute | solution.py:218
  61.2 3.7 %collective-permute-start.19 = (bf16[128,896]{1,0:T(8,128)(2,1)S(1)}, bf16[128,896]{1,0:T(8,128)(2,1)S(1)}, u32[]{:S(2)}, u32[]{:S(2)}) collective-permute-start(bf16[128,896]{1,0:T(8,128)(2,1)S(1)} %collective-permute-done.16.refs_8_), channel_id=1, source_target_pairs={{0,1},{1,0},{2,3},{3,2},{4,5},{5,4},{6,7},{7,6},{8,9},{9,8},{10,11... | collective-permute-start | bytes 688136 | tf_op jit(solution)/shard_map/ppermute | solution.py:218
  61.2 2.2 %collective-permute-start.8 = (bf16[64,768]{1,0:T(8,128)(2,1)S(1)}, bf16[64,768]{1,0:T(8,128)(2,1)S(1)}, u32[]{:S(2)}, u32[]{:S(2)}) collective-permute-start(bf16[64,768]{1,0:T(8,128)(2,1)S(1)} %add_convert_fusion.2.refs_0_), channel_id=1, source_target_pairs={{0,1},{1,0},{2,3},{3,2},{4,5},{5,4},{6,7},{7,6},{8,9},{9,8},{10,11... | collective-permute-start | bytes 294920 | tf_op jit(solution)/shard_map/ppermute | solution.py:218
  62.9 2.0 %collective-permute-start.10 = (bf16[128,768]{1,0:T(8,128)(2,1)S(1)}, bf16[128,768]{1,0:T(8,128)(2,1)S(1)}, u32[]{:S(2)}, u32[]{:S(2)}) collective-permute-start(bf16[128,768]{1,0:T(8,128)(2,1)S(1)} %collective-permute-done.7.refs_2_), channel_id=1, source_target_pairs={{0,1},{1,0},{2,3},{3,2},{4,5},{5,4},{6,7},{7,6},{8,9},{9,8},{10,11... | collective-permute-start | bytes 589832 | tf_op jit(solution)/shard_map/ppermute | solution.py:218
  62.9 2.0 %collective-permute-start.17 = (bf16[64,896]{1,0:T(8,128)(2,1)S(1)}, bf16[64,896]{1,0:T(8,128)(2,1)S(1)}, u32[]{:S(2)}, u32[]{:S(2)}) collective-permute-start(bf16[64,896]{1,0:T(8,128)(2,1)S(1)} %add_convert_fusion.refs_6_), channel_id=1, source_target_pairs={{0,1},{1,0},{2,3},{3,2},{4,5},{5,4},{6,7},{7,6},{8,9},{9,8},{10,11... | collective-permute-start | bytes 344072 | tf_op jit(solution)/shard_map/ppermute | solution.py:218
  63.4 1.5 %collective-permute-start.18 = (bf16[64,896]{1,0:T(8,128)(2,1)S(1)}, bf16[64,896]{1,0:T(8,128)(2,1)S(1)}, u32[]{:S(2)}, u32[]{:S(2)}) collective-permute-start(bf16[64,896]{1,0:T(8,128)(2,1)S(1)} %collective-permute-done.15.refs_7_), channel_id=1, source_target_pairs={{0,1},{1,0},{2,3},{3,2},{4,5},{5,4},{6,7},{7,6},{8,9},{9,8},{10,11... | collective-permute-start | bytes 344072 | tf_op jit(solution)/shard_map/ppermute | solution.py:218
  63.4 1.5 %collective-permute-start.9 = (bf16[64,768]{1,0:T(8,128)(2,1)S(1)}, bf16[64,768]{1,0:T(8,128)(2,1)S(1)}, u32[]{:S(2)}, u32[]{:S(2)}) collective-permute-start(bf16[64,768]{1,0:T(8,128)(2,1)S(1)} %collective-permute-done.6.refs_1_), channel_id=1, source_target_pairs={{0,1},{1,0},{2,3},{3,2},{4,5},{5,4},{6,7},{7,6},{8,9},{9,8},{10,11... | collective-permute-start | bytes 294920 | tf_op jit(solution)/shard_map/ppermute | solution.py:218

commit v4 on v3

v4 whole, which is shorter than its diff:
```python
import functools
import math

import jax
import jax.numpy as jnp
from jax import lax
from jax.experimental import pallas as pl
from jax.experimental.pallas import tpu as pltpu
from jax.sharding import PartitionSpec as P

SENT = (256, 256)
PARTS = 2
F32 = jnp.float32
BF16 = jnp.bfloat16
VMEM = pl.BlockSpec(memory_space=pltpu.VMEM)
SMEM = pl.BlockSpec(memory_space=pltpu.SMEM)
HBM = pl.BlockSpec(memory_space=pltpu.HBM)
NT = (((1,), (1,)), ((), ()))


def call(kernel, out_shape, args, smem=0, far=0, scratch=(), flops=0):
    specs = [SMEM] * smem + [HBM] * far + [VMEM] * (len(args) - smem - far)
    moved = sum(a.size * a.dtype.itemsize for a in args)
    moved += sum(math.prod(o.shape) * o.dtype.itemsize for o in out_shape)
    return pl.pallas_call(
        kernel,
        out_shape=out_shape,
        in_specs=specs,
        out_specs=[VMEM] * len(out_shape),
        scratch_shapes=list(scratch),
        compiler_params=pltpu.CompilerParams(vmem_limit_bytes=48 * 2**20),
        cost_estimate=pl.CostEstimate(flops=flops, bytes_accessed=moved, transcendentals=0),
    )(*args)


def is_top():
    return lax.axis_index("section") == lax.axis_size("section") - 1


def dp_bit(n):
    return lax.rem(lax.div(lax.axis_index("dp"), 1 << n), 2)


def like(shape, dtype):
    return jax.ShapeDtypeStruct(shape, dtype)


def put_taps(values, taps, bins, dilation, orientation):
    rows, cols = values.shape
    place = lax.broadcasted_iota(jnp.int32, (bins, cols), 0)
    taps[:, cols : 2 * cols] = values
    for b in range(rows // bins):
        at = slice(b * bins, (b + 1) * bins)
        group = values[at].astype(F32)
        later = pltpu.roll(group, bins - dilation, 0)
        later = jnp.where(place < bins - dilation, later, 0.0).astype(BF16)
        earlier = pltpu.roll(group, dilation, 0)
        earlier = jnp.where(place >= dilation, earlier, 0.0).astype(BF16)
        first, third = (earlier, later) if orientation == 1 else (later, earlier)
        taps[at, 0:cols] = first
        taps[at, 2 * cols : 3 * cols] = third


def back_product(taps, weight, cols):
    total = None
    for k in range(3):
        part = lax.dot_general(
            taps[:, k * cols : (k + 1) * cols], weight[k], NT, preferred_element_type=F32
        )
        total = part if total is None else total + part
    return total


def forward(mixed, at, taps, bins, dilation, weight, slope):
    put_taps(mixed[at, :], taps, bins, dilation, 1)
    flat = weight[...].reshape(-1, weight.shape[2])
    y = jnp.dot(taps[...], flat, preferred_element_type=F32)
    gate = jax.nn.sigmoid(y)
    slope[...] = gate * (1.0 + y * (1.0 - gate))


def backward(g, taps, bins, dilation, slope):
    delta = (g * slope[...]).astype(BF16)
    put_taps(delta, taps, bins, dilation, -1)


def below_of(g, taps, weight, col, out):
    cols = slice(col, col + out.shape[1])
    dh = back_product(taps, weight[:, cols, :], weight.shape[2])
    out[...] = (g[:, cols].astype(F32) + dh).astype(BF16)


def first_kernel(dil, ts, x, table, weight, top, mixed, weight_v, top_v, hot, slope, taps, g_out, *s):
    ts_s, x_v, table_v, tab, forward_taps, sems = s
    pairs = ((ts, ts_s), (x, x_v), (table, table_v), (weight, weight_v), (top, top_v))
    copies = [pltpu.make_async_copy(a, b, sems.at[n]) for n, (a, b) in enumerate(pairs)]
    for copy in copies:
        copy.start()
    groups, bins, chans = x.shape
    for copy in copies[:3]:
        copy.wait()
    tab[...] = table_v[...].astype(F32)
    for b in range(groups):
        row = x_v[b].astype(F32) + tab[pl.ds(ts_s[b], 1), :]
        mixed[b * bins : (b + 1) * bins, :] = row.astype(BF16)
    steps = lax.broadcasted_iota(jnp.int32, hot.shape, 0)
    lanes = lax.broadcasted_iota(jnp.int32, hot.shape, 1)
    marks = jnp.zeros(hot.shape, F32)
    for b in range(groups):
        marks = jnp.where((lanes == b) & (steps == ts_s[b]), 1.0, marks)
    hot[...] = marks
    copies[3].wait()
    rows = slope.shape[0]
    forward(mixed, slice(0, rows), forward_taps, bins, dil[0], weight_v, slope)
    copies[4].wait()
    g = top_v[...].reshape(groups * bins, chans)[0:rows]
    backward(g.astype(F32), taps, bins, dil[0], slope)
    below_of(g, taps, weight_v, 0, g_out)


def other_kernel(start, bins, dil, mixed, weight, top, slope, taps, g_out, forward_taps):
    at = slice(start, start + slope.shape[0])
    forward(mixed, at, forward_taps, bins, dil[0], weight, slope)
    g = top[...].reshape(mixed.shape)[at]
    backward(g.astype(F32), taps, bins, dil[0], slope)
    below_of(g, taps, weight, 0, g_out)


def rest_kernel(col, weight, top, *rest):
    taps, g_out = rest[:-1], rest[-1]
    part = taps[0].shape[0]
    g = top[...].reshape(-1, top.shape[2])
    for n, ref in enumerate(taps):
        at = slice(n * part, (n + 1) * part)
        below_of(g[at], ref, weight, col, g_out.at[at])


def turn_kernel(mixed, h_t):
    h_t[...] = mixed[...].T


def layer_kernel(start, bins, dil, slope, weight, top, *rest):
    early, late, out, out_late, taps = rest
    rows = slope.shape[0]
    got = jnp.concatenate([early[...], late[start : start + rows]], axis=1)
    fresh = top[...].reshape(-1, top.shape[2])[start : start + rows]
    g = jnp.where(is_top(), fresh.astype(F32), got.astype(F32))
    backward(g, taps, bins, dil[0], slope)
    below_of(g, taps, weight, 0, out)
    below_of(g, taps, weight, out.shape[1], out_late)


def upstream(col, top, recv):
    got = [ref[...].astype(F32) for ref in recv]
    got = got[0] if len(got) == 1 else jnp.concatenate(got, axis=0)
    rows, width = got.shape
    fresh = top[...].reshape(rows, top.shape[-1])[:, col : col + width]
    return jnp.where(is_top(), fresh.astype(F32), got)


def delta_of(g, slope, col):
    width = g.shape[1]
    factor = jnp.concatenate([ref[:, col : col + width] for ref in slope], axis=0)
    return (g * factor).astype(BF16)


def round_bit(orders, n, other=0):
    mine, theirs = dp_bit(orders[other][n]), dp_bit(orders[1 - other][n])
    return jnp.where(dp_bit(0) == 0, mine, theirs)


def weight_blocks(h_t, taps, scale, keep, send, cols):
    half = h_t.shape[0] // 2
    bit = dp_bit(0)
    for ref, part in ((keep, bit), (send, 1 - bit)):
        left = h_t[pl.ds(pl.multiple_of(part * half, half), half), :]
        prod = jnp.dot(left, taps[...], preferred_element_type=F32)
        ref[:, 0:cols] = (prod * scale).astype(BF16)


def weight_kernel(col, scale, dil, top, h_t, *rest):
    slope, recv, out = rest[:PARTS], rest[PARTS:-4], rest[-4:]
    g_used, taps, keep, send = out
    width = g_used.shape[1]
    g = upstream(col, top, recv)
    g_used[...] = g.astype(BF16)
    delta = delta_of(g, slope, col)
    put_taps(delta, taps, top.shape[1], dil[0], -1)
    weight_blocks(h_t, taps, scale, keep, send, 3 * width)


def back_kernel(col, taps, weight, acc):
    width = taps.shape[1] // 3
    acc[...] = back_product(taps, weight[:, :, col : col + width], width)


def last_kernel(col, scale, prior, dil, top, h_t, weight, hot, *rest):
    slope, recv = rest[:PARTS], rest[PARTS : -4 - 2 * prior]
    g_prior, acc = rest[-4 - 2 * prior : -4 - prior], rest[-4 - prior : -4]
    keep, send, grad, taps = rest[-4:]
    groups, bins, chans = grad.shape
    width = taps.shape[1] // 3
    g = upstream(col, top, recv)
    delta = delta_of(g, slope, col)
    put_taps(delta, taps, bins, dil[0], -1)
    dh = back_product(taps, weight[:, :, col : col + width], width)
    for ref in acc:
        dh = dh + ref[...]
    whole = jnp.concatenate([ref[...].astype(F32) for ref in g_prior] + [g], axis=1)
    grad[...] = (whole + dh).astype(BF16).reshape(groups, bins, chans)
    table = jnp.zeros((hot.shape[0], chans), F32)
    for b in range(groups):
        total = jnp.sum(dh[b * bins : (b + 1) * bins], axis=0, keepdims=True)
        table = table + hot[:, b : b + 1] * (total * scale)
    table_t = table.T.astype(BF16)
    weight_blocks(h_t, taps, scale, keep, send, 3 * width)
    half = chans // 2
    bit = dp_bit(0)
    for ref, part in ((send, 1 - bit), (keep, bit)):
        ref[:, 3 * width :] = jnp.where(part == 0, table_t[0:half], table_t[half:])


def fold_kernel(orders, n, keep, recv, keep_out, send_out):
    size = keep_out.shape[0]
    bit = round_bit(orders, n)
    for ref, part in ((keep_out, bit), (send_out, 1 - bit)):
        at = pl.ds(pl.multiple_of(part * size, size), size)
        ref[...] = (keep[at, :].astype(F32) + recv[at, :].astype(F32)).astype(BF16)


def assemble_kernel(orders, widths, lists, *refs):
    weight_out, table_out, table_t = refs[-3:]
    pieces = list(refs[:-3])
    col = 0
    for width in widths:
        for offsets in lists:
            ref = pieces.pop(0)
            size = ref.shape[0] // len(offsets)
            for slot, (core, flips) in enumerate(offsets):
                block = dp_bit(0) if core == 0 else 1 - dp_bit(0)
                for n in range(len(orders[0])):
                    bit = round_bit(orders, n, core)
                    block = block * 2 + (1 - bit if (flips >> n) & 1 else bit)
                row = pl.ds(pl.multiple_of(block * size, size), size)
                here = slice(slot * size, (slot + 1) * size)
                for k in range(3):
                    weight_out[k, row, col : col + width] = ref[here, k * width : (k + 1) * width]
                if ref.shape[1] > 3 * width:
                    table_t[row, :] = ref[here, 3 * width :].astype(F32)
        col += width
    table_out[...] = table_t[...].T[: table_out.shape[0]].astype(BF16)


def swap(value, bit, other=None):
    count = lax.axis_size("dp")
    bits = (bit, bit if other is None else other)
    return lax.ppermute(value, "dp", [(i, i ^ (1 << bits[i % 2])) for i in range(count)])


def body(section_input, top_grad, conv_weight, step_table, timesteps, dilations):
    section_count = lax.axis_size("section")
    dp_count = lax.axis_size("dp")
    dp_bits = dp_count.bit_length() - 1
    x = section_input[0]
    weight = conv_weight[0]
    table = step_table[0]
    groups, bins, chans = x.shape
    rows = groups * bins
    sent = SENT
    scale = 1.0 / math.sqrt(groups * dp_count * bins)
    unit = 2 * rows * chans * chans * 3
    starts = [sum(sent[:n]) for n in range(len(sent))]

    part = rows // PARTS
    room = pltpu.VMEM((part, 3 * chans), BF16)
    of_part = [
        like((part, chans), F32),
        like((part, 3 * chans), BF16),
        like((part, sent[0]), BF16),
    ]
    far = (timesteps, x, table, weight, top_grad)
    mixed, weight, top, hot, *first = call(
        first_kernel,
        [
            like((rows, chans), BF16),
            like(weight.shape, BF16),
            like(x.shape, BF16),
            like((128, 128), F32),
        ]
        + of_part,
        (dilations,) + tuple(pltpu.with_memory_space_constraint(v, pltpu.HBM) for v in far),
        smem=1,
        far=5,
        scratch=[
            pltpu.SMEM(timesteps.shape, jnp.int32),
            pltpu.VMEM(x.shape, BF16),
            pltpu.VMEM(table.shape, BF16),
            pltpu.VMEM(table.shape, F32),
            room,
            pltpu.SemaphoreType.DMA((5,)),
        ],
        flops=2 * unit // PARTS,
    )

    def below(value):
        return lax.ppermute(value, "section", [(i, i - 1) for i in range(1, section_count)])

    made = [first]
    for n in range(1, PARTS):
        made.append(
            call(
                functools.partial(other_kernel, n * part, bins),
                of_part,
                (dilations, mixed, weight, top),
                smem=1,
                scratch=[room],
                flops=2 * unit // PARTS,
            )
        )
    slope = [v[0] for v in made]
    late = call(
        functools.partial(rest_kernel, sent[0]),
        [like((rows, sent[1]), BF16)],
        (weight, top) + tuple(v[1] for v in made),
        flops=unit // 2,
    )[0]
    got = [[below(v[2]) for v in made], [below(late)]]
    h_t = call(turn_kernel, [like((chans, rows), BF16)], (mixed,), flops=unit // 9)[0]
    for _ in range(section_count - 2):
        pieces = [
            call(
                functools.partial(layer_kernel, n * part, bins),
                [like((part, cols), BF16) for cols in sent],
                (dilations, slope[n], weight, top, got[0][n], got[1][0]),
                smem=1,
                scratch=[room],
                flops=unit // PARTS,
            )
            for n in range(PARTS)
        ]
        late = jnp.concatenate([v[1] for v in pieces], axis=0)
        got = [[below(v[0]) for v in pieces], [below(late)]]

    inner = list(range(1, dp_bits - 1))
    orders = (inner, inner[::-1])
    chains = []
    used = []
    accs = []
    for n, width in enumerate(sent):
        col = starts[n]
        recv = tuple(slope) + tuple(got[n])
        if n < len(sent) - 1:
            g_now, taps_now, *blocks = call(
                functools.partial(weight_kernel, col, scale),
                [like((rows, width), BF16), like((rows, 3 * width), BF16)]
                + [like((chans // 2, 3 * width), BF16)] * 2,
                (dilations, top, h_t) + recv,
                smem=1,
                    flops=unit * width // chans,
            )
            acc = call(
                functools.partial(back_kernel, col),
                [like((rows, chans), F32)],
                (taps_now, weight),
                flops=10**11,
            )[0]
            used.append(g_now)
            accs.append(acc)
        else:
            *blocks, grad = call(
                functools.partial(last_kernel, col, scale, len(used)),
                [like((chans // 2, 3 * width + 128), BF16)] * 2 + [like(x.shape, BF16)],
                (dilations, top, h_t, weight, hot) + recv + tuple(used) + tuple(accs),
                smem=1,
                    scratch=[pltpu.VMEM((rows, 3 * width), BF16)],
                flops=10**11,
            )
        chains.append((width, blocks))

    widths = []
    pieces = []
    before = []
    for width, (keep, send) in chains:
        rounds = []

        def ordered(arrived):
            rounds.append(arrived)
            if len(rounds) < len(before):
                arrived = lax.optimization_barrier((arrived, before[len(rounds)]))[0]
            return arrived

        if before:
            send = lax.optimization_barrier((send, before[1]))[0]
        recv = ordered(swap(send, 0))
        for n in range(len(inner)):
            half = [like((keep.shape[0] // 2, keep.shape[1]), BF16)] * 2
            keep, send = call(functools.partial(fold_kernel, orders, n), half, (keep, recv))
            recv = ordered(swap(send, orders[0][n], orders[1][n]))
        keep = (keep.astype(F32) + recv.astype(F32)).astype(BF16)
        own = (keep.astype(F32) + ordered(swap(keep, dp_bits - 1)).astype(F32)).astype(BF16)
        held = [(own, [(0, 0)])]
        for n in reversed(range(len(inner))):
            message = jnp.concatenate([v for v, _ in held], axis=0) if len(held) > 1 else own
            flips = [(0, f ^ (1 << n)) for _, offs in held for _, f in offs]
            held.append((ordered(swap(message, orders[0][n], orders[1][n])), flips))
        early = jnp.concatenate([v for v, _ in held[:-1]], axis=0)
        held.append((swap(early, 0), [(1, f) for _, offs in held[:-1] for _, f in offs]))
        held.append((swap(held[-2][0], 0), [(1, f) for _, f in held[-2][1]]))
        pieces += [v for v, _ in held]
        widths.append(width)
        before = rounds

    weight_out, table_out = call(
        functools.partial(assemble_kernel, orders, widths, [o for _, o in held]),
        [like(weight.shape, BF16), like(table.shape, BF16)],
        tuple(pieces),
        scratch=[pltpu.VMEM((chans, 128), F32)],
    )
    return (grad[None], weight_out[None], table_out[None])


def solution(mesh):
    placed = (
        P("section", "dp", None, None),
        P("dp", None, None),
        P("section", None, None, None),
        P("section", None, None),
        P("dp"),
        P("section"),
    )
    return jax.shard_map(
        body,
        mesh=mesh,
        in_specs=placed,
        out_specs=(
            P("section", "dp", None, None),
            P("section", None, None, None),
            P("section", None, None),
        ),
        check_vma=False,
    )
```

time: 66.4 us -> 62.4 us (0.940)
  waiting for transfers between devices: 34.3 us -> 26.7 us
  starting transfers between devices: 19.5 us -> 22.8 us
    ppermute x2 -> x3, waiting for transfers between devices: 11.3 us -> 5.16 us  [below(): lax.ppermute(value, 'section', [(i, i - 1) for i in range(1, section_coun...]
    ppermute x18 -> x16, starting transfers between devices: 16.9 us -> 19 us  [swap(): lax.ppermute(value, 'dp', [(i, i ^ 1 << bits[i % 2]) for i in range(count)])]
    ppermute x18 -> x16, waiting for transfers between devices: 23 us -> 21.5 us  [swap(): lax.ppermute(value, 'dp', [(i, i ^ 1 << bits[i % 2]) for i in range(count)])]
    ppermute x2 -> x3, starting transfers between devices: 2.58 us -> 3.88 us  [below(): lax.ppermute(value, 'section', [(i, i - 1) for i in range(1, section_coun...]
    pallas_call x10 -> x12, Pallas kernels: 10.9 us -> 11.1 us  [call(): pl.pallas_call(kernel, out_shape=out_shape, in_specs=specs, out_specs=[VM...]
  transfers between devices with their start and end apart: 20 -> 19, of which waited for: 11 -> 15; matrix products, arithmetic and copies ran while one was open for 0% -> 0% of each run, Pallas kernels for 4% -> 10%
where the time goes in v4:
time: 62.4 us; the launch traced here: 62.2 us
  waiting for transfers between devices  26.7 us (43%)
  starting transfers between devices  22.8 us (37%)
  Pallas kernels  11.1 us (18%)
  between operations  1.4 us (2%)
    ppermute x16, waiting for transfers between devices, swap(): lax.ppermute(value, 'dp', [(i, i ^ 1 << bits[i % 2]) for i in range(count)])  21.5 us
    ppermute x16, starting transfers between devices, swap(): lax.ppermute(value, 'dp', [(i, i ^ 1 << bits[i % 2]) for i in range(count)])  19 us
    pallas_call x12, Pallas kernels, call(): pl.pallas_call(kernel, out_shape=out_shape, in_specs=specs, out_specs=[VM...  11.1 us
    ppermute x3, waiting for transfers between devices, below(): lax.ppermute(value, 'section', [(i, i - 1) for i in range(1, section_coun...  5.16 us
    ppermute x3, starting transfers between devices, below(): lax.ppermute(value, 'section', [(i, i - 1) for i in range(1, section_coun...  3.88 us
  transfers between devices with their start and end apart: 19, of which 15 were waited for; matrix products, arithmetic and copies ran while one was open for 0% of the time, Pallas kernels for 10%

profile of v4, /device:TPU:0, one launch (start us, length us, event | category | flops | bytes accessed | tf_op | source)
XLA Modules:
  0.0 62.2 jit_solution(2776687319470574666)
XLA Ops:
  1.3 3.6 %shard_map.85 = (bf16[512,512]{1,0:T(8,128)(2,1)S(1)}, bf16[3,512,512]{2,1,0:T(8,128)(2,1)S(1)}, bf16[4,128,512]{2,1,0:T(8,128)(2,1)S(1)}, f32[128,128]{1,0:T(8,...) custom-call(s32[1]{0:T(128)S(6)} %copy.9.dil, s32[4]{0:T(128)} %ts.1, ...), custom_call_target="tpu_custom_call" | custom-call | flops 805306368 | bytes 6801428 | tf_op jit(solution)/shard_map/pallas_call | solution.py:25
  4.9 1.3 %collective-permute-start.1 = (bf16[256,256]{1,0:T(8,128)(2,1)S(1)}, bf16[256,256]{1,0:T(8,128)(2,1)S(1)}, u32[]{:S(2)}, u32[]{:S(2)}) collective-permute-start(bf16[256,256]{1,0:T(8,128)(2,1)S(1)} %get-tuple-element.44), channel_id=1, source_target_pairs={{16,0},{17,1},{18,2},{19,3},{20,4},{21,5},{22,6},{23,7},{24,8},{25... | collective-permute-start | bytes 393224 | tf_op jit(solution)/shard_map/ppermute | solution.py:306
  6.2 1.8 %shard_map.87 = (f32[256,512]{1,0:T(8,128)S(1)}, bf16[256,1536]{1,0:T(8,128)(2,1)S(1)}, bf16[256,256]{1,0:T(8,128)(2,1)S(1)}) custom-call(s32[1]{0:T(128)S(6)} %copy.9.dil, bf16[512,512]{1,0:T(8,128)(2,1)S(1)} %get-tuple-element.37.mixed, bf16[3,512,512]{2,1,0:T(8,128)(2,1)S(1)} %get-tuple-element.38.weight, bf16[4,128,512]{2,1,0:T(8,128)(2,1)S(1)} %get-tuple-element.36.top), custom_call_target="tpu_custom_call" | custom-call | flops 805306368 | bytes 4063236 | tf_op jit(solution)/shard_map/pallas_call | solution.py:25
  8.1 1.3 %collective-permute-start.2 = (bf16[256,256]{1,0:T(8,128)(2,1)S(1)}, bf16[256,256]{1,0:T(8,128)(2,1)S(1)}, u32[]{:S(2)}, u32[]{:S(2)}) collective-permute-start(bf16[256,256]{1,0:T(8,128)(2,1)S(1)} %get-tuple-element.45), channel_id=1, source_target_pairs={{16,0},{17,1},{18,2},{19,3},{20,4},{21,5},{22,6},{23,7},{24,8},{25... | collective-permute-start | bytes 393224 | tf_op jit(solution)/shard_map/ppermute | solution.py:306
  9.4 0.6 shard_map.88
  10.0 1.3 %collective-permute-start = (bf16[512,256]{1,0:T(8,128)(2,1)S(1)}, bf16[512,256]{1,0:T(8,128)(2,1)S(1)}, u32[]{:S(2)}, u32[]{:S(2)}) collective-permute-start(bf16[512,256]{1,0:T(8,128)(2,1)S(1)} %shard_map.88), channel_id=1, source_target_pairs={{16,0},{17,1},{18,2},{19,3},{20,4},{21,5},{22,6},{23,7},{24,8},{25... | collective-permute-start | bytes 786440 | tf_op jit(solution)/shard_map/ppermute | solution.py:306
  11.3 0.2 shard_map.86.h_t
  11.5 1.2 %collective-permute-done.1.rest_2_ = bf16[256,256]{1,0:T(8,128)(2,1)S(1)} collective-permute-done((bf16[256,256]{1,0:T(8,128)(2,1)S(1)}, bf16[256,256]{1,0:T(8,128)(2,1)S(1)}, u32[]{:S(2)}, u32[]{:S(2)}) %collective-permute-start.1) | collective-permute-done | bytes 131104 | tf_op jit(solution)/shard_map/ppermute | solution.py:306
  12.7 4.0 %collective-permute-done.2.rest_3_ = bf16[256,256]{1,0:T(8,128)(2,1)S(1)} collective-permute-done((bf16[256,256]{1,0:T(8,128)(2,1)S(1)}, bf16[256,256]{1,0:T(8,128)(2,1)S(1)}, u32[]{:S(2)}, u32[]{:S(2)}) %collective-permute-start.2) | collective-permute-done | bytes 131104 | tf_op jit(solution)/shard_map/ppermute | solution.py:306
  16.6 1.0 %shard_map.89 = (bf16[512,256]{1,0:T(8,128)(2,1)S(1)}, bf16[512,768]{1,0:T(8,128)(2,1)S(1)}, bf16[256,768]{1,0:T(8,128)(2,1)S(1)}, bf16[256,768]{1,0:T(8,128)(2,1)S(1)}) custom-call(s32[1]{0:T(128)S(6)} %copy.9.dil, bf16[4,128,512]{2,1,0:T(8,128)(2,1)S(1)} %get-tuple-element.36.top, bf16[512,512]{1,0:T(8,128)(2,1)S(1)} %shard_map.86.h_t, ...), custom_call_target="tpu_custom_call" | custom-call | flops 402653184 | bytes 4194308 | tf_op jit(solution)/shard_map/pallas_call | solution.py:25
  17.6 0.1 collective-permute-start.3
  17.7 0.6 shard_map.90.rest_4_
  18.3 1.1 %collective-permute-done.3.recv = bf16[256,768]{1,0:T(8,128)(2,1)S(1)} collective-permute-done((bf16[256,768]{1,0:T(8,128)(2,1)S(1)}, bf16[256,768]{1,0:T(8,128)(2,1)S(1)}, u32[]{:S(2)}, u32[]{:S(2)}) %collective-permute-start.3) | collective-permute-done | bytes 393248 | tf_op jit(solution)/shard_map/ppermute | solution.py:257
  19.4 0.1 shard_map.92
  19.5 2.5 %collective-permute-start.4 = (bf16[128,768]{1,0:T(8,128)(2,1)S(1)}, bf16[128,768]{1,0:T(8,128)(2,1)S(1)}, u32[]{:S(2)}, u32[]{:S(2)}) collective-permute-start(bf16[128,768]{1,0:T(8,128)(2,1)S(1)} %get-tuple-element.52), channel_id=1, source_target_pairs={{0,2},{1,5},{2,0},{3,7},{4,6},{5,1},{6,4},{7,3},{8,10},{9,13},{10,... | collective-permute-start | bytes 589832 | tf_op jit(solution)/shard_map/ppermute | solution.py:257
  22.1 0.0 collective-permute-done.rest_2_
  22.1 1.6 %shard_map.91 = (bf16[256,896]{1,0:T(8,128)(2,1)S(1)}, bf16[256,896]{1,0:T(8,128)(2,1)S(1)}, bf16[4,128,512]{2,1,0:T(8,128)(2,1)}) custom-call(s32[1]{0:T(128)S(6)} %copy.9.dil, bf16[4,128,512]{2,1,0:T(8,128)(2,1)S(1)} %get-tuple-element.36.top, bf16[512,512]{1,0:T(8,128)(2,1)S(1)} %shard_map.86.h_t, bf16[3,512,512]{2,1,0:T(8,128)(2,1)S(1)} %get-tuple-element.38.weight, ...), custom_call_target="tpu_custom_call" | custom-call | flops 99999997952 | bytes 6750212 | tf_op jit(solution)/shard_map/pallas_call | solution.py:25
  23.7 2.0 %collective-permute-done.4.recv = bf16[128,768]{1,0:T(8,128)(2,1)S(1)} collective-permute-done((bf16[128,768]{1,0:T(8,128)(2,1)S(1)}, bf16[128,768]{1,0:T(8,128)(2,1)S(1)}, u32[]{:S(2)}, u32[]{:S(2)}) %collective-permute-start.4) | collective-permute-done | bytes 196640 | tf_op jit(solution)/shard_map/ppermute | solution.py:257
  25.7 0.0 collective-permute-start.11
  25.8 2.1 %collective-permute-start.5 = (bf16[64,768]{1,0:T(8,128)(2,1)S(1)}, bf16[64,768]{1,0:T(8,128)(2,1)S(1)}, u32[]{:S(2)}, u32[]{:S(2)}) collective-permute-start(bf16[64,768]{1,0:T(8,128)(2,1)S(1)} %get-tuple-element.54), channel_id=1, source_target_pairs={{0,4},{1,3},{2,6},{3,1},{4,0},{5,7},{6,2},{7,5},{8,12},{9,11},{10,... | collective-permute-start | bytes 294920 | tf_op jit(solution)/shard_map/ppermute | solution.py:257
  27.9 0.0 collective-permute-done.11.recv
  27.9 0.1 shard_map.94
  28.0 1.7 %collective-permute-start.12 = (bf16[128,896]{1,0:T(8,128)(2,1)S(1)}, bf16[128,896]{1,0:T(8,128)(2,1)S(1)}, u32[]{:S(2)}, u32[]{:S(2)}) collective-permute-start(bf16[128,896]{1,0:T(8,128)(2,1)S(1)} %get-tuple-element.60), channel_id=1, source_target_pairs={{0,2},{1,5},{2,0},{3,7},{4,6},{5,1},{6,4},{7,3},{8,10},{9,13},{10,... | collective-permute-start | bytes 688136 | tf_op jit(solution)/shard_map/ppermute | solution.py:257
  29.7 0.8 %collective-permute-done.5 = bf16[64,768]{1,0:T(8,128)(2,1)S(1)} collective-permute-done((bf16[64,768]{1,0:T(8,128)(2,1)S(1)}, bf16[64,768]{1,0:T(8,128)(2,1)S(1)}, u32[]{:S(2)}, u32[]{:S(2)}) %collective-permute-start.5) | collective-permute-done | bytes 98336 | tf_op jit(solution)/shard_map/ppermute | solution.py:257
  30.5 3.1 %collective-permute-start.6 = (bf16[64,768]{1,0:T(8,128)(2,1)S(1)}, bf16[64,768]{1,0:T(8,128)(2,1)S(1)}, u32[]{:S(2)}, u32[]{:S(2)}) collective-permute-start(bf16[64,768]{1,0:T(8,128)(2,1)S(1)} %add_convert_fusion.3), channel_id=1, source_target_pairs={{0,8},{1,9},{2,10},{3,11},{4,12},{5,13},{6,14},{7,15},{8,0},{9,1},... | collective-permute-start | bytes 294920 | tf_op jit(solution)/shard_map/ppermute | solution.py:257
  33.7 0.5 collective-permute-done.12.recv
  34.1 0.1 shard_map.95
  34.2 1.8 %collective-permute-start.13 = (bf16[64,896]{1,0:T(8,128)(2,1)S(1)}, bf16[64,896]{1,0:T(8,128)(2,1)S(1)}, u32[]{:S(2)}, u32[]{:S(2)}) collective-permute-start(bf16[64,896]{1,0:T(8,128)(2,1)S(1)} %get-tuple-element.63), channel_id=1, source_target_pairs={{0,4},{1,3},{2,6},{3,1},{4,0},{5,7},{6,2},{7,5},{8,12},{9,11},{10,... | collective-permute-start | bytes 344072 | tf_op jit(solution)/shard_map/ppermute | solution.py:257
  35.9 2.5 %collective-permute-done.6 = bf16[64,768]{1,0:T(8,128)(2,1)S(1)} collective-permute-done((bf16[64,768]{1,0:T(8,128)(2,1)S(1)}, bf16[64,768]{1,0:T(8,128)(2,1)S(1)}, u32[]{:S(2)}, u32[]{:S(2)}) %collective-permute-start.6) | collective-permute-done | bytes 98336 | tf_op jit(solution)/shard_map/ppermute | solution.py:257
  38.4 0.7 %collective-permute-start.7 = (bf16[64,768]{1,0:T(8,128)(2,1)S(1)}, bf16[64,768]{1,0:T(8,128)(2,1)S(1)}, u32[]{:S(2)}, u32[]{:S(2)}) collective-permute-start(bf16[64,768]{1,0:T(8,128)(2,1)S(1)} %add_convert_fusion.2.refs_0_), channel_id=1, source_target_pairs={{0,4},{1,3},{2,6},{3,1},{4,0},{5,7},{6,2},{7,5},{8,12},{9,11},{10,... | collective-permute-start | bytes 294920 | tf_op jit(solution)/shard_map/ppermute | solution.py:257
  39.2 0.4 collective-permute-done.13
  39.6 3.1 %collective-permute-start.14 = (bf16[64,896]{1,0:T(8,128)(2,1)S(1)}, bf16[64,896]{1,0:T(8,128)(2,1)S(1)}, u32[]{:S(2)}, u32[]{:S(2)}) collective-permute-start(bf16[64,896]{1,0:T(8,128)(2,1)S(1)} %add_convert_fusion.1), channel_id=1, source_target_pairs={{0,8},{1,9},{2,10},{3,11},{4,12},{5,13},{6,14},{7,15},{8,0},{9,1},... | collective-permute-start | bytes 344072 | tf_op jit(solution)/shard_map/ppermute | solution.py:257
  42.7 0.7 %collective-permute-done.7.refs_1_ = bf16[64,768]{1,0:T(8,128)(2,1)S(1)} collective-permute-done((bf16[64,768]{1,0:T(8,128)(2,1)S(1)}, bf16[64,768]{1,0:T(8,128)(2,1)S(1)}, u32[]{:S(2)}, u32[]{:S(2)}) %collective-permute-start.7) | collective-permute-done | bytes 98336 | tf_op jit(solution)/shard_map/ppermute | solution.py:257
  43.4 1.7 %collective-permute-start.8 = (bf16[128,768]{1,0:T(8,128)(2,1)S(1)}, bf16[128,768]{1,0:T(8,128)(2,1)S(1)}, u32[]{:S(2)}, u32[]{:S(2)}) collective-permute-start(bf16[128,768]{1,0:T(8,128)(2,1)S(1)} %pad_maximum_fusion.1), channel_id=1, source_target_pairs={{0,2},{1,5},{2,0},{3,7},{4,6},{5,1},{6,4},{7,3},{8,10},{9,13},{10,... | collective-permute-start | bytes 589832 | tf_op jit(solution)/shard_map/ppermute | solution.py:257
  45.1 2.7 %collective-permute-done.14 = bf16[64,896]{1,0:T(8,128)(2,1)S(1)} collective-permute-done((bf16[64,896]{1,0:T(8,128)(2,1)S(1)}, bf16[64,896]{1,0:T(8,128)(2,1)S(1)}, u32[]{:S(2)}, u32[]{:S(2)}) %collective-permute-start.14) | collective-permute-done | bytes 114720 | tf_op jit(solution)/shard_map/ppermute | solution.py:257
  47.8 0.7 %collective-permute-start.15 = (bf16[64,896]{1,0:T(8,128)(2,1)S(1)}, bf16[64,896]{1,0:T(8,128)(2,1)S(1)}, u32[]{:S(2)}, u32[]{:S(2)}) collective-permute-start(bf16[64,896]{1,0:T(8,128)(2,1)S(1)} %add_convert_fusion.refs_5_), channel_id=1, source_target_pairs={{0,4},{1,3},{2,6},{3,1},{4,0},{5,7},{6,2},{7,5},{8,12},{9,11},{10,... | collective-permute-start | bytes 344072 | tf_op jit(solution)/shard_map/ppermute | solution.py:257
  48.5 0.8 %collective-permute-done.8.refs_2_ = bf16[128,768]{1,0:T(8,128)(2,1)S(1)} collective-permute-done((bf16[128,768]{1,0:T(8,128)(2,1)S(1)}, bf16[128,768]{1,0:T(8,128)(2,1)S(1)}, u32[]{:S(2)}, u32[]{:S(2)}) %collective-permute-start.8) | collective-permute-done | bytes 196640 | tf_op jit(solution)/shard_map/ppermute | solution.py:257
  49.3 3.4 %collective-permute-done.15.refs_6_ = bf16[64,896]{1,0:T(8,128)(2,1)S(1)} collective-permute-done((bf16[64,896]{1,0:T(8,128)(2,1)S(1)}, bf16[64,896]{1,0:T(8,128)(2,1)S(1)}, u32[]{:S(2)}, u32[]{:S(2)}) %collective-permute-start.15) | collective-permute-done | bytes 114720 | tf_op jit(solution)/shard_map/ppermute | solution.py:257
  52.7 0.9 %collective-permute-start.16 = (bf16[128,896]{1,0:T(8,128)(2,1)S(1)}, bf16[128,896]{1,0:T(8,128)(2,1)S(1)}, u32[]{:S(2)}, u32[]{:S(2)}) collective-permute-start(bf16[128,896]{1,0:T(8,128)(2,1)S(1)} %pad_maximum_fusion), channel_id=1, source_target_pairs={{0,2},{1,5},{2,0},{3,7},{4,6},{5,1},{6,4},{7,3},{8,10},{9,13},{10,... | collective-permute-start | bytes 688136 | tf_op jit(solution)/shard_map/ppermute | solution.py:257
  53.6 0.0 collective-permute-start.17
  53.7 5.1 %collective-permute-done.16.refs_7_ = bf16[128,896]{1,0:T(8,128)(2,1)S(1)} collective-permute-done((bf16[128,896]{1,0:T(8,128)(2,1)S(1)}, bf16[128,896]{1,0:T(8,128)(2,1)S(1)}, u32[]{:S(2)}, u32[]{:S(2)}) %collective-permute-start.16) | collective-permute-done | bytes 229408 | tf_op jit(solution)/shard_map/ppermute | solution.py:257
  58.8 0.0 collective-permute-start.18
  58.8 0.5 collective-permute-start.9
  59.3 0.0 collective-permute-start.10
  59.3 1.3 %collective-permute-done.9.refs_3_ = bf16[128,768]{1,0:T(8,128)(2,1)S(1)} collective-permute-done((bf16[128,768]{1,0:T(8,128)(2,1)S(1)}, bf16[128,768]{1,0:T(8,128)(2,1)S(1)}, u32[]{:S(2)}, u32[]{:S(2)}) %collective-permute-start.9) | collective-permute-done | bytes 196640 | tf_op jit(solution)/shard_map/ppermute | solution.py:257
  60.6 0.3 collective-permute-done.10.refs_4_
  60.9 0.0 collective-permute-done.17.refs_8_
  60.9 1.3 %shard_map.96 = (bf16[3,512,512]{2,1,0:T(8,128)(2,1)}, bf16[50,512]{1,0:T(8,128)(2,1)}) custom-call(bf16[64,768]{1,0:T(8,128)(2,1)S(1)} %add_convert_fusion.2.refs_0_, bf16[64,768]{1,0:T(8,128)(2,1)S(1)} %collective-permute-done.7.refs_1_, bf16[128,768]{1,0:T(8,128)(2,1)S(1)} %collective-permute-done.8.refs_2_, ...), custom_call_target="tpu_custom_call" | custom-call | bytes 3328000 | tf_op jit(solution)/shard_map/pallas_call | solution.py:25
  (8 shorter events, 0.2 us)
Async XLA Ops:
  4.9 7.8 %collective-permute-start.1 = (bf16[256,256]{1,0:T(8,128)(2,1)S(1)}, bf16[256,256]{1,0:T(8,128)(2,1)S(1)}, u32[]{:S(2)}, u32[]{:S(2)}) collective-permute-start(bf16[256,256]{1,0:T(8,128)(2,1)S(1)} %get-tuple-element.44), channel_id=1, source_target_pairs={{16,0},{17,1},{18,2},{19,3},{20,4},{21,5},{22,6},{23,7},{24,8},{25... | collective-permute-start | bytes 393224 | tf_op jit(solution)/shard_map/ppermute | solution.py:306
  8.1 8.6 %collective-permute-start.2 = (bf16[256,256]{1,0:T(8,128)(2,1)S(1)}, bf16[256,256]{1,0:T(8,128)(2,1)S(1)}, u32[]{:S(2)}, u32[]{:S(2)}) collective-permute-start(bf16[256,256]{1,0:T(8,128)(2,1)S(1)} %get-tuple-element.45), channel_id=1, source_target_pairs={{16,0},{17,1},{18,2},{19,3},{20,4},{21,5},{22,6},{23,7},{24,8},{25... | collective-permute-start | bytes 393224 | tf_op jit(solution)/shard_map/ppermute | solution.py:306
  10.0 12.1 %collective-permute-start = (bf16[512,256]{1,0:T(8,128)(2,1)S(1)}, bf16[512,256]{1,0:T(8,128)(2,1)S(1)}, u32[]{:S(2)}, u32[]{:S(2)}) collective-permute-start(bf16[512,256]{1,0:T(8,128)(2,1)S(1)} %shard_map.88), channel_id=1, source_target_pairs={{16,0},{17,1},{18,2},{19,3},{20,4},{21,5},{22,6},{23,7},{24,8},{25... | collective-permute-start | bytes 786440 | tf_op jit(solution)/shard_map/ppermute | solution.py:306
  17.6 1.8 %collective-permute-start.3 = (bf16[256,768]{1,0:T(8,128)(2,1)S(1)}, bf16[256,768]{1,0:T(8,128)(2,1)S(1)}, u32[]{:S(2)}, u32[]{:S(2)}) collective-permute-start(bf16[256,768]{1,0:T(8,128)(2,1)S(1)} %get-tuple-element.50), channel_id=1, source_target_pairs={{0,1},{1,0},{2,3},{3,2},{4,5},{5,4},{6,7},{7,6},{8,9},{9,8},{10,11... | collective-permute-start | bytes 1179656 | tf_op jit(solution)/shard_map/ppermute | solution.py:257
  19.5 6.2 %collective-permute-start.4 = (bf16[128,768]{1,0:T(8,128)(2,1)S(1)}, bf16[128,768]{1,0:T(8,128)(2,1)S(1)}, u32[]{:S(2)}, u32[]{:S(2)}) collective-permute-start(bf16[128,768]{1,0:T(8,128)(2,1)S(1)} %get-tuple-element.52), channel_id=1, source_target_pairs={{0,2},{1,5},{2,0},{3,7},{4,6},{5,1},{6,4},{7,3},{8,10},{9,13},{10,... | collective-permute-start | bytes 589832 | tf_op jit(solution)/shard_map/ppermute | solution.py:257
  25.7 2.2 %collective-permute-start.11 = (bf16[256,896]{1,0:T(8,128)(2,1)S(1)}, bf16[256,896]{1,0:T(8,128)(2,1)S(1)}, u32[]{:S(2)}, u32[]{:S(2)}) collective-permute-start(bf16[256,896]{1,0:T(8,128)(2,1)S(1)} %get-tuple-element.57), channel_id=1, source_target_pairs={{0,1},{1,0},{2,3},{3,2},{4,5},{5,4},{6,7},{7,6},{8,9},{9,8},{10,11... | collective-permute-start | bytes 1376264 | tf_op jit(solution)/shard_map/ppermute | solution.py:257
  25.8 4.7 %collective-permute-start.5 = (bf16[64,768]{1,0:T(8,128)(2,1)S(1)}, bf16[64,768]{1,0:T(8,128)(2,1)S(1)}, u32[]{:S(2)}, u32[]{:S(2)}) collective-permute-start(bf16[64,768]{1,0:T(8,128)(2,1)S(1)} %get-tuple-element.54), channel_id=1, source_target_pairs={{0,4},{1,3},{2,6},{3,1},{4,0},{5,7},{6,2},{7,5},{8,12},{9,11},{10,... | collective-permute-start | bytes 294920 | tf_op jit(solution)/shard_map/ppermute | solution.py:257
  28.0 6.1 %collective-permute-start.12 = (bf16[128,896]{1,0:T(8,128)(2,1)S(1)}, bf16[128,896]{1,0:T(8,128)(2,1)S(1)}, u32[]{:S(2)}, u32[]{:S(2)}) collective-permute-start(bf16[128,896]{1,0:T(8,128)(2,1)S(1)} %get-tuple-element.60), channel_id=1, source_target_pairs={{0,2},{1,5},{2,0},{3,7},{4,6},{5,1},{6,4},{7,3},{8,10},{9,13},{10,... | collective-permute-start | bytes 688136 | tf_op jit(solution)/shard_map/ppermute | solution.py:257
  30.5 7.9 %collective-permute-start.6 = (bf16[64,768]{1,0:T(8,128)(2,1)S(1)}, bf16[64,768]{1,0:T(8,128)(2,1)S(1)}, u32[]{:S(2)}, u32[]{:S(2)}) collective-permute-start(bf16[64,768]{1,0:T(8,128)(2,1)S(1)} %add_convert_fusion.3), channel_id=1, source_target_pairs={{0,8},{1,9},{2,10},{3,11},{4,12},{5,13},{6,14},{7,15},{8,0},{9,1},... | collective-permute-start | bytes 294920 | tf_op jit(solution)/shard_map/ppermute | solution.py:257
  34.2 5.4 %collective-permute-start.13 = (bf16[64,896]{1,0:T(8,128)(2,1)S(1)}, bf16[64,896]{1,0:T(8,128)(2,1)S(1)}, u32[]{:S(2)}, u32[]{:S(2)}) collective-permute-start(bf16[64,896]{1,0:T(8,128)(2,1)S(1)} %get-tuple-element.63), channel_id=1, source_target_pairs={{0,4},{1,3},{2,6},{3,1},{4,0},{5,7},{6,2},{7,5},{8,12},{9,11},{10,... | collective-permute-start | bytes 344072 | tf_op jit(solution)/shard_map/ppermute | solution.py:257
  38.4 4.9 %collective-permute-start.7 = (bf16[64,768]{1,0:T(8,128)(2,1)S(1)}, bf16[64,768]{1,0:T(8,128)(2,1)S(1)}, u32[]{:S(2)}, u32[]{:S(2)}) collective-permute-start(bf16[64,768]{1,0:T(8,128)(2,1)S(1)} %add_convert_fusion.2.refs_0_), channel_id=1, source_target_pairs={{0,4},{1,3},{2,6},{3,1},{4,0},{5,7},{6,2},{7,5},{8,12},{9,11},{10,... | collective-permute-start | bytes 294920 | tf_op jit(solution)/shard_map/ppermute | solution.py:257
  39.6 8.1 %collective-permute-start.14 = (bf16[64,896]{1,0:T(8,128)(2,1)S(1)}, bf16[64,896]{1,0:T(8,128)(2,1)S(1)}, u32[]{:S(2)}, u32[]{:S(2)}) collective-permute-start(bf16[64,896]{1,0:T(8,128)(2,1)S(1)} %add_convert_fusion.1), channel_id=1, source_target_pairs={{0,8},{1,9},{2,10},{3,11},{4,12},{5,13},{6,14},{7,15},{8,0},{9,1},... | collective-permute-start | bytes 344072 | tf_op jit(solution)/shard_map/ppermute | solution.py:257
  43.4 5.9 %collective-permute-start.8 = (bf16[128,768]{1,0:T(8,128)(2,1)S(1)}, bf16[128,768]{1,0:T(8,128)(2,1)S(1)}, u32[]{:S(2)}, u32[]{:S(2)}) collective-permute-start(bf16[128,768]{1,0:T(8,128)(2,1)S(1)} %pad_maximum_fusion.1), channel_id=1, source_target_pairs={{0,2},{1,5},{2,0},{3,7},{4,6},{5,1},{6,4},{7,3},{8,10},{9,13},{10,... | collective-permute-start | bytes 589832 | tf_op jit(solution)/shard_map/ppermute | solution.py:257
  47.8 4.9 %collective-permute-start.15 = (bf16[64,896]{1,0:T(8,128)(2,1)S(1)}, bf16[64,896]{1,0:T(8,128)(2,1)S(1)}, u32[]{:S(2)}, u32[]{:S(2)}) collective-permute-start(bf16[64,896]{1,0:T(8,128)(2,1)S(1)} %add_convert_fusion.refs_5_), channel_id=1, source_target_pairs={{0,4},{1,3},{2,6},{3,1},{4,0},{5,7},{6,2},{7,5},{8,12},{9,11},{10,... | collective-permute-start | bytes 344072 | tf_op jit(solution)/shard_map/ppermute | solution.py:257
  52.7 6.1 %collective-permute-start.16 = (bf16[128,896]{1,0:T(8,128)(2,1)S(1)}, bf16[128,896]{1,0:T(8,128)(2,1)S(1)}, u32[]{:S(2)}, u32[]{:S(2)}) collective-permute-start(bf16[128,896]{1,0:T(8,128)(2,1)S(1)} %pad_maximum_fusion), channel_id=1, source_target_pairs={{0,2},{1,5},{2,0},{3,7},{4,6},{5,1},{6,4},{7,3},{8,10},{9,13},{10,... | collective-permute-start | bytes 688136 | tf_op jit(solution)/shard_map/ppermute | solution.py:257
  53.6 7.2 %collective-permute-start.17 = (bf16[128,896]{1,0:T(8,128)(2,1)S(1)}, bf16[128,896]{1,0:T(8,128)(2,1)S(1)}, u32[]{:S(2)}, u32[]{:S(2)}) collective-permute-start(bf16[128,896]{1,0:T(8,128)(2,1)S(1)} %pad_maximum_fusion), channel_id=1, source_target_pairs={{0,1},{1,0},{2,3},{3,2},{4,5},{5,4},{6,7},{7,6},{8,9},{9,8},{10,11... | collective-permute-start | bytes 688136 | tf_op jit(solution)/shard_map/ppermute | solution.py:257
  58.8 2.1 %collective-permute-start.18 = (bf16[128,896]{1,0:T(8,128)(2,1)S(1)}, bf16[128,896]{1,0:T(8,128)(2,1)S(1)}, u32[]{:S(2)}, u32[]{:S(2)}) collective-permute-start(bf16[128,896]{1,0:T(8,128)(2,1)S(1)} %collective-permute-done.16.refs_7_), channel_id=1, source_target_pairs={{0,1},{1,0},{2,3},{3,2},{4,5},{5,4},{6,7},{7,6},{8,9},{9,8},{10,11... | collective-permute-start | bytes 688136 | tf_op jit(solution)/shard_map/ppermute | solution.py:257
  58.8 1.8 %collective-permute-start.9 = (bf16[128,768]{1,0:T(8,128)(2,1)S(1)}, bf16[128,768]{1,0:T(8,128)(2,1)S(1)}, u32[]{:S(2)}, u32[]{:S(2)}) collective-permute-start(bf16[128,768]{1,0:T(8,128)(2,1)S(1)} %pad_maximum_fusion.1), channel_id=1, source_target_pairs={{0,1},{1,0},{2,3},{3,2},{4,5},{5,4},{6,7},{7,6},{8,9},{9,8},{10,11... | collective-permute-start | bytes 589832 | tf_op jit(solution)/shard_map/ppermute | solution.py:257
  59.3 1.5 %collective-permute-start.10 = (bf16[128,768]{1,0:T(8,128)(2,1)S(1)}, bf16[128,768]{1,0:T(8,128)(2,1)S(1)}, u32[]{:S(2)}, u32[]{:S(2)}) collective-permute-start(bf16[128,768]{1,0:T(8,128)(2,1)S(1)} %collective-permute-done.8.refs_2_), channel_id=1, source_target_pairs={{0,1},{1,0},{2,3},{3,2},{4,5},{5,4},{6,7},{7,6},{8,9},{9,8},{10,11... | collective-permute-start | bytes 589832 | tf_op jit(solution)/shard_map/ppermute | solution.py:257

commit v5 on v4

--- a/solution.py
+++ b/solution.py
@@ -164,9 +164,19 @@
     return (g * factor).astype(BF16)
 
 
-def round_bit(orders, n, other=0):
-    mine, theirs = dp_bit(orders[other][n]), dp_bit(orders[1 - other][n])
-    return jnp.where(dp_bit(0) == 0, mine, theirs)
+def by_core(even, odd, other=False):
+    return jnp.where(dp_bit(0) == (1 if other else 0), even, odd)
+
+
+def place_in(bits, mask=0):
+    place = 0
+    for n in reversed(bits):
+        place = place * 2 + (1 - dp_bit(n) if (mask >> n) & 1 else dp_bit(n))
+    return place
+
+
+def mask_of(bits, offset):
+    return sum(1 << n for j, n in enumerate(bits) if (offset >> j) & 1)
 
 
 def weight_blocks(h_t, taps, scale, keep, send, cols):
@@ -220,27 +230,37 @@
         ref[:, 3 * width :] = jnp.where(part == 0, table_t[0:half], table_t[half:])
 
 
-def fold_kernel(orders, n, keep, recv, keep_out, send_out):
-    size = keep_out.shape[0]
-    bit = round_bit(orders, n)
-    for ref, part in ((keep_out, bit), (send_out, 1 - bit)):
+def fold_kernel(level, count, *refs):
+    summands, out = refs[:count], refs[count:]
+    size = out[0].shape[0]
+    for offset, ref in enumerate(out):
+        part = by_core(*(place_in(bits, mask_of(bits, offset)) for bits in level))
         at = pl.ds(pl.multiple_of(part * size, size), size)
-        ref[...] = (keep[at, :].astype(F32) + recv[at, :].astype(F32)).astype(BF16)
-
-
-def assemble_kernel(orders, widths, lists, *refs):
+        total = summands[0][at, :].astype(F32)
+        for other in summands[1:]:
+            total = total + other[at, :].astype(F32)
+        ref[...] = total.astype(BF16)
+
+
+def assemble_kernel(plans, *refs):
     weight_out, table_out, table_t = refs[-3:]
     pieces = list(refs[:-3])
     col = 0
-    for width in widths:
+    for width, levels, lists in plans:
         for offsets in lists:
             ref = pieces.pop(0)
             size = ref.shape[0] // len(offsets)
-            for slot, (core, flips) in enumerate(offsets):
-                block = dp_bit(0) if core == 0 else 1 - dp_bit(0)
-                for n in range(len(orders[0])):
-                    bit = round_bit(orders, n, core)
-                    block = block * 2 + (1 - bit if (flips >> n) & 1 else bit)
+            for slot, (core, masks) in enumerate(offsets):
+                blocks = []
+                for parity in (0, 1):
+                    block = 0
+                    for level in levels:
+                        bits = level[parity]
+                        block = block * (1 << len(bits)) + place_in(bits, masks[parity])
+                    blocks.append(block)
+                block = by_core(*blocks, other=core == 1)
+                half = dp_bit(0) if core == 0 else 1 - dp_bit(0)
+                block = block + half * (weight_out.shape[1] // 2 // size)
                 row = pl.ds(pl.multiple_of(block * size, size), size)
                 here = slice(slot * size, (slot + 1) * size)
                 for k in range(3):
@@ -251,10 +271,23 @@
     table_out[...] = table_t[...].T[: table_out.shape[0]].astype(BF16)
 
 
-def swap(value, bit, other=None):
+def swap(value, even, odd=None):
     count = lax.axis_size("dp")
-    bits = (bit, bit if other is None else other)
-    return lax.ppermute(value, "dp", [(i, i ^ (1 << bits[i % 2])) for i in range(count)])
+    masks = (even, even if odd is None else odd)
+    return lax.ppermute(value, "dp", [(i, i ^ masks[i % 2]) for i in range(count)])
+
+
+def single(bits):
+    return [((a,), (b,)) for a, b in zip(bits, reversed(bits))]
+
+
+def double(bits):
+    pairs = [tuple(bits[n : n + 2]) for n in range(0, len(bits), 2)]
+    return [(pair, pair) for pair in pairs]
+
+
+def offsets_in(level):
+    return range(1, 1 << len(level[0]))
 
 
 def body(section_input, top_grad, conv_weight, step_table, timesteps, dilations):
@@ -342,12 +375,16 @@
         got = [[below(v[0]) for v in pieces], [below(late)]]
 
     inner = list(range(1, dp_bits - 1))
-    orders = (inner, inner[::-1])
-    chains = []
+    plans = []
+    pieces = []
+    before = []
+    ahead = None
     used = []
     accs = []
     for n, width in enumerate(sent):
         col = starts[n]
+        if ahead is not None and HOLD:
+            got[n], _ = lax.optimization_barrier((got[n], ahead))
         recv = tuple(slope) + tuple(got[n])
         if n < len(sent) - 1:
             g_now, taps_now, *blocks = call(
@@ -375,48 +412,70 @@
                     scratch=[pltpu.VMEM((rows, 3 * width), BF16)],
                 flops=10**11,
             )
-        chains.append((width, blocks))
-
-    widths = []
-    pieces = []
-    before = []
-    for width, (keep, send) in chains:
+        reduce_by, gather_by = CHAINS[n]
+        levels = reduce_by(inner)
         rounds = []
 
-        def ordered(arrived):
+        def ordered(*arrived):
+            arrived = list(arrived)
+            at = TIES.get(len(rounds))
             rounds.append(arrived)
-            if len(rounds) < len(before):
-                arrived = lax.optimization_barrier((arrived, before[len(rounds)]))[0]
+            if before and at is not None:
+                arrived = list(lax.optimization_barrier((*arrived, *before[at]))[: len(arrived)])
             return arrived
 
-        if before:
-            send = lax.optimization_barrier((send, before[1]))[0]
-        recv = ordered(swap(send, 0))
-        for n in range(len(inner)):
-            half = [like((keep.shape[0] // 2, keep.shape[1]), BF16)] * 2
-            keep, send = call(functools.partial(fold_kernel, orders, n), half, (keep, recv))
-            recv = ordered(swap(send, orders[0][n], orders[1][n]))
-        keep = (keep.astype(F32) + recv.astype(F32)).astype(BF16)
-        own = (keep.astype(F32) + ordered(swap(keep, dp_bits - 1)).astype(F32)).astype(BF16)
-        held = [(own, [(0, 0)])]
-        for n in reversed(range(len(inner))):
+        if before and FIRST:
+            blocks[1] = lax.optimization_barrier((blocks[1], *before[1]))[0]
+        blocks = [blocks[0]] + ordered(swap(blocks[1], 1))
+        for level in levels:
+            split = 1 << len(level[0])
+            blocks = call(
+                functools.partial(fold_kernel, level, len(blocks)),
+                [like((blocks[0].shape[0] // split, blocks[0].shape[1]), BF16)] * split,
+                tuple(blocks),
+            )
+            ahead = blocks[1]
+            arrived = [
+                swap(blocks[o], *(mask_of(bits, o) for bits in level)) for o in offsets_in(level)
+            ]
+            blocks = [blocks[0]] + ordered(*arrived)
+        keep = sum(v.astype(F32) for v in blocks).astype(BF16)
+        arrived = ordered(swap(keep, 1 << (dp_bits - 1)))
+        own = (keep.astype(F32) + arrived[0].astype(F32)).astype(BF16)
+        held = [(own, [(0, (0, 0))])]
+        for level in reversed(gather_by(inner)):
             message = jnp.concatenate([v for v, _ in held], axis=0) if len(held) > 1 else own
-            flips = [(0, f ^ (1 << n)) for _, offs in held for _, f in offs]
-            held.append((ordered(swap(message, orders[0][n], orders[1][n])), flips))
-        early = jnp.concatenate([v for v, _ in held[:-1]], axis=0)
-        held.append((swap(early, 0), [(1, f) for _, offs in held[:-1] for _, f in offs]))
-        held.append((swap(held[-2][0], 0), [(1, f) for _, f in held[-2][1]]))
+            offsets = [m for _, offs in held for _, m in offs]
+            masks = [tuple(mask_of(bits, o) for bits in level) for o in offsets_in(level)]
+            arrived = ordered(*(swap(message, *mask) for mask in masks))
+            held += [
+                (v, [(0, (m[0] ^ e, m[1] ^ o)) for m in offsets]) for v, (e, o) in zip(arrived, masks)
+            ]
+        late = 1 if gather_by is single else 3
+        early = jnp.concatenate([v for v, _ in held[:-late]], axis=0) if len(held) > late + 1 else held[0][0]
+        late = jnp.concatenate([v for v, _ in held[-late:]], axis=0) if late > 1 else held[-1][0]
+        count = early.shape[0] // own.shape[0]
+        masks = [m for _, offs in held for _, m in offs]
+        arrived = ordered(swap(early, 1), swap(late, 1))
+        held.append((arrived[0], [(1, m) for m in masks[:count]]))
+        held.append((arrived[1], [(1, m) for m in masks[count:]]))
         pieces += [v for v, _ in held]
-        widths.append(width)
+        plans.append((width, levels, [offs for _, offs in held]))
         before = rounds
 
     weight_out, table_out = call(
-        functools.partial(assemble_kernel, orders, widths, [o for _, o in held]),
+        functools.partial(assemble_kernel, plans),
         [like(weight.shape, BF16), like(table.shape, BF16)],
         tuple(pieces),
         scratch=[pltpu.VMEM((chans, 128), F32)],
     )
     return (grad[None], weight_out[None], table_out[None])
+
+
+CHAINS = ((single, single), (single, double))
+TIES = {4: 5}
+FIRST = True
+HOLD = False
 
 
 def solution(mesh):

time: 62.4 us -> 59.4 us (0.952)
  waiting for transfers between devices: 26.7 us -> 21.1 us
  starting transfers between devices: 22.8 us -> 25.3 us
    ppermute x16 -> x17, waiting for transfers between devices: 21.5 us -> 16 us  [swap(): lax.ppermute(value, 'dp', [(i, i ^ masks[i % 2]) for i in range(count)])]
    ppermute x16 -> x17, starting transfers between devices: 19 us -> 21.5 us  [swap(): lax.ppermute(value, 'dp', [(i, i ^ masks[i % 2]) for i in range(count)])]
  transfers between devices with their start and end apart: 19 -> 20, of which waited for: 15 -> 16; matrix products, arithmetic and copies ran while one was open for 0% -> 0% of each run, Pallas kernels for 10% -> 10%
where the time goes in v5:
time: 59.4 us; the launch traced here: 59.2 us
  starting transfers between devices  25.3 us (43%)
  waiting for transfers between devices  21.1 us (36%)
  Pallas kernels  11.1 us (19%)
  between operations  1.41 us (2%)
    ppermute x17, starting transfers between devices, swap(): lax.ppermute(value, 'dp', [(i, i ^ masks[i % 2]) for i in range(count)])  21.5 us
    ppermute x17, waiting for transfers between devices, swap(): lax.ppermute(value, 'dp', [(i, i ^ masks[i % 2]) for i in range(count)])  16 us
    pallas_call x12, Pallas kernels, call(): pl.pallas_call(kernel, out_shape=out_shape, in_specs=specs, out_specs=[VM...  11.1 us
    ppermute x3, waiting for transfers between devices, below(): lax.ppermute(value, 'section', [(i, i - 1) for i in range(1, section_coun...  5.16 us
    ppermute x3, starting transfers between devices, below(): lax.ppermute(value, 'section', [(i, i - 1) for i in range(1, section_coun...  3.88 us
  transfers between devices with their start and end apart: 20, of which 16 were waited for; matrix products, arithmetic and copies ran while one was open for 0% of the time, Pallas kernels for 10%

profile of v5, /device:TPU:0, one launch (start us, length us, event | category | flops | bytes accessed | tf_op | source)
XLA Modules:
  0.0 59.2 jit_solution(12345860759222080777)
XLA Ops:
  1.3 3.6 %shard_map.85 = (bf16[512,512]{1,0:T(8,128)(2,1)S(1)}, bf16[3,512,512]{2,1,0:T(8,128)(2,1)S(1)}, bf16[4,128,512]{2,1,0:T(8,128)(2,1)S(1)}, f32[128,128]{1,0:T(8,...) custom-call(s32[1]{0:T(128)S(6)} %copy.9.dil, s32[4]{0:T(128)} %ts.1, ...), custom_call_target="tpu_custom_call" | custom-call | flops 805306368 | bytes 6801428 | tf_op jit(solution)/shard_map/pallas_call | solution.py:25
  4.9 1.3 %collective-permute-start.1 = (bf16[256,256]{1,0:T(8,128)(2,1)S(1)}, bf16[256,256]{1,0:T(8,128)(2,1)S(1)}, u32[]{:S(2)}, u32[]{:S(2)}) collective-permute-start(bf16[256,256]{1,0:T(8,128)(2,1)S(1)} %get-tuple-element.42), channel_id=1, source_target_pairs={{16,0},{17,1},{18,2},{19,3},{20,4},{21,5},{22,6},{23,7},{24,8},{25... | collective-permute-start | bytes 393224 | tf_op jit(solution)/shard_map/ppermute | solution.py:339
  6.2 1.8 %shard_map.87 = (f32[256,512]{1,0:T(8,128)S(1)}, bf16[256,1536]{1,0:T(8,128)(2,1)S(1)}, bf16[256,256]{1,0:T(8,128)(2,1)S(1)}) custom-call(s32[1]{0:T(128)S(6)} %copy.9.dil, bf16[512,512]{1,0:T(8,128)(2,1)S(1)} %get-tuple-element.35.mixed, bf16[3,512,512]{2,1,0:T(8,128)(2,1)S(1)} %get-tuple-element.36.weight, bf16[4,128,512]{2,1,0:T(8,128)(2,1)S(1)} %get-tuple-element.34.top), custom_call_target="tpu_custom_call" | custom-call | flops 805306368 | bytes 4063236 | tf_op jit(solution)/shard_map/pallas_call | solution.py:25
  8.1 1.3 %collective-permute-start.2 = (bf16[256,256]{1,0:T(8,128)(2,1)S(1)}, bf16[256,256]{1,0:T(8,128)(2,1)S(1)}, u32[]{:S(2)}, u32[]{:S(2)}) collective-permute-start(bf16[256,256]{1,0:T(8,128)(2,1)S(1)} %get-tuple-element.43), channel_id=1, source_target_pairs={{16,0},{17,1},{18,2},{19,3},{20,4},{21,5},{22,6},{23,7},{24,8},{25... | collective-permute-start | bytes 393224 | tf_op jit(solution)/shard_map/ppermute | solution.py:339
  9.4 0.6 %shard_map.88 = bf16[512,256]{1,0:T(8,128)(2,1)S(1)} custom-call(bf16[3,512,512]{2,1,0:T(8,128)(2,1)S(1)} %get-tuple-element.36.weight, bf16[4,128,512]{2,1,0:T(8,128)(2,1)S(1)} %get-tuple-element.34.top, bf16[256,1536]{1,0:T(8,128)(2,1)S(1)} %get-tuple-element.40.rest_0_, bf16[256,1536]{1,0:T(8,128)(2,1)S(1)} %get-tuple-element.41.rest_1_), custom_call_target="tpu_custom_call" | custom-call | flops 402653184 | bytes 3932160 | tf_op jit(solution)/shard_map/pallas_call | solution.py:25
  10.0 1.3 %collective-permute-start = (bf16[512,256]{1,0:T(8,128)(2,1)S(1)}, bf16[512,256]{1,0:T(8,128)(2,1)S(1)}, u32[]{:S(2)}, u32[]{:S(2)}) collective-permute-start(bf16[512,256]{1,0:T(8,128)(2,1)S(1)} %shard_map.88), channel_id=1, source_target_pairs={{16,0},{17,1},{18,2},{19,3},{20,4},{21,5},{22,6},{23,7},{24,8},{25... | collective-permute-start | bytes 786440 | tf_op jit(solution)/shard_map/ppermute | solution.py:339
  11.3 0.2 shard_map.86.h_t
  11.5 1.2 %collective-permute-done.1.rest_2_ = bf16[256,256]{1,0:T(8,128)(2,1)S(1)} collective-permute-done((bf16[256,256]{1,0:T(8,128)(2,1)S(1)}, bf16[256,256]{1,0:T(8,128)(2,1)S(1)}, u32[]{:S(2)}, u32[]{:S(2)}) %collective-permute-start.1) | collective-permute-done | bytes 131104 | tf_op jit(solution)/shard_map/ppermute | solution.py:339
  12.7 4.0 %collective-permute-done.2.rest_3_ = bf16[256,256]{1,0:T(8,128)(2,1)S(1)} collective-permute-done((bf16[256,256]{1,0:T(8,128)(2,1)S(1)}, bf16[256,256]{1,0:T(8,128)(2,1)S(1)}, u32[]{:S(2)}, u32[]{:S(2)}) %collective-permute-start.2) | collective-permute-done | bytes 131104 | tf_op jit(solution)/shard_map/ppermute | solution.py:339
  16.6 1.0 %shard_map.89 = (bf16[512,256]{1,0:T(8,128)(2,1)S(1)}, bf16[512,768]{1,0:T(8,128)(2,1)S(1)}, bf16[256,768]{1,0:T(8,128)(2,1)S(1)}, bf16[256,768]{1,0:T(8,128)(2,1)S(1)}) custom-call(s32[1]{0:T(128)S(6)} %copy.9.dil, bf16[4,128,512]{2,1,0:T(8,128)(2,1)S(1)} %get-tuple-element.34.top, bf16[512,512]{1,0:T(8,128)(2,1)S(1)} %shard_map.86.h_t, ...), custom_call_target="tpu_custom_call" | custom-call | flops 402653184 | bytes 4194308 | tf_op jit(solution)/shard_map/pallas_call | solution.py:25
  17.6 0.1 collective-permute-start.3
  17.7 0.6 %shard_map.90.rest_4_ = f32[512,512]{1,0:T(8,128)S(1)} custom-call(bf16[512,768]{1,0:T(8,128)(2,1)S(1)} %get-tuple-element.45.taps, bf16[3,512,512]{2,1,0:T(8,128)(2,1)S(1)} %get-tuple-element.36.weight), custom_call_target="tpu_custom_call" | custom-call | flops 99999997952 | bytes 3407872 | tf_op jit(solution)/shard_map/pallas_call | solution.py:25
  18.3 1.1 %collective-permute-done.3.refs_1_ = bf16[256,768]{1,0:T(8,128)(2,1)S(1)} collective-permute-done((bf16[256,768]{1,0:T(8,128)(2,1)S(1)}, bf16[256,768]{1,0:T(8,128)(2,1)S(1)}, u32[]{:S(2)}, u32[]{:S(2)}) %collective-permute-start.3) | collective-permute-done | bytes 393248 | tf_op jit(solution)/shard_map/ppermute | solution.py:277
  19.4 0.1 shard_map.92
  19.5 2.5 %collective-permute-start.4 = (bf16[128,768]{1,0:T(8,128)(2,1)S(1)}, bf16[128,768]{1,0:T(8,128)(2,1)S(1)}, u32[]{:S(2)}, u32[]{:S(2)}) collective-permute-start(bf16[128,768]{1,0:T(8,128)(2,1)S(1)} %get-tuple-element.50), channel_id=1, source_target_pairs={{0,2},{1,5},{2,0},{3,7},{4,6},{5,1},{6,4},{7,3},{8,10},{9,13},{10,... | collective-permute-start | bytes 589832 | tf_op jit(solution)/shard_map/ppermute | solution.py:277
  22.1 0.0 collective-permute-done.rest_2_
  22.1 1.6 %shard_map.91 = (bf16[256,896]{1,0:T(8,128)(2,1)S(1)}, bf16[256,896]{1,0:T(8,128)(2,1)S(1)}, bf16[4,128,512]{2,1,0:T(8,128)(2,1)}) custom-call(s32[1]{0:T(128)S(6)} %copy.9.dil, bf16[4,128,512]{2,1,0:T(8,128)(2,1)S(1)} %get-tuple-element.34.top, bf16[512,512]{1,0:T(8,128)(2,1)S(1)} %shard_map.86.h_t, bf16[3,512,512]{2,1,0:T(8,128)(2,1)S(1)} %get-tuple-element.36.weight, ...), custom_call_target="tpu_custom_call" | custom-call | flops 99999997952 | bytes 6750212 | tf_op jit(solution)/shard_map/pallas_call | solution.py:25
  23.7 2.0 %collective-permute-done.4.refs_1_ = bf16[128,768]{1,0:T(8,128)(2,1)S(1)} collective-permute-done((bf16[128,768]{1,0:T(8,128)(2,1)S(1)}, bf16[128,768]{1,0:T(8,128)(2,1)S(1)}, u32[]{:S(2)}, u32[]{:S(2)}) %collective-permute-start.4) | collective-permute-done | bytes 196640 | tf_op jit(solution)/shard_map/ppermute | solution.py:277
  25.7 0.0 collective-permute-start.11
  25.8 2.1 %collective-permute-start.5 = (bf16[64,768]{1,0:T(8,128)(2,1)S(1)}, bf16[64,768]{1,0:T(8,128)(2,1)S(1)}, u32[]{:S(2)}, u32[]{:S(2)}) collective-permute-start(bf16[64,768]{1,0:T(8,128)(2,1)S(1)} %get-tuple-element.52), channel_id=1, source_target_pairs={{0,4},{1,3},{2,6},{3,1},{4,0},{5,7},{6,2},{7,5},{8,12},{9,11},{10,... | collective-permute-start | bytes 294920 | tf_op jit(solution)/shard_map/ppermute | solution.py:277
  27.9 0.1 shard_map.94
  28.0 1.7 %collective-permute-start.12 = (bf16[128,896]{1,0:T(8,128)(2,1)S(1)}, bf16[128,896]{1,0:T(8,128)(2,1)S(1)}, u32[]{:S(2)}, u32[]{:S(2)}) collective-permute-start(bf16[128,896]{1,0:T(8,128)(2,1)S(1)} %get-tuple-element.57), channel_id=1, source_target_pairs={{0,2},{1,5},{2,0},{3,7},{4,6},{5,1},{6,4},{7,3},{8,10},{9,13},{10,... | collective-permute-start | bytes 688136 | tf_op jit(solution)/shard_map/ppermute | solution.py:277
  29.7 0.8 %collective-permute-done.5 = bf16[64,768]{1,0:T(8,128)(2,1)S(1)} collective-permute-done((bf16[64,768]{1,0:T(8,128)(2,1)S(1)}, bf16[64,768]{1,0:T(8,128)(2,1)S(1)}, u32[]{:S(2)}, u32[]{:S(2)}) %collective-permute-start.5) | collective-permute-done | bytes 98336 | tf_op jit(solution)/shard_map/ppermute | solution.py:277
  30.5 3.1 %collective-permute-start.6 = (bf16[64,768]{1,0:T(8,128)(2,1)S(1)}, bf16[64,768]{1,0:T(8,128)(2,1)S(1)}, u32[]{:S(2)}, u32[]{:S(2)}) collective-permute-start(bf16[64,768]{1,0:T(8,128)(2,1)S(1)} %add_convert_fusion.3), channel_id=1, source_target_pairs={{0,8},{1,9},{2,10},{3,11},{4,12},{5,13},{6,14},{7,15},{8,0},{9,1},... | collective-permute-start | bytes 294920 | tf_op jit(solution)/shard_map/ppermute | solution.py:277
  33.7 0.5 collective-permute-done.12.refs_1_
  34.1 0.1 shard_map.95
  34.2 1.8 %collective-permute-start.13 = (bf16[64,896]{1,0:T(8,128)(2,1)S(1)}, bf16[64,896]{1,0:T(8,128)(2,1)S(1)}, u32[]{:S(2)}, u32[]{:S(2)}) collective-permute-start(bf16[64,896]{1,0:T(8,128)(2,1)S(1)} %get-tuple-element.59), channel_id=1, source_target_pairs={{0,4},{1,3},{2,6},{3,1},{4,0},{5,7},{6,2},{7,5},{8,12},{9,11},{10,... | collective-permute-start | bytes 344072 | tf_op jit(solution)/shard_map/ppermute | solution.py:277
  35.9 2.5 %collective-permute-done.6 = bf16[64,768]{1,0:T(8,128)(2,1)S(1)} collective-permute-done((bf16[64,768]{1,0:T(8,128)(2,1)S(1)}, bf16[64,768]{1,0:T(8,128)(2,1)S(1)}, u32[]{:S(2)}, u32[]{:S(2)}) %collective-permute-start.6) | collective-permute-done | bytes 98336 | tf_op jit(solution)/shard_map/ppermute | solution.py:277
  38.4 0.7 %collective-permute-start.7 = (bf16[64,768]{1,0:T(8,128)(2,1)S(1)}, bf16[64,768]{1,0:T(8,128)(2,1)S(1)}, u32[]{:S(2)}, u32[]{:S(2)}) collective-permute-start(bf16[64,768]{1,0:T(8,128)(2,1)S(1)} %add_convert_fusion.2.refs_0_), channel_id=1, source_target_pairs={{0,4},{1,3},{2,6},{3,1},{4,0},{5,7},{6,2},{7,5},{8,12},{9,11},{10,... | collective-permute-start | bytes 294920 | tf_op jit(solution)/shard_map/ppermute | solution.py:277
  39.2 0.4 collective-permute-done.13
  39.6 3.1 %collective-permute-start.14 = (bf16[64,896]{1,0:T(8,128)(2,1)S(1)}, bf16[64,896]{1,0:T(8,128)(2,1)S(1)}, u32[]{:S(2)}, u32[]{:S(2)}) collective-permute-start(bf16[64,896]{1,0:T(8,128)(2,1)S(1)} %add_convert_fusion.1), channel_id=1, source_target_pairs={{0,8},{1,9},{2,10},{3,11},{4,12},{5,13},{6,14},{7,15},{8,0},{9,1},... | collective-permute-start | bytes 344072 | tf_op jit(solution)/shard_map/ppermute | solution.py:277
  42.7 0.7 %collective-permute-done.7.refs_1_ = bf16[64,768]{1,0:T(8,128)(2,1)S(1)} collective-permute-done((bf16[64,768]{1,0:T(8,128)(2,1)S(1)}, bf16[64,768]{1,0:T(8,128)(2,1)S(1)}, u32[]{:S(2)}, u32[]{:S(2)}) %collective-permute-start.7) | collective-permute-done | bytes 98336 | tf_op jit(solution)/shard_map/ppermute | solution.py:277
  43.4 1.7 %collective-permute-start.8 = (bf16[128,768]{1,0:T(8,128)(2,1)S(1)}, bf16[128,768]{1,0:T(8,128)(2,1)S(1)}, u32[]{:S(2)}, u32[]{:S(2)}) collective-permute-start(bf16[128,768]{1,0:T(8,128)(2,1)S(1)} %pad_maximum_fusion.1), channel_id=1, source_target_pairs={{0,2},{1,5},{2,0},{3,7},{4,6},{5,1},{6,4},{7,3},{8,10},{9,13},{10,... | collective-permute-start | bytes 589832 | tf_op jit(solution)/shard_map/ppermute | solution.py:277
  45.1 2.7 %collective-permute-done.14 = bf16[64,896]{1,0:T(8,128)(2,1)S(1)} collective-permute-done((bf16[64,896]{1,0:T(8,128)(2,1)S(1)}, bf16[64,896]{1,0:T(8,128)(2,1)S(1)}, u32[]{:S(2)}, u32[]{:S(2)}) %collective-permute-start.14) | collective-permute-done | bytes 114720 | tf_op jit(solution)/shard_map/ppermute | solution.py:277
  47.8 1.0 %collective-permute-start.15 = (bf16[64,896]{1,0:T(8,128)(2,1)S(1)}, bf16[64,896]{1,0:T(8,128)(2,1)S(1)}, u32[]{:S(2)}, u32[]{:S(2)}) collective-permute-start(bf16[64,896]{1,0:T(8,128)(2,1)S(1)} %add_convert_fusion.refs_5_), channel_id=1, source_target_pairs={{0,2},{1,3},{2,0},{3,1},{4,6},{5,7},{6,4},{7,5},{8,10},{9,11},{10,... | collective-permute-start | bytes 344072 | tf_op jit(solution)/shard_map/ppermute | solution.py:277
  48.8 0.2 collective-permute-start.16
  49.0 2.4 %collective-permute-start.17 = (bf16[64,896]{1,0:T(8,128)(2,1)S(1)}, bf16[64,896]{1,0:T(8,128)(2,1)S(1)}, u32[]{:S(2)}, u32[]{:S(2)}) collective-permute-start(bf16[64,896]{1,0:T(8,128)(2,1)S(1)} %add_convert_fusion.refs_5_), channel_id=1, source_target_pairs={{0,6},{1,7},{2,4},{3,5},{4,2},{5,3},{6,0},{7,1},{8,14},{9,15},{10,... | collective-permute-start | bytes 344072 | tf_op jit(solution)/shard_map/ppermute | solution.py:277
  51.4 1.6 %collective-permute-done.15.refs_6_ = bf16[64,896]{1,0:T(8,128)(2,1)S(1)} collective-permute-done((bf16[64,896]{1,0:T(8,128)(2,1)S(1)}, bf16[64,896]{1,0:T(8,128)(2,1)S(1)}, u32[]{:S(2)}, u32[]{:S(2)}) %collective-permute-start.15) | collective-permute-done | bytes 114720 | tf_op jit(solution)/shard_map/ppermute | solution.py:277
  53.0 0.6 collective-permute-done.16.refs_7_
  53.6 1.8 %collective-permute-done.17.refs_8_ = bf16[64,896]{1,0:T(8,128)(2,1)S(1)} collective-permute-done((bf16[64,896]{1,0:T(8,128)(2,1)S(1)}, bf16[64,896]{1,0:T(8,128)(2,1)S(1)}, u32[]{:S(2)}, u32[]{:S(2)}) %collective-permute-start.17) | collective-permute-done | bytes 114720 | tf_op jit(solution)/shard_map/ppermute | solution.py:277
  55.4 0.1 collective-permute-start.19
  55.5 0.5 collective-permute-start.9
  56.0 0.1 collective-permute-start.10
  56.0 0.4 collective-permute-start.18
  56.5 0.9 %collective-permute-done.9.refs_3_ = bf16[128,768]{1,0:T(8,128)(2,1)S(1)} collective-permute-done((bf16[128,768]{1,0:T(8,128)(2,1)S(1)}, bf16[128,768]{1,0:T(8,128)(2,1)S(1)}, u32[]{:S(2)}, u32[]{:S(2)}) %collective-permute-start.9) | collective-permute-done | bytes 196640 | tf_op jit(solution)/shard_map/ppermute | solution.py:277
  57.4 0.3 collective-permute-done.10.refs_4_
  57.7 0.2 collective-permute-done.18.refs_9_
  57.8 1.3 %shard_map.96 = (bf16[3,512,512]{2,1,0:T(8,128)(2,1)}, bf16[50,512]{1,0:T(8,128)(2,1)}) custom-call(bf16[64,768]{1,0:T(8,128)(2,1)S(1)} %add_convert_fusion.2.refs_0_, bf16[64,768]{1,0:T(8,128)(2,1)S(1)} %collective-permute-done.7.refs_1_, bf16[128,768]{1,0:T(8,128)(2,1)S(1)} %collective-permute-done.8.refs_2_, ...), custom_call_target="tpu_custom_call" | custom-call | bytes 3328000 | tf_op jit(solution)/shard_map/pallas_call | solution.py:25
  (10 shorter events, 0.2 us)
Async XLA Ops:
  4.9 7.8 %collective-permute-start.1 = (bf16[256,256]{1,0:T(8,128)(2,1)S(1)}, bf16[256,256]{1,0:T(8,128)(2,1)S(1)}, u32[]{:S(2)}, u32[]{:S(2)}) collective-permute-start(bf16[256,256]{1,0:T(8,128)(2,1)S(1)} %get-tuple-element.42), channel_id=1, source_target_pairs={{16,0},{17,1},{18,2},{19,3},{20,4},{21,5},{22,6},{23,7},{24,8},{25... | collective-permute-start | bytes 393224 | tf_op jit(solution)/shard_map/ppermute | solution.py:339
  8.1 8.6 %collective-permute-start.2 = (bf16[256,256]{1,0:T(8,128)(2,1)S(1)}, bf16[256,256]{1,0:T(8,128)(2,1)S(1)}, u32[]{:S(2)}, u32[]{:S(2)}) collective-permute-start(bf16[256,256]{1,0:T(8,128)(2,1)S(1)} %get-tuple-element.43), channel_id=1, source_target_pairs={{16,0},{17,1},{18,2},{19,3},{20,4},{21,5},{22,6},{23,7},{24,8},{25... | collective-permute-start | bytes 393224 | tf_op jit(solution)/shard_map/ppermute | solution.py:339
  10.0 12.1 %collective-permute-start = (bf16[512,256]{1,0:T(8,128)(2,1)S(1)}, bf16[512,256]{1,0:T(8,128)(2,1)S(1)}, u32[]{:S(2)}, u32[]{:S(2)}) collective-permute-start(bf16[512,256]{1,0:T(8,128)(2,1)S(1)} %shard_map.88), channel_id=1, source_target_pairs={{16,0},{17,1},{18,2},{19,3},{20,4},{21,5},{22,6},{23,7},{24,8},{25... | collective-permute-start | bytes 786440 | tf_op jit(solution)/shard_map/ppermute | solution.py:339
  17.6 1.8 %collective-permute-start.3 = (bf16[256,768]{1,0:T(8,128)(2,1)S(1)}, bf16[256,768]{1,0:T(8,128)(2,1)S(1)}, u32[]{:S(2)}, u32[]{:S(2)}) collective-permute-start(bf16[256,768]{1,0:T(8,128)(2,1)S(1)} %get-tuple-element.48), channel_id=1, source_target_pairs={{0,1},{1,0},{2,3},{3,2},{4,5},{5,4},{6,7},{7,6},{8,9},{9,8},{10,11... | collective-permute-start | bytes 1179656 | tf_op jit(solution)/shard_map/ppermute | solution.py:277
  19.5 6.2 %collective-permute-start.4 = (bf16[128,768]{1,0:T(8,128)(2,1)S(1)}, bf16[128,768]{1,0:T(8,128)(2,1)S(1)}, u32[]{:S(2)}, u32[]{:S(2)}) collective-permute-start(bf16[128,768]{1,0:T(8,128)(2,1)S(1)} %get-tuple-element.50), channel_id=1, source_target_pairs={{0,2},{1,5},{2,0},{3,7},{4,6},{5,1},{6,4},{7,3},{8,10},{9,13},{10,... | collective-permute-start | bytes 589832 | tf_op jit(solution)/shard_map/ppermute | solution.py:277
  25.7 2.2 %collective-permute-start.11 = (bf16[256,896]{1,0:T(8,128)(2,1)S(1)}, bf16[256,896]{1,0:T(8,128)(2,1)S(1)}, u32[]{:S(2)}, u32[]{:S(2)}) collective-permute-start(bf16[256,896]{1,0:T(8,128)(2,1)S(1)} %get-tuple-element.55), channel_id=1, source_target_pairs={{0,1},{1,0},{2,3},{3,2},{4,5},{5,4},{6,7},{7,6},{8,9},{9,8},{10,11... | collective-permute-start | bytes 1376264 | tf_op jit(solution)/shard_map/ppermute | solution.py:277
  25.8 4.7 %collective-permute-start.5 = (bf16[64,768]{1,0:T(8,128)(2,1)S(1)}, bf16[64,768]{1,0:T(8,128)(2,1)S(1)}, u32[]{:S(2)}, u32[]{:S(2)}) collective-permute-start(bf16[64,768]{1,0:T(8,128)(2,1)S(1)} %get-tuple-element.52), channel_id=1, source_target_pairs={{0,4},{1,3},{2,6},{3,1},{4,0},{5,7},{6,2},{7,5},{8,12},{9,11},{10,... | collective-permute-start | bytes 294920 | tf_op jit(solution)/shard_map/ppermute | solution.py:277
  28.0 6.1 %collective-permute-start.12 = (bf16[128,896]{1,0:T(8,128)(2,1)S(1)}, bf16[128,896]{1,0:T(8,128)(2,1)S(1)}, u32[]{:S(2)}, u32[]{:S(2)}) collective-permute-start(bf16[128,896]{1,0:T(8,128)(2,1)S(1)} %get-tuple-element.57), channel_id=1, source_target_pairs={{0,2},{1,5},{2,0},{3,7},{4,6},{5,1},{6,4},{7,3},{8,10},{9,13},{10,... | collective-permute-start | bytes 688136 | tf_op jit(solution)/shard_map/ppermute | solution.py:277
  30.5 7.9 %collective-permute-start.6 = (bf16[64,768]{1,0:T(8,128)(2,1)S(1)}, bf16[64,768]{1,0:T(8,128)(2,1)S(1)}, u32[]{:S(2)}, u32[]{:S(2)}) collective-permute-start(bf16[64,768]{1,0:T(8,128)(2,1)S(1)} %add_convert_fusion.3), channel_id=1, source_target_pairs={{0,8},{1,9},{2,10},{3,11},{4,12},{5,13},{6,14},{7,15},{8,0},{9,1},... | collective-permute-start | bytes 294920 | tf_op jit(solution)/shard_map/ppermute | solution.py:277
  34.2 5.4 %collective-permute-start.13 = (bf16[64,896]{1,0:T(8,128)(2,1)S(1)}, bf16[64,896]{1,0:T(8,128)(2,1)S(1)}, u32[]{:S(2)}, u32[]{:S(2)}) collective-permute-start(bf16[64,896]{1,0:T(8,128)(2,1)S(1)} %get-tuple-element.59), channel_id=1, source_target_pairs={{0,4},{1,3},{2,6},{3,1},{4,0},{5,7},{6,2},{7,5},{8,12},{9,11},{10,... | collective-permute-start | bytes 344072 | tf_op jit(solution)/shard_map/ppermute | solution.py:277
  38.4 4.9 %collective-permute-start.7 = (bf16[64,768]{1,0:T(8,128)(2,1)S(1)}, bf16[64,768]{1,0:T(8,128)(2,1)S(1)}, u32[]{:S(2)}, u32[]{:S(2)}) collective-permute-start(bf16[64,768]{1,0:T(8,128)(2,1)S(1)} %add_convert_fusion.2.refs_0_), channel_id=1, source_target_pairs={{0,4},{1,3},{2,6},{3,1},{4,0},{5,7},{6,2},{7,5},{8,12},{9,11},{10,... | collective-permute-start | bytes 294920 | tf_op jit(solution)/shard_map/ppermute | solution.py:277
  39.6 8.1 %collective-permute-start.14 = (bf16[64,896]{1,0:T(8,128)(2,1)S(1)}, bf16[64,896]{1,0:T(8,128)(2,1)S(1)}, u32[]{:S(2)}, u32[]{:S(2)}) collective-permute-start(bf16[64,896]{1,0:T(8,128)(2,1)S(1)} %add_convert_fusion.1), channel_id=1, source_target_pairs={{0,8},{1,9},{2,10},{3,11},{4,12},{5,13},{6,14},{7,15},{8,0},{9,1},... | collective-permute-start | bytes 344072 | tf_op jit(solution)/shard_map/ppermute | solution.py:277
  43.4 8.0 %collective-permute-start.8 = (bf16[128,768]{1,0:T(8,128)(2,1)S(1)}, bf16[128,768]{1,0:T(8,128)(2,1)S(1)}, u32[]{:S(2)}, u32[]{:S(2)}) collective-permute-start(bf16[128,768]{1,0:T(8,128)(2,1)S(1)} %pad_maximum_fusion.1), channel_id=1, source_target_pairs={{0,2},{1,5},{2,0},{3,7},{4,6},{5,1},{6,4},{7,3},{8,10},{9,13},{10,... | collective-permute-start | bytes 589832 | tf_op jit(solution)/shard_map/ppermute | solution.py:277
  47.8 5.2 %collective-permute-start.15 = (bf16[64,896]{1,0:T(8,128)(2,1)S(1)}, bf16[64,896]{1,0:T(8,128)(2,1)S(1)}, u32[]{:S(2)}, u32[]{:S(2)}) collective-permute-start(bf16[64,896]{1,0:T(8,128)(2,1)S(1)} %add_convert_fusion.refs_5_), channel_id=1, source_target_pairs={{0,2},{1,3},{2,0},{3,1},{4,6},{5,7},{6,4},{7,5},{8,10},{9,11},{10,... | collective-permute-start | bytes 344072 | tf_op jit(solution)/shard_map/ppermute | solution.py:277
  48.8 4.8 %collective-permute-start.16 = (bf16[64,896]{1,0:T(8,128)(2,1)S(1)}, bf16[64,896]{1,0:T(8,128)(2,1)S(1)}, u32[]{:S(2)}, u32[]{:S(2)}) collective-permute-start(bf16[64,896]{1,0:T(8,128)(2,1)S(1)} %add_convert_fusion.refs_5_), channel_id=1, source_target_pairs={{0,4},{1,5},{2,6},{3,7},{4,0},{5,1},{6,2},{7,3},{8,12},{9,13},{10,... | collective-permute-start | bytes 344072 | tf_op jit(solution)/shard_map/ppermute | solution.py:277
  49.0 6.4 %collective-permute-start.17 = (bf16[64,896]{1,0:T(8,128)(2,1)S(1)}, bf16[64,896]{1,0:T(8,128)(2,1)S(1)}, u32[]{:S(2)}, u32[]{:S(2)}) collective-permute-start(bf16[64,896]{1,0:T(8,128)(2,1)S(1)} %add_convert_fusion.refs_5_), channel_id=1, source_target_pairs={{0,6},{1,7},{2,4},{3,5},{4,2},{5,3},{6,0},{7,1},{8,14},{9,15},{10,... | collective-permute-start | bytes 344072 | tf_op jit(solution)/shard_map/ppermute | solution.py:277
  55.4 2.4 %collective-permute-start.19 = (bf16[192,896]{1,0:T(8,128)(2,1)S(1)}, bf16[192,896]{1,0:T(8,128)(2,1)S(1)}, u32[]{:S(2)}, u32[]{:S(2)}) collective-permute-start(bf16[192,896]{1,0:T(8,128)(2,1)S(1)} %pad_maximum_fusion), channel_id=1, source_target_pairs={{0,1},{1,0},{2,3},{3,2},{4,5},{5,4},{6,7},{7,6},{8,9},{9,8},{10,11... | collective-permute-start | bytes 1032200 | tf_op jit(solution)/shard_map/ppermute | solution.py:277
  55.5 1.9 %collective-permute-start.9 = (bf16[128,768]{1,0:T(8,128)(2,1)S(1)}, bf16[128,768]{1,0:T(8,128)(2,1)S(1)}, u32[]{:S(2)}, u32[]{:S(2)}) collective-permute-start(bf16[128,768]{1,0:T(8,128)(2,1)S(1)} %pad_maximum_fusion.1), channel_id=1, source_target_pairs={{0,1},{1,0},{2,3},{3,2},{4,5},{5,4},{6,7},{7,6},{8,9},{9,8},{10,11... | collective-permute-start | bytes 589832 | tf_op jit(solution)/shard_map/ppermute | solution.py:277
  56.0 1.7 %collective-permute-start.10 = (bf16[128,768]{1,0:T(8,128)(2,1)S(1)}, bf16[128,768]{1,0:T(8,128)(2,1)S(1)}, u32[]{:S(2)}, u32[]{:S(2)}) collective-permute-start(bf16[128,768]{1,0:T(8,128)(2,1)S(1)} %collective-permute-done.8.refs_2_), channel_id=1, source_target_pairs={{0,1},{1,0},{2,3},{3,2},{4,5},{5,4},{6,7},{7,6},{8,9},{9,8},{10,11... | collective-permute-start | bytes 589832 | tf_op jit(solution)/shard_map/ppermute | solution.py:277
  56.0 1.8 %collective-permute-start.18 = (bf16[64,896]{1,0:T(8,128)(2,1)S(1)}, bf16[64,896]{1,0:T(8,128)(2,1)S(1)}, u32[]{:S(2)}, u32[]{:S(2)}) collective-permute-start(bf16[64,896]{1,0:T(8,128)(2,1)S(1)} %add_convert_fusion.refs_5_), channel_id=1, source_target_pairs={{0,1},{1,0},{2,3},{3,2},{4,5},{5,4},{6,7},{7,6},{8,9},{9,8},{10,11... | collective-permute-start | bytes 344072 | tf_op jit(solution)/shard_map/ppermute | solution.py:277

commit v6 on v5

--- a/solution.py
+++ b/solution.py
@@ -28,7 +28,7 @@
         in_specs=specs,
         out_specs=[VMEM] * len(out_shape),
         scratch_shapes=list(scratch),
-        compiler_params=pltpu.CompilerParams(vmem_limit_bytes=48 * 2**20),
+        compiler_params=pltpu.CompilerParams(vmem_limit_bytes=32 * 2**20),
         cost_estimate=pl.CostEstimate(flops=flops, bytes_accessed=moved, transcendentals=0),
     )(*args)
 
@@ -45,17 +45,21 @@
     return jax.ShapeDtypeStruct(shape, dtype)
 
 
-def put_taps(values, taps, bins, dilation, orientation):
+def shift_matrix(bins, dilation):
+    row = lax.broadcasted_iota(jnp.int32, (bins, bins), 0)
+    col = lax.broadcasted_iota(jnp.int32, (bins, bins), 1)
+    both = [jnp.where(col == row + by, 1.0, 0.0).astype(BF16) for by in (-dilation, dilation)]
+    return jnp.concatenate(both, axis=0)
+
+
+def put_taps(values, taps, shift, orientation):
     rows, cols = values.shape
-    place = lax.broadcasted_iota(jnp.int32, (bins, cols), 0)
+    bins = shift.shape[1]
     taps[:, cols : 2 * cols] = values
     for b in range(rows // bins):
         at = slice(b * bins, (b + 1) * bins)
-        group = values[at].astype(F32)
-        later = pltpu.roll(group, bins - dilation, 0)
-        later = jnp.where(place < bins - dilation, later, 0.0).astype(BF16)
-        earlier = pltpu.roll(group, dilation, 0)
-        earlier = jnp.where(place >= dilation, earlier, 0.0).astype(BF16)
+        moved = jnp.dot(shift[...], values[at], preferred_element_type=F32).astype(BF16)
+        earlier, later = moved[:bins], moved[bins:]
         first, third = (earlier, later) if orientation == 1 else (later, earlier)
         taps[at, 0:cols] = first
         taps[at, 2 * cols : 3 * cols] = third
@@ -71,17 +75,22 @@
     return total
 
 
-def forward(mixed, at, taps, bins, dilation, weight, slope):
-    put_taps(mixed[at, :], taps, bins, dilation, 1)
-    flat = weight[...].reshape(-1, weight.shape[2])
-    y = jnp.dot(taps[...], flat, preferred_element_type=F32)
+def forward(h, taps, shift, weight, slope, wait=None):
+    put_taps(h, taps, shift, 1)
+    chans = h.shape[1]
+    y = None
+    for k in range(3):
+        if wait is not None:
+            wait(k)
+        part = jnp.dot(taps[:, k * chans : (k + 1) * chans], weight[k], preferred_element_type=F32)
+        y = part if y is None else y + part
     gate = jax.nn.sigmoid(y)
     slope[...] = gate * (1.0 + y * (1.0 - gate))
 
 
-def backward(g, taps, bins, dilation, slope):
+def backward(g, taps, shift, slope):
     delta = (g * slope[...]).astype(BF16)
-    put_taps(delta, taps, bins, dilation, -1)
+    put_taps(delta, taps, shift, -1)
 
 
 def below_of(g, taps, weight, col, out):
@@ -90,39 +99,53 @@
     out[...] = (g[:, cols].astype(F32) + dh).astype(BF16)
 
 
-def first_kernel(dil, ts, x, table, weight, top, mixed, weight_v, top_v, hot, slope, taps, g_out, *s):
-    ts_s, x_v, table_v, tab, forward_taps, sems = s
-    pairs = ((ts, ts_s), (x, x_v), (table, table_v), (weight, weight_v), (top, top_v))
+def first_kernel(dil, ts, x, table, weight, top, mixed, weight_v, top_v, hot, shift, *rest):
+    slope, taps, g_out, ts_s, x_v, table_v, tab, forward_taps, sems = rest
+    groups, bins, chans = x.shape
+    rows = slope.shape[0]
+    near = slice(0, rows // bins)
+    others = slice(rows // bins, groups)
+    pairs = [(ts, ts_s), (table, table_v), (x.at[near], x_v.at[near])]
+    pairs += [(weight.at[k], weight_v.at[k]) for k in range(3)]
+    pairs += [(top.at[near], top_v.at[near]), (x.at[others], x_v.at[others]), (top.at[others], top_v.at[others])]
     copies = [pltpu.make_async_copy(a, b, sems.at[n]) for n, (a, b) in enumerate(pairs)]
     for copy in copies:
         copy.start()
-    groups, bins, chans = x.shape
+    shift[...] = shift_matrix(bins, dil[0])
     for copy in copies[:3]:
         copy.wait()
     tab[...] = table_v[...].astype(F32)
-    for b in range(groups):
+
+    def mix(b):
         row = x_v[b].astype(F32) + tab[pl.ds(ts_s[b], 1), :]
         mixed[b * bins : (b + 1) * bins, :] = row.astype(BF16)
+
+    for b in range(rows // bins):
+        mix(b)
+    forward(
+        mixed[0:rows, :], forward_taps, shift, weight_v, slope, lambda k: copies[3 + k].wait()
+    )
+    copies[6].wait()
+    g = top_v[near].reshape(rows, chans)
+    backward(g.astype(F32), taps, shift, slope)
+    below_of(g, taps, weight_v, 0, g_out)
     steps = lax.broadcasted_iota(jnp.int32, hot.shape, 0)
     lanes = lax.broadcasted_iota(jnp.int32, hot.shape, 1)
     marks = jnp.zeros(hot.shape, F32)
     for b in range(groups):
         marks = jnp.where((lanes == b) & (steps == ts_s[b]), 1.0, marks)
     hot[...] = marks
-    copies[3].wait()
-    rows = slope.shape[0]
-    forward(mixed, slice(0, rows), forward_taps, bins, dil[0], weight_v, slope)
-    copies[4].wait()
-    g = top_v[...].reshape(groups * bins, chans)[0:rows]
-    backward(g.astype(F32), taps, bins, dil[0], slope)
-    below_of(g, taps, weight_v, 0, g_out)
-
-
-def other_kernel(start, bins, dil, mixed, weight, top, slope, taps, g_out, forward_taps):
+    copies[7].wait()
+    for b in range(rows // bins, groups):
+        mix(b)
+    copies[8].wait()
+
+
+def other_kernel(start, shift, mixed, weight, top, slope, taps, g_out, forward_taps):
     at = slice(start, start + slope.shape[0])
-    forward(mixed, at, forward_taps, bins, dil[0], weight, slope)
+    forward(mixed[at, :], forward_taps, shift, weight, slope)
     g = top[...].reshape(mixed.shape)[at]
-    backward(g.astype(F32), taps, bins, dil[0], slope)
+    backward(g.astype(F32), taps, shift, slope)
     below_of(g, taps, weight, 0, g_out)
 
 
@@ -139,13 +162,13 @@
     h_t[...] = mixed[...].T
 
 
-def layer_kernel(start, bins, dil, slope, weight, top, *rest):
+def layer_kernel(start, shift, slope, weight, top, *rest):
     early, late, out, out_late, taps = rest
     rows = slope.shape[0]
     got = jnp.concatenate([early[...], late[start : start + rows]], axis=1)
     fresh = top[...].reshape(-1, top.shape[2])[start : start + rows]
     g = jnp.where(is_top(), fresh.astype(F32), got.astype(F32))
-    backward(g, taps, bins, dil[0], slope)
+    backward(g, taps, shift, slope)
     below_of(g, taps, weight, 0, out)
     below_of(g, taps, weight, out.shape[1], out_late)
 
@@ -188,14 +211,14 @@
         ref[:, 0:cols] = (prod * scale).astype(BF16)
 
 
-def weight_kernel(col, scale, dil, top, h_t, *rest):
+def weight_kernel(col, scale, shift, top, h_t, *rest):
     slope, recv, out = rest[:PARTS], rest[PARTS:-4], rest[-4:]
     g_used, taps, keep, send = out
     width = g_used.shape[1]
     g = upstream(col, top, recv)
     g_used[...] = g.astype(BF16)
     delta = delta_of(g, slope, col)
-    put_taps(delta, taps, top.shape[1], dil[0], -1)
+    put_taps(delta, taps, shift, -1)
     weight_blocks(h_t, taps, scale, keep, send, 3 * width)
 
 
@@ -204,7 +227,7 @@
     acc[...] = back_product(taps, weight[:, :, col : col + width], width)
 
 
-def last_kernel(col, scale, prior, dil, top, h_t, weight, hot, *rest):
+def last_kernel(col, scale, prior, shift, top, h_t, weight, hot, *rest):
     slope, recv = rest[:PARTS], rest[PARTS : -4 - 2 * prior]
     g_prior, acc = rest[-4 - 2 * prior : -4 - prior], rest[-4 - prior : -4]
     keep, send, grad, taps = rest[-4:]
@@ -212,7 +235,7 @@
     width = taps.shape[1] // 3
     g = upstream(col, top, recv)
     delta = delta_of(g, slope, col)
-    put_taps(delta, taps, bins, dil[0], -1)
+    put_taps(delta, taps, shift, -1)
     dh = back_product(taps, weight[:, :, col : col + width], width)
     for ref in acc:
         dh = dh + ref[...]
@@ -312,13 +335,14 @@
         like((part, sent[0]), BF16),
     ]
     far = (timesteps, x, table, weight, top_grad)
-    mixed, weight, top, hot, *first = call(
+    mixed, weight, top, hot, shift, *first = call(
         first_kernel,
         [
             like((rows, chans), BF16),
             like(weight.shape, BF16),
             like(x.shape, BF16),
             like((128, 128), F32),
+            like((2 * bins, bins), BF16),
         ]
         + of_part,
         (dilations,) + tuple(pltpu.with_memory_space_constraint(v, pltpu.HBM) for v in far),
@@ -330,7 +354,7 @@
             pltpu.VMEM(table.shape, BF16),
             pltpu.VMEM(table.shape, F32),
             room,
-            pltpu.SemaphoreType.DMA((5,)),
+            pltpu.SemaphoreType.DMA((9,)),
         ],
         flops=2 * unit // PARTS,
     )
@@ -342,10 +366,9 @@
     for n in range(1, PARTS):
         made.append(
             call(
-                functools.partial(other_kernel, n * part, bins),
+                functools.partial(other_kernel, n * part),
                 of_part,
-                (dilations, mixed, weight, top),
-                smem=1,
+                (shift, mixed, weight, top),
                 scratch=[room],
                 flops=2 * unit // PARTS,
             )
@@ -362,10 +385,9 @@
     for _ in range(section_count - 2):
         pieces = [
             call(
-                functools.partial(layer_kernel, n * part, bins),
+                functools.partial(layer_kernel, n * part),
                 [like((part, cols), BF16) for cols in sent],
-                (dilations, slope[n], weight, top, got[0][n], got[1][0]),
-                smem=1,
+                (shift, slope[n], weight, top, got[0][n], got[1][0]),
                 scratch=[room],
                 flops=unit // PARTS,
             )
@@ -391,8 +413,7 @@
                 functools.partial(weight_kernel, col, scale),
                 [like((rows, width), BF16), like((rows, 3 * width), BF16)]
                 + [like((chans // 2, 3 * width), BF16)] * 2,
-                (dilations, top, h_t) + recv,
-                smem=1,
+                (shift, top, h_t) + recv,
                     flops=unit * width // chans,
             )
             acc = call(
@@ -407,8 +428,7 @@
             *blocks, grad = call(
                 functools.partial(last_kernel, col, scale, len(used)),
                 [like((chans // 2, 3 * width + 128), BF16)] * 2 + [like(x.shape, BF16)],
-                (dilations, top, h_t, weight, hot) + recv + tuple(used) + tuple(accs),
-                smem=1,
+                (shift, top, h_t, weight, hot) + recv + tuple(used) + tuple(accs),
                     scratch=[pltpu.VMEM((rows, 3 * width), BF16)],
                 flops=10**11,
             )
@@ -451,14 +471,9 @@
             held += [
                 (v, [(0, (m[0] ^ e, m[1] ^ o)) for m in offsets]) for v, (e, o) in zip(arrived, masks)
             ]
-        late = 1 if gather_by is single else 3
-        early = jnp.concatenate([v for v, _ in held[:-late]], axis=0) if len(held) > late + 1 else held[0][0]
-        late = jnp.concatenate([v for v, _ in held[-late:]], axis=0) if late > 1 else held[-1][0]
-        count = early.shape[0] // own.shape[0]
+        message = jnp.concatenate([v for v, _ in held], axis=0)
         masks = [m for _, offs in held for _, m in offs]
-        arrived = ordered(swap(early, 1), swap(late, 1))
-        held.append((arrived[0], [(1, m) for m in masks[:count]]))
-        held.append((arrived[1], [(1, m) for m in masks[count:]]))
+        held.append((ordered(swap(message, 1))[0], [(1, m) for m in masks]))
         pieces += [v for v, _ in held]
         plans.append((width, levels, [offs for _, offs in held]))
         before = rounds

time: 59.4 us -> 58.3 us (0.981)
  Pallas kernels: 11.1 us -> 9.9 us
    pallas_call x12, Pallas kernels: 11.1 us -> 9.9 us  [call(): pl.pallas_call(kernel, out_shape=out_shape, in_specs=specs, out_specs=[VM...]
    ppermute x17 -> x15, waiting for transfers between devices: 16 us -> 16.4 us  [swap(): lax.ppermute(value, 'dp', [(i, i ^ masks[i % 2]) for i in range(count)])]
    ppermute x17 -> x15, starting transfers between devices: 21.5 us -> 21.2 us  [swap(): lax.ppermute(value, 'dp', [(i, i ^ masks[i % 2]) for i in range(count)])]
  transfers between devices with their start and end apart: 20 -> 18, of which waited for: 16 -> 14; matrix products, arithmetic and copies ran while one was open for 0% -> 0% of each run, Pallas kernels for 10% -> 10%
where the time goes in v6:
time: 58.3 us; the launch traced here: 58.1 us
  starting transfers between devices  25.1 us (43%)
  waiting for transfers between devices  21.5 us (37%)
  Pallas kernels  9.9 us (17%)
  between operations  1.42 us (2%)
    ppermute x15, starting transfers between devices, swap(): lax.ppermute(value, 'dp', [(i, i ^ masks[i % 2]) for i in range(count)])  21.2 us
    ppermute x15, waiting for transfers between devices, swap(): lax.ppermute(value, 'dp', [(i, i ^ masks[i % 2]) for i in range(count)])  16.4 us
    pallas_call x12, Pallas kernels, call(): pl.pallas_call(kernel, out_shape=out_shape, in_specs=specs, out_specs=[VM...  9.9 us
    ppermute x3, waiting for transfers between devices, below(): lax.ppermute(value, 'section', [(i, i - 1) for i in range(1, section_coun...  5.14 us
    ppermute x3, starting transfers between devices, below(): lax.ppermute(value, 'section', [(i, i - 1) for i in range(1, section_coun...  3.88 us
  transfers between devices with their start and end apart: 18, of which 14 were waited for; matrix products, arithmetic and copies ran while one was open for 0% of the time, Pallas kernels for 10%

profile of v6, /device:TPU:0, one launch (start us, length us, event | category | flops | bytes accessed | tf_op | source)
XLA Modules:
  0.0 58.1 jit_solution(15801827000458565806)
XLA Ops:
  1.3 3.0 %shard_map.85 = (bf16[512,512]{1,0:T(8,128)(2,1)S(1)}, bf16[3,512,512]{2,1,0:T(8,128)(2,1)S(1)}, bf16[4,128,512]{2,1,0:T(8,128)(2,1)S(1)}, f32[128,128]{1,0:T(8,...) custom-call(s32[1]{0:T(128)S(6)} %copy.9.dil, ...), custom_call_target="tpu_custom_call" | custom-call | flops 805306368 | bytes 6866964 | tf_op jit(solution)/shard_map/pallas_call | solution.py:25
  4.3 1.3 %collective-permute-start.1 = (bf16[256,256]{1,0:T(8,128)(2,1)S(1)}, bf16[256,256]{1,0:T(8,128)(2,1)S(1)}, u32[]{:S(2)}, u32[]{:S(2)}) collective-permute-start(bf16[256,256]{1,0:T(8,128)(2,1)S(1)} %get-tuple-element.44), channel_id=1, source_target_pairs={{16,0},{17,1},{18,2},{19,3},{20,4},{21,5},{22,6},{23,7},{24,8},{25... | collective-permute-start | bytes 393224 | tf_op jit(solution)/shard_map/ppermute | solution.py:363
  5.6 1.4 %shard_map.87 = (f32[256,512]{1,0:T(8,128)S(1)}, bf16[256,1536]{1,0:T(8,128)(2,1)S(1)}, bf16[256,256]{1,0:T(8,128)(2,1)S(1)}) custom-call(bf16[256,128]{1,0:T(8,128)(2,1)S(1)} %get-tuple-element.35.shift, bf16[512,512]{1,0:T(8,128)(2,1)S(1)} %get-tuple-element.37.mixed, bf16[3,512,512]{2,1,0:T(8,128)(2,1)S(1)} %get-tuple-element.38.weight, ...), custom_call_target="tpu_custom_call" | custom-call | flops 805306368 | bytes 4128768 | tf_op jit(solution)/shard_map/pallas_call | solution.py:25
  7.1 1.3 %collective-permute-start.2 = (bf16[256,256]{1,0:T(8,128)(2,1)S(1)}, bf16[256,256]{1,0:T(8,128)(2,1)S(1)}, u32[]{:S(2)}, u32[]{:S(2)}) collective-permute-start(bf16[256,256]{1,0:T(8,128)(2,1)S(1)} %get-tuple-element.45), channel_id=1, source_target_pairs={{16,0},{17,1},{18,2},{19,3},{20,4},{21,5},{22,6},{23,7},{24,8},{25... | collective-permute-start | bytes 393224 | tf_op jit(solution)/shard_map/ppermute | solution.py:363
  8.4 0.6 %shard_map.88 = bf16[512,256]{1,0:T(8,128)(2,1)S(1)} custom-call(bf16[3,512,512]{2,1,0:T(8,128)(2,1)S(1)} %get-tuple-element.38.weight, bf16[4,128,512]{2,1,0:T(8,128)(2,1)S(1)} %get-tuple-element.36.top, bf16[256,1536]{1,0:T(8,128)(2,1)S(1)} %get-tuple-element.42.rest_0_, bf16[256,1536]{1,0:T(8,128)(2,1)S(1)} %get-tuple-element.43.rest_1_), custom_call_target="tpu_custom_call" | custom-call | flops 402653184 | bytes 3932160 | tf_op jit(solution)/shard_map/pallas_call | solution.py:25
  9.0 1.3 %collective-permute-start = (bf16[512,256]{1,0:T(8,128)(2,1)S(1)}, bf16[512,256]{1,0:T(8,128)(2,1)S(1)}, u32[]{:S(2)}, u32[]{:S(2)}) collective-permute-start(bf16[512,256]{1,0:T(8,128)(2,1)S(1)} %shard_map.88), channel_id=1, source_target_pairs={{16,0},{17,1},{18,2},{19,3},{20,4},{21,5},{22,6},{23,7},{24,8},{25... | collective-permute-start | bytes 786440 | tf_op jit(solution)/shard_map/ppermute | solution.py:363
  10.3 0.2 shard_map.86.h_t
  10.5 1.6 %collective-permute-done.1.rest_2_ = bf16[256,256]{1,0:T(8,128)(2,1)S(1)} collective-permute-done((bf16[256,256]{1,0:T(8,128)(2,1)S(1)}, bf16[256,256]{1,0:T(8,128)(2,1)S(1)}, u32[]{:S(2)}, u32[]{:S(2)}) %collective-permute-start.1) | collective-permute-done | bytes 131104 | tf_op jit(solution)/shard_map/ppermute | solution.py:363
  12.1 3.5 %collective-permute-done.2.rest_3_ = bf16[256,256]{1,0:T(8,128)(2,1)S(1)} collective-permute-done((bf16[256,256]{1,0:T(8,128)(2,1)S(1)}, bf16[256,256]{1,0:T(8,128)(2,1)S(1)}, u32[]{:S(2)}, u32[]{:S(2)}) %collective-permute-start.2) | collective-permute-done | bytes 131104 | tf_op jit(solution)/shard_map/ppermute | solution.py:363
  15.6 0.8 %shard_map.89 = (bf16[512,256]{1,0:T(8,128)(2,1)S(1)}, bf16[512,768]{1,0:T(8,128)(2,1)S(1)}, bf16[256,768]{1,0:T(8,128)(2,1)S(1)}, bf16[256,768]{1,0:T(8,128)(2,1)S(1)}) custom-call(bf16[256,128]{1,0:T(8,128)(2,1)S(1)} %get-tuple-element.35.shift, bf16[4,128,512]{2,1,0:T(8,128)(2,1)S(1)} %get-tuple-element.36.top, bf16[512,512]{1,0:T(8,128)(2,1)S(1)} %shard_map.86.h_t, ...), custom_call_target="tpu_custom_call" | custom-call | flops 402653184 | bytes 4259840 | tf_op jit(solution)/shard_map/pallas_call | solution.py:25
  16.4 0.1 collective-permute-start.3
  16.5 0.6 %shard_map.90.rest_4_ = f32[512,512]{1,0:T(8,128)S(1)} custom-call(bf16[512,768]{1,0:T(8,128)(2,1)S(1)} %get-tuple-element.47.taps, bf16[3,512,512]{2,1,0:T(8,128)(2,1)S(1)} %get-tuple-element.38.weight), custom_call_target="tpu_custom_call" | custom-call | flops 99999997952 | bytes 3407872 | tf_op jit(solution)/shard_map/pallas_call | solution.py:25
  17.1 1.1 %collective-permute-done.3.refs_1_ = bf16[256,768]{1,0:T(8,128)(2,1)S(1)} collective-permute-done((bf16[256,768]{1,0:T(8,128)(2,1)S(1)}, bf16[256,768]{1,0:T(8,128)(2,1)S(1)}, u32[]{:S(2)}, u32[]{:S(2)}) %collective-permute-start.3) | collective-permute-done | bytes 393248 | tf_op jit(solution)/shard_map/ppermute | solution.py:300
  18.2 0.1 shard_map.92
  18.3 2.7 %collective-permute-start.4 = (bf16[128,768]{1,0:T(8,128)(2,1)S(1)}, bf16[128,768]{1,0:T(8,128)(2,1)S(1)}, u32[]{:S(2)}, u32[]{:S(2)}) collective-permute-start(bf16[128,768]{1,0:T(8,128)(2,1)S(1)} %get-tuple-element.52), channel_id=1, source_target_pairs={{0,2},{1,5},{2,0},{3,7},{4,6},{5,1},{6,4},{7,3},{8,10},{9,13},{10,... | collective-permute-start | bytes 589832 | tf_op jit(solution)/shard_map/ppermute | solution.py:300
  21.0 0.0 collective-permute-done.rest_2_
  21.0 1.6 %shard_map.91 = (bf16[256,896]{1,0:T(8,128)(2,1)S(1)}, bf16[256,896]{1,0:T(8,128)(2,1)S(1)}, bf16[4,128,512]{2,1,0:T(8,128)(2,1)}) custom-call(bf16[256,128]{1,0:T(8,128)(2,1)S(1)} %get-tuple-element.35.shift, bf16[4,128,512]{2,1,0:T(8,128)(2,1)S(1)} %get-tuple-element.36.top, bf16[512,512]{1,0:T(8,128)(2,1)S(1)} %shard_map.86.h_t, ...), custom_call_target="tpu_custom_call" | custom-call | flops 99999997952 | bytes 6815744 | tf_op jit(solution)/shard_map/pallas_call | solution.py:25
  22.6 2.0 %collective-permute-done.4.refs_1_ = bf16[128,768]{1,0:T(8,128)(2,1)S(1)} collective-permute-done((bf16[128,768]{1,0:T(8,128)(2,1)S(1)}, bf16[128,768]{1,0:T(8,128)(2,1)S(1)}, u32[]{:S(2)}, u32[]{:S(2)}) %collective-permute-start.4) | collective-permute-done | bytes 196640 | tf_op jit(solution)/shard_map/ppermute | solution.py:300
  24.6 0.0 collective-permute-start.10
  24.7 2.1 %collective-permute-start.5 = (bf16[64,768]{1,0:T(8,128)(2,1)S(1)}, bf16[64,768]{1,0:T(8,128)(2,1)S(1)}, u32[]{:S(2)}, u32[]{:S(2)}) collective-permute-start(bf16[64,768]{1,0:T(8,128)(2,1)S(1)} %get-tuple-element.54), channel_id=1, source_target_pairs={{0,4},{1,3},{2,6},{3,1},{4,0},{5,7},{6,2},{7,5},{8,12},{9,11},{10,... | collective-permute-start | bytes 294920 | tf_op jit(solution)/shard_map/ppermute | solution.py:300
  26.8 0.0 collective-permute-done.10.refs_1_
  26.8 0.1 shard_map.94
  27.0 1.7 %collective-permute-start.11 = (bf16[128,896]{1,0:T(8,128)(2,1)S(1)}, bf16[128,896]{1,0:T(8,128)(2,1)S(1)}, u32[]{:S(2)}, u32[]{:S(2)}) collective-permute-start(bf16[128,896]{1,0:T(8,128)(2,1)S(1)} %get-tuple-element.59), channel_id=1, source_target_pairs={{0,2},{1,5},{2,0},{3,7},{4,6},{5,1},{6,4},{7,3},{8,10},{9,13},{10,... | collective-permute-start | bytes 688136 | tf_op jit(solution)/shard_map/ppermute | solution.py:300
  28.7 0.8 %collective-permute-done.5 = bf16[64,768]{1,0:T(8,128)(2,1)S(1)} collective-permute-done((bf16[64,768]{1,0:T(8,128)(2,1)S(1)}, bf16[64,768]{1,0:T(8,128)(2,1)S(1)}, u32[]{:S(2)}, u32[]{:S(2)}) %collective-permute-start.5) | collective-permute-done | bytes 98336 | tf_op jit(solution)/shard_map/ppermute | solution.py:300
  29.5 3.1 %collective-permute-start.6 = (bf16[64,768]{1,0:T(8,128)(2,1)S(1)}, bf16[64,768]{1,0:T(8,128)(2,1)S(1)}, u32[]{:S(2)}, u32[]{:S(2)}) collective-permute-start(bf16[64,768]{1,0:T(8,128)(2,1)S(1)} %add_convert_fusion.3), channel_id=1, source_target_pairs={{0,8},{1,9},{2,10},{3,11},{4,12},{5,13},{6,14},{7,15},{8,0},{9,1},... | collective-permute-start | bytes 294920 | tf_op jit(solution)/shard_map/ppermute | solution.py:300
  32.6 0.5 collective-permute-done.11.refs_1_
  33.0 0.1 shard_map.95
  33.1 1.8 %collective-permute-start.12 = (bf16[64,896]{1,0:T(8,128)(2,1)S(1)}, bf16[64,896]{1,0:T(8,128)(2,1)S(1)}, u32[]{:S(2)}, u32[]{:S(2)}) collective-permute-start(bf16[64,896]{1,0:T(8,128)(2,1)S(1)} %get-tuple-element.61), channel_id=1, source_target_pairs={{0,4},{1,3},{2,6},{3,1},{4,0},{5,7},{6,2},{7,5},{8,12},{9,11},{10,... | collective-permute-start | bytes 344072 | tf_op jit(solution)/shard_map/ppermute | solution.py:300
  34.9 2.5 %collective-permute-done.6 = bf16[64,768]{1,0:T(8,128)(2,1)S(1)} collective-permute-done((bf16[64,768]{1,0:T(8,128)(2,1)S(1)}, bf16[64,768]{1,0:T(8,128)(2,1)S(1)}, u32[]{:S(2)}, u32[]{:S(2)}) %collective-permute-start.6) | collective-permute-done | bytes 98336 | tf_op jit(solution)/shard_map/ppermute | solution.py:300
  37.4 0.7 %collective-permute-start.7 = (bf16[64,768]{1,0:T(8,128)(2,1)S(1)}, bf16[64,768]{1,0:T(8,128)(2,1)S(1)}, u32[]{:S(2)}, u32[]{:S(2)}) collective-permute-start(bf16[64,768]{1,0:T(8,128)(2,1)S(1)} %add_convert_fusion.2.refs_0_), channel_id=1, source_target_pairs={{0,4},{1,3},{2,6},{3,1},{4,0},{5,7},{6,2},{7,5},{8,12},{9,11},{10,... | collective-permute-start | bytes 294920 | tf_op jit(solution)/shard_map/ppermute | solution.py:300
  38.1 0.4 collective-permute-done.12
  38.5 3.1 %collective-permute-start.13 = (bf16[64,896]{1,0:T(8,128)(2,1)S(1)}, bf16[64,896]{1,0:T(8,128)(2,1)S(1)}, u32[]{:S(2)}, u32[]{:S(2)}) collective-permute-start(bf16[64,896]{1,0:T(8,128)(2,1)S(1)} %add_convert_fusion.1), channel_id=1, source_target_pairs={{0,8},{1,9},{2,10},{3,11},{4,12},{5,13},{6,14},{7,15},{8,0},{9,1},... | collective-permute-start | bytes 344072 | tf_op jit(solution)/shard_map/ppermute | solution.py:300
  41.6 0.7 %collective-permute-done.7.refs_1_ = bf16[64,768]{1,0:T(8,128)(2,1)S(1)} collective-permute-done((bf16[64,768]{1,0:T(8,128)(2,1)S(1)}, bf16[64,768]{1,0:T(8,128)(2,1)S(1)}, u32[]{:S(2)}, u32[]{:S(2)}) %collective-permute-start.7) | collective-permute-done | bytes 98336 | tf_op jit(solution)/shard_map/ppermute | solution.py:300
  42.3 1.7 %collective-permute-start.8 = (bf16[128,768]{1,0:T(8,128)(2,1)S(1)}, bf16[128,768]{1,0:T(8,128)(2,1)S(1)}, u32[]{:S(2)}, u32[]{:S(2)}) collective-permute-start(bf16[128,768]{1,0:T(8,128)(2,1)S(1)} %pad_maximum_fusion.2), channel_id=1, source_target_pairs={{0,2},{1,5},{2,0},{3,7},{4,6},{5,1},{6,4},{7,3},{8,10},{9,13},{10,... | collective-permute-start | bytes 589832 | tf_op jit(solution)/shard_map/ppermute | solution.py:300
  44.0 2.7 %collective-permute-done.13 = bf16[64,896]{1,0:T(8,128)(2,1)S(1)} collective-permute-done((bf16[64,896]{1,0:T(8,128)(2,1)S(1)}, bf16[64,896]{1,0:T(8,128)(2,1)S(1)}, u32[]{:S(2)}, u32[]{:S(2)}) %collective-permute-start.13) | collective-permute-done | bytes 114720 | tf_op jit(solution)/shard_map/ppermute | solution.py:300
  46.7 1.0 %collective-permute-start.14 = (bf16[64,896]{1,0:T(8,128)(2,1)S(1)}, bf16[64,896]{1,0:T(8,128)(2,1)S(1)}, u32[]{:S(2)}, u32[]{:S(2)}) collective-permute-start(bf16[64,896]{1,0:T(8,128)(2,1)S(1)} %add_convert_fusion.refs_4_), channel_id=1, source_target_pairs={{0,2},{1,3},{2,0},{3,1},{4,6},{5,7},{6,4},{7,5},{8,10},{9,11},{10,... | collective-permute-start | bytes 344072 | tf_op jit(solution)/shard_map/ppermute | solution.py:300
  47.7 0.2 collective-permute-start.15
  47.9 2.4 %collective-permute-start.16 = (bf16[64,896]{1,0:T(8,128)(2,1)S(1)}, bf16[64,896]{1,0:T(8,128)(2,1)S(1)}, u32[]{:S(2)}, u32[]{:S(2)}) collective-permute-start(bf16[64,896]{1,0:T(8,128)(2,1)S(1)} %add_convert_fusion.refs_4_), channel_id=1, source_target_pairs={{0,6},{1,7},{2,4},{3,5},{4,2},{5,3},{6,0},{7,1},{8,14},{9,15},{10,... | collective-permute-start | bytes 344072 | tf_op jit(solution)/shard_map/ppermute | solution.py:300
  50.3 0.0 collective-permute-done.8.refs_2_
  50.3 1.6 %collective-permute-done.14.refs_5_ = bf16[64,896]{1,0:T(8,128)(2,1)S(1)} collective-permute-done((bf16[64,896]{1,0:T(8,128)(2,1)S(1)}, bf16[64,896]{1,0:T(8,128)(2,1)S(1)}, u32[]{:S(2)}, u32[]{:S(2)}) %collective-permute-start.14) | collective-permute-done | bytes 114720 | tf_op jit(solution)/shard_map/ppermute | solution.py:300
  51.9 0.6 collective-permute-done.15.refs_6_
  52.5 1.8 %collective-permute-done.16.refs_7_ = bf16[64,896]{1,0:T(8,128)(2,1)S(1)} collective-permute-done((bf16[64,896]{1,0:T(8,128)(2,1)S(1)}, bf16[64,896]{1,0:T(8,128)(2,1)S(1)}, u32[]{:S(2)}, u32[]{:S(2)}) %collective-permute-start.16) | collective-permute-done | bytes 114720 | tf_op jit(solution)/shard_map/ppermute | solution.py:300
  54.3 0.1 collective-permute-start.17
  54.4 0.6 collective-permute-start.9
  55.0 1.8 %collective-permute-done.9.refs_3_ = bf16[256,768]{1,0:T(8,128)(2,1)S(1)} collective-permute-done((bf16[256,768]{1,0:T(8,128)(2,1)S(1)}, bf16[256,768]{1,0:T(8,128)(2,1)S(1)}, u32[]{:S(2)}, u32[]{:S(2)}) %collective-permute-start.9) | collective-permute-done | bytes 393248 | tf_op jit(solution)/shard_map/ppermute | solution.py:300
  56.8 0.0 collective-permute-done.17.refs_8_
  56.8 1.3 %shard_map.96 = (bf16[3,512,512]{2,1,0:T(8,128)(2,1)}, bf16[50,512]{1,0:T(8,128)(2,1)}) custom-call(bf16[64,768]{1,0:T(8,128)(2,1)S(1)} %add_convert_fusion.2.refs_0_, bf16[64,768]{1,0:T(8,128)(2,1)S(1)} %collective-permute-done.7.refs_1_, bf16[128,768]{1,0:T(8,128)(2,1)S(1)} %collective-permute-done.8.refs_2_, ...), custom_call_target="tpu_custom_call" | custom-call | bytes 3328000 | tf_op jit(solution)/shard_map/pallas_call | solution.py:25
  (8 shorter events, 0.2 us)
Async XLA Ops:
  4.3 7.8 %collective-permute-start.1 = (bf16[256,256]{1,0:T(8,128)(2,1)S(1)}, bf16[256,256]{1,0:T(8,128)(2,1)S(1)}, u32[]{:S(2)}, u32[]{:S(2)}) collective-permute-start(bf16[256,256]{1,0:T(8,128)(2,1)S(1)} %get-tuple-element.44), channel_id=1, source_target_pairs={{16,0},{17,1},{18,2},{19,3},{20,4},{21,5},{22,6},{23,7},{24,8},{25... | collective-permute-start | bytes 393224 | tf_op jit(solution)/shard_map/ppermute | solution.py:363
  7.1 8.5 %collective-permute-start.2 = (bf16[256,256]{1,0:T(8,128)(2,1)S(1)}, bf16[256,256]{1,0:T(8,128)(2,1)S(1)}, u32[]{:S(2)}, u32[]{:S(2)}) collective-permute-start(bf16[256,256]{1,0:T(8,128)(2,1)S(1)} %get-tuple-element.45), channel_id=1, source_target_pairs={{16,0},{17,1},{18,2},{19,3},{20,4},{21,5},{22,6},{23,7},{24,8},{25... | collective-permute-start | bytes 393224 | tf_op jit(solution)/shard_map/ppermute | solution.py:363
  9.0 12.0 %collective-permute-start = (bf16[512,256]{1,0:T(8,128)(2,1)S(1)}, bf16[512,256]{1,0:T(8,128)(2,1)S(1)}, u32[]{:S(2)}, u32[]{:S(2)}) collective-permute-start(bf16[512,256]{1,0:T(8,128)(2,1)S(1)} %shard_map.88), channel_id=1, source_target_pairs={{16,0},{17,1},{18,2},{19,3},{20,4},{21,5},{22,6},{23,7},{24,8},{25... | collective-permute-start | bytes 786440 | tf_op jit(solution)/shard_map/ppermute | solution.py:363
  16.4 1.8 %collective-permute-start.3 = (bf16[256,768]{1,0:T(8,128)(2,1)S(1)}, bf16[256,768]{1,0:T(8,128)(2,1)S(1)}, u32[]{:S(2)}, u32[]{:S(2)}) collective-permute-start(bf16[256,768]{1,0:T(8,128)(2,1)S(1)} %get-tuple-element.50), channel_id=1, source_target_pairs={{0,1},{1,0},{2,3},{3,2},{4,5},{5,4},{6,7},{7,6},{8,9},{9,8},{10,11... | collective-permute-start | bytes 1179656 | tf_op jit(solution)/shard_map/ppermute | solution.py:300
  18.3 6.4 %collective-permute-start.4 = (bf16[128,768]{1,0:T(8,128)(2,1)S(1)}, bf16[128,768]{1,0:T(8,128)(2,1)S(1)}, u32[]{:S(2)}, u32[]{:S(2)}) collective-permute-start(bf16[128,768]{1,0:T(8,128)(2,1)S(1)} %get-tuple-element.52), channel_id=1, source_target_pairs={{0,2},{1,5},{2,0},{3,7},{4,6},{5,1},{6,4},{7,3},{8,10},{9,13},{10,... | collective-permute-start | bytes 589832 | tf_op jit(solution)/shard_map/ppermute | solution.py:300
  24.6 2.2 %collective-permute-start.10 = (bf16[256,896]{1,0:T(8,128)(2,1)S(1)}, bf16[256,896]{1,0:T(8,128)(2,1)S(1)}, u32[]{:S(2)}, u32[]{:S(2)}) collective-permute-start(bf16[256,896]{1,0:T(8,128)(2,1)S(1)} %get-tuple-element.57), channel_id=1, source_target_pairs={{0,1},{1,0},{2,3},{3,2},{4,5},{5,4},{6,7},{7,6},{8,9},{9,8},{10,11... | collective-permute-start | bytes 1376264 | tf_op jit(solution)/shard_map/ppermute | solution.py:300
  24.7 4.7 %collective-permute-start.5 = (bf16[64,768]{1,0:T(8,128)(2,1)S(1)}, bf16[64,768]{1,0:T(8,128)(2,1)S(1)}, u32[]{:S(2)}, u32[]{:S(2)}) collective-permute-start(bf16[64,768]{1,0:T(8,128)(2,1)S(1)} %get-tuple-element.54), channel_id=1, source_target_pairs={{0,4},{1,3},{2,6},{3,1},{4,0},{5,7},{6,2},{7,5},{8,12},{9,11},{10,... | collective-permute-start | bytes 294920 | tf_op jit(solution)/shard_map/ppermute | solution.py:300
  27.0 6.1 %collective-permute-start.11 = (bf16[128,896]{1,0:T(8,128)(2,1)S(1)}, bf16[128,896]{1,0:T(8,128)(2,1)S(1)}, u32[]{:S(2)}, u32[]{:S(2)}) collective-permute-start(bf16[128,896]{1,0:T(8,128)(2,1)S(1)} %get-tuple-element.59), channel_id=1, source_target_pairs={{0,2},{1,5},{2,0},{3,7},{4,6},{5,1},{6,4},{7,3},{8,10},{9,13},{10,... | collective-permute-start | bytes 688136 | tf_op jit(solution)/shard_map/ppermute | solution.py:300
  29.5 7.9 %collective-permute-start.6 = (bf16[64,768]{1,0:T(8,128)(2,1)S(1)}, bf16[64,768]{1,0:T(8,128)(2,1)S(1)}, u32[]{:S(2)}, u32[]{:S(2)}) collective-permute-start(bf16[64,768]{1,0:T(8,128)(2,1)S(1)} %add_convert_fusion.3), channel_id=1, source_target_pairs={{0,8},{1,9},{2,10},{3,11},{4,12},{5,13},{6,14},{7,15},{8,0},{9,1},... | collective-permute-start | bytes 294920 | tf_op jit(solution)/shard_map/ppermute | solution.py:300
  33.1 5.4 %collective-permute-start.12 = (bf16[64,896]{1,0:T(8,128)(2,1)S(1)}, bf16[64,896]{1,0:T(8,128)(2,1)S(1)}, u32[]{:S(2)}, u32[]{:S(2)}) collective-permute-start(bf16[64,896]{1,0:T(8,128)(2,1)S(1)} %get-tuple-element.61), channel_id=1, source_target_pairs={{0,4},{1,3},{2,6},{3,1},{4,0},{5,7},{6,2},{7,5},{8,12},{9,11},{10,... | collective-permute-start | bytes 344072 | tf_op jit(solution)/shard_map/ppermute | solution.py:300
  37.4 4.9 %collective-permute-start.7 = (bf16[64,768]{1,0:T(8,128)(2,1)S(1)}, bf16[64,768]{1,0:T(8,128)(2,1)S(1)}, u32[]{:S(2)}, u32[]{:S(2)}) collective-permute-start(bf16[64,768]{1,0:T(8,128)(2,1)S(1)} %add_convert_fusion.2.refs_0_), channel_id=1, source_target_pairs={{0,4},{1,3},{2,6},{3,1},{4,0},{5,7},{6,2},{7,5},{8,12},{9,11},{10,... | collective-permute-start | bytes 294920 | tf_op jit(solution)/shard_map/ppermute | solution.py:300
  38.5 8.1 %collective-permute-start.13 = (bf16[64,896]{1,0:T(8,128)(2,1)S(1)}, bf16[64,896]{1,0:T(8,128)(2,1)S(1)}, u32[]{:S(2)}, u32[]{:S(2)}) collective-permute-start(bf16[64,896]{1,0:T(8,128)(2,1)S(1)} %add_convert_fusion.1), channel_id=1, source_target_pairs={{0,8},{1,9},{2,10},{3,11},{4,12},{5,13},{6,14},{7,15},{8,0},{9,1},... | collective-permute-start | bytes 344072 | tf_op jit(solution)/shard_map/ppermute | solution.py:300
  42.3 8.0 %collective-permute-start.8 = (bf16[128,768]{1,0:T(8,128)(2,1)S(1)}, bf16[128,768]{1,0:T(8,128)(2,1)S(1)}, u32[]{:S(2)}, u32[]{:S(2)}) collective-permute-start(bf16[128,768]{1,0:T(8,128)(2,1)S(1)} %pad_maximum_fusion.2), channel_id=1, source_target_pairs={{0,2},{1,5},{2,0},{3,7},{4,6},{5,1},{6,4},{7,3},{8,10},{9,13},{10,... | collective-permute-start | bytes 589832 | tf_op jit(solution)/shard_map/ppermute | solution.py:300
  46.7 5.2 %collective-permute-start.14 = (bf16[64,896]{1,0:T(8,128)(2,1)S(1)}, bf16[64,896]{1,0:T(8,128)(2,1)S(1)}, u32[]{:S(2)}, u32[]{:S(2)}) collective-permute-start(bf16[64,896]{1,0:T(8,128)(2,1)S(1)} %add_convert_fusion.refs_4_), channel_id=1, source_target_pairs={{0,2},{1,3},{2,0},{3,1},{4,6},{5,7},{6,4},{7,5},{8,10},{9,11},{10,... | collective-permute-start | bytes 344072 | tf_op jit(solution)/shard_map/ppermute | solution.py:300
  47.7 4.8 %collective-permute-start.15 = (bf16[64,896]{1,0:T(8,128)(2,1)S(1)}, bf16[64,896]{1,0:T(8,128)(2,1)S(1)}, u32[]{:S(2)}, u32[]{:S(2)}) collective-permute-start(bf16[64,896]{1,0:T(8,128)(2,1)S(1)} %add_convert_fusion.refs_4_), channel_id=1, source_target_pairs={{0,4},{1,5},{2,6},{3,7},{4,0},{5,1},{6,2},{7,3},{8,12},{9,13},{10,... | collective-permute-start | bytes 344072 | tf_op jit(solution)/shard_map/ppermute | solution.py:300
  47.9 6.4 %collective-permute-start.16 = (bf16[64,896]{1,0:T(8,128)(2,1)S(1)}, bf16[64,896]{1,0:T(8,128)(2,1)S(1)}, u32[]{:S(2)}, u32[]{:S(2)}) collective-permute-start(bf16[64,896]{1,0:T(8,128)(2,1)S(1)} %add_convert_fusion.refs_4_), channel_id=1, source_target_pairs={{0,6},{1,7},{2,4},{3,5},{4,2},{5,3},{6,0},{7,1},{8,14},{9,15},{10,... | collective-permute-start | bytes 344072 | tf_op jit(solution)/shard_map/ppermute | solution.py:300
  54.3 2.4 %collective-permute-start.17 = (bf16[256,896]{1,0:T(8,128)(2,1)S(1)}, bf16[256,896]{1,0:T(8,128)(2,1)S(1)}, u32[]{:S(2)}, u32[]{:S(2)}) collective-permute-start(bf16[256,896]{1,0:T(8,128)(2,1)S(1)} %pad_maximum_fusion), channel_id=1, source_target_pairs={{0,1},{1,0},{2,3},{3,2},{4,5},{5,4},{6,7},{7,6},{8,9},{9,8},{10,11... | collective-permute-start | bytes 1376264 | tf_op jit(solution)/shard_map/ppermute | solution.py:300
  54.4 2.3 %collective-permute-start.9 = (bf16[256,768]{1,0:T(8,128)(2,1)S(1)}, bf16[256,768]{1,0:T(8,128)(2,1)S(1)}, u32[]{:S(2)}, u32[]{:S(2)}) collective-permute-start(bf16[256,768]{1,0:T(8,128)(2,1)S(1)} %pad_maximum_fusion.1), channel_id=1, source_target_pairs={{0,1},{1,0},{2,3},{3,2},{4,5},{5,4},{6,7},{7,6},{8,9},{9,8},{10,11... | collective-permute-start | bytes 1179656 | tf_op jit(solution)/shard_map/ppermute | solution.py:300

commit v7 on v6

--- a/solution.py
+++ b/solution.py
@@ -269,8 +269,8 @@
     weight_out, table_out, table_t = refs[-3:]
     pieces = list(refs[:-3])
     col = 0
-    for width, levels, lists in plans:
-        for offsets in lists:
+    for width, total, levels, lists in plans:
+        for left, offsets in lists:
             ref = pieces.pop(0)
             size = ref.shape[0] // len(offsets)
             for slot, (core, masks) in enumerate(offsets):
@@ -287,9 +287,11 @@
                 row = pl.ds(pl.multiple_of(block * size, size), size)
                 here = slice(slot * size, (slot + 1) * size)
                 for k in range(3):
-                    weight_out[k, row, col : col + width] = ref[here, k * width : (k + 1) * width]
-                if ref.shape[1] > 3 * width:
-                    table_t[row, :] = ref[here, 3 * width :].astype(F32)
+                    weight_out[k, row, col : col + width] = ref[
+                        here, left + k * width : left + (k + 1) * width
+                    ]
+                if total > 3 * width:
+                    table_t[row, :] = ref[here, left + 3 * width : left + total].astype(F32)
         col += width
     table_out[...] = table_t[...].T[: table_out.shape[0]].astype(BF16)
 
@@ -360,7 +362,10 @@
     )
 
     def below(value):
-        return lax.ppermute(value, "section", [(i, i - 1) for i in range(1, section_count)])
+        pairs = [(i, i - 1) for i in range(1, section_count)]
+        if section_count == 2:
+            pairs.append((0, 1))
+        return lax.ppermute(value, "section", pairs)
 
     made = [first]
     for n in range(1, PARTS):
@@ -397,8 +402,7 @@
         got = [[below(v[0]) for v in pieces], [below(late)]]
 
     inner = list(range(1, dp_bits - 1))
-    plans = []
-    pieces = []
+    gathered = []
     before = []
     ahead = None
     used = []
@@ -471,12 +475,19 @@
             held += [
                 (v, [(0, (m[0] ^ e, m[1] ^ o)) for m in offsets]) for v, (e, o) in zip(arrived, masks)
             ]
-        message = jnp.concatenate([v for v, _ in held], axis=0)
-        masks = [m for _, offs in held for _, m in offs]
-        held.append((ordered(swap(message, 1))[0], [(1, m) for m in masks]))
-        pieces += [v for v, _ in held]
-        plans.append((width, levels, [offs for _, offs in held]))
+        gathered.append((width, levels, held))
         before = rounds
+
+    both = [jnp.concatenate([v for v, _ in held], axis=0) for _, _, held in gathered]
+    crossed = swap(jnp.concatenate(both, axis=1), 1)
+    plans = []
+    pieces = []
+    at = 0
+    for width, levels, held in gathered:
+        lists = [(0, offs) for _, offs in held] + [(at, [(1, m) for _, offs in held for _, m in offs])]
+        plans.append((width, held[0][0].shape[1], levels, lists))
+        pieces += [v for v, _ in held] + [crossed]
+        at += held[0][0].shape[1]
 
     weight_out, table_out = call(
         functools.partial(assemble_kernel, plans),

time: 58.3 us -> 56.6 us (0.971)
  starting transfers between devices: 25.1 us -> 22.9 us
  waiting for transfers between devices: 21.5 us -> 22.1 us
    ppermute x15 -> x14, starting transfers between devices: 21.2 us -> 17.7 us  [swap(): lax.ppermute(value, 'dp', [(i, i ^ masks[i % 2]) for i in range(count)])]
    ppermute x15 -> x14, waiting for transfers between devices: 16.4 us -> 18.5 us  [swap(): lax.ppermute(value, 'dp', [(i, i ^ masks[i % 2]) for i in range(count)])]
    ppermute x3, waiting for transfers between devices: 5.14 us -> 3.54 us  [below(): return lax.ppermute(value, 'section', pairs)]
    ppermute x3, starting transfers between devices: 3.88 us -> 5.16 us  [below(): return lax.ppermute(value, 'section', pairs)]
  transfers between devices with their start and end apart: 18 -> 17, of which waited for: 14 -> 14; matrix products, arithmetic and copies ran while one was open for 0% -> 0% of each run, Pallas kernels for 10% -> 10%
where the time goes in v7:
time: 56.6 us; the launch traced here: 56.4 us
  starting transfers between devices  22.9 us (40%)
  waiting for transfers between devices  22.1 us (39%)
  Pallas kernels  9.9 us (17%)
  between operations  1.39 us (2%)
    ppermute x14, waiting for transfers between devices, swap(): lax.ppermute(value, 'dp', [(i, i ^ masks[i % 2]) for i in range(count)])  18.5 us
    ppermute x14, starting transfers between devices, swap(): lax.ppermute(value, 'dp', [(i, i ^ masks[i % 2]) for i in range(count)])  17.7 us
    pallas_call x12, Pallas kernels, call(): pl.pallas_call(kernel, out_shape=out_shape, in_specs=specs, out_specs=[VM...  9.9 us
    ppermute x3, starting transfers between devices, below(): return lax.ppermute(value, 'section', pairs)  5.16 us
    ppermute x3, waiting for transfers between devices, below(): return lax.ppermute(value, 'section', pairs)  3.54 us
  transfers between devices with their start and end apart: 17, of which 14 were waited for; matrix products, arithmetic and copies ran while one was open for 0% of the time, Pallas kernels for 10%

profile of v7, /device:TPU:0, one launch (start us, length us, event | category | flops | bytes accessed | tf_op | source)
XLA Modules:
  0.0 56.4 jit_solution(5700061780080381936)
XLA Ops:
  1.3 3.0 %shard_map.85 = (bf16[512,512]{1,0:T(8,128)(2,1)S(1)}, bf16[3,512,512]{2,1,0:T(8,128)(2,1)S(1)}, bf16[4,128,512]{2,1,0:T(8,128)(2,1)S(1)}, f32[128,128]{1,0:T(8,...) custom-call(s32[1]{0:T(128)S(6)} %copy.9.dil, ...), custom_call_target="tpu_custom_call" | custom-call | flops 805306368 | bytes 6866964 | tf_op jit(solution)/shard_map/pallas_call | solution.py:25
  4.3 3.0 %collective-permute-start.1 = (bf16[256,256]{1,0:T(8,128)(2,1)S(1)}, bf16[256,256]{1,0:T(8,128)(2,1)S(1)}, u32[]{:S(2)}, u32[]{:S(2)}) collective-permute-start(bf16[256,256]{1,0:T(8,128)(2,1)S(1)} %get-tuple-element.44), channel_id=1, source_target_pairs={{16,0},{0,16},{17,1},{1,17},{18,2},{2,18},{19,3},{3,19},{20,4},{4,... | collective-permute-start | bytes 393224 | tf_op jit(solution)/shard_map/ppermute | solution.py:368
  7.3 1.4 %shard_map.87 = (f32[256,512]{1,0:T(8,128)S(1)}, bf16[256,1536]{1,0:T(8,128)(2,1)S(1)}, bf16[256,256]{1,0:T(8,128)(2,1)S(1)}) custom-call(bf16[256,128]{1,0:T(8,128)(2,1)S(1)} %get-tuple-element.35.shift, bf16[512,512]{1,0:T(8,128)(2,1)S(1)} %get-tuple-element.37.mixed, bf16[3,512,512]{2,1,0:T(8,128)(2,1)S(1)} %get-tuple-element.38.weight, ...), custom_call_target="tpu_custom_call" | custom-call | flops 805306368 | bytes 4128768 | tf_op jit(solution)/shard_map/pallas_call | solution.py:25
  8.8 0.1 collective-permute-start.2
  8.8 0.6 %shard_map.88 = bf16[512,256]{1,0:T(8,128)(2,1)S(1)} custom-call(bf16[3,512,512]{2,1,0:T(8,128)(2,1)S(1)} %get-tuple-element.38.weight, bf16[4,128,512]{2,1,0:T(8,128)(2,1)S(1)} %get-tuple-element.36.top, bf16[256,1536]{1,0:T(8,128)(2,1)S(1)} %get-tuple-element.42.rest_0_, bf16[256,1536]{1,0:T(8,128)(2,1)S(1)} %get-tuple-element.43.rest_1_), custom_call_target="tpu_custom_call" | custom-call | flops 402653184 | bytes 3932160 | tf_op jit(solution)/shard_map/pallas_call | solution.py:25
  9.4 2.1 %collective-permute-start = (bf16[512,256]{1,0:T(8,128)(2,1)S(1)}, bf16[512,256]{1,0:T(8,128)(2,1)S(1)}, u32[]{:S(2)}, u32[]{:S(2)}) collective-permute-start(bf16[512,256]{1,0:T(8,128)(2,1)S(1)} %shard_map.88), channel_id=1, source_target_pairs={{16,0},{0,16},{17,1},{1,17},{18,2},{2,18},{19,3},{3,19},{20,4},{4,... | collective-permute-start | bytes 786440 | tf_op jit(solution)/shard_map/ppermute | solution.py:368
  11.5 0.2 shard_map.86.h_t
  11.7 0.0 collective-permute-done.1.rest_2_
  11.7 3.5 %collective-permute-done.2.rest_3_ = bf16[256,256]{1,0:T(8,128)(2,1)S(1)} collective-permute-done((bf16[256,256]{1,0:T(8,128)(2,1)S(1)}, bf16[256,256]{1,0:T(8,128)(2,1)S(1)}, u32[]{:S(2)}, u32[]{:S(2)}) %collective-permute-start.2) | collective-permute-done | bytes 131104 | tf_op jit(solution)/shard_map/ppermute | solution.py:368
  15.3 0.8 %shard_map.89 = (bf16[512,256]{1,0:T(8,128)(2,1)S(1)}, bf16[512,768]{1,0:T(8,128)(2,1)S(1)}, bf16[256,768]{1,0:T(8,128)(2,1)S(1)}, bf16[256,768]{1,0:T(8,128)(2,1)S(1)}) custom-call(bf16[256,128]{1,0:T(8,128)(2,1)S(1)} %get-tuple-element.35.shift, bf16[4,128,512]{2,1,0:T(8,128)(2,1)S(1)} %get-tuple-element.36.top, bf16[512,512]{1,0:T(8,128)(2,1)S(1)} %shard_map.86.h_t, ...), custom_call_target="tpu_custom_call" | custom-call | flops 402653184 | bytes 4259840 | tf_op jit(solution)/shard_map/pallas_call | solution.py:25
  16.1 0.1 collective-permute-start.3
  16.1 0.6 %shard_map.90.rest_4_ = f32[512,512]{1,0:T(8,128)S(1)} custom-call(bf16[512,768]{1,0:T(8,128)(2,1)S(1)} %get-tuple-element.47.taps, bf16[3,512,512]{2,1,0:T(8,128)(2,1)S(1)} %get-tuple-element.38.weight), custom_call_target="tpu_custom_call" | custom-call | flops 99999997952 | bytes 3407872 | tf_op jit(solution)/shard_map/pallas_call | solution.py:25
  16.7 1.1 %collective-permute-done.3.refs_1_ = bf16[256,768]{1,0:T(8,128)(2,1)S(1)} collective-permute-done((bf16[256,768]{1,0:T(8,128)(2,1)S(1)}, bf16[256,768]{1,0:T(8,128)(2,1)S(1)}, u32[]{:S(2)}, u32[]{:S(2)}) %collective-permute-start.3) | collective-permute-done | bytes 393248 | tf_op jit(solution)/shard_map/ppermute | solution.py:302
  17.8 0.1 shard_map.92
  17.9 1.6 %collective-permute-start.4 = (bf16[128,768]{1,0:T(8,128)(2,1)S(1)}, bf16[128,768]{1,0:T(8,128)(2,1)S(1)}, u32[]{:S(2)}, u32[]{:S(2)}) collective-permute-start(bf16[128,768]{1,0:T(8,128)(2,1)S(1)} %get-tuple-element.52), channel_id=1, source_target_pairs={{0,2},{1,5},{2,0},{3,7},{4,6},{5,1},{6,4},{7,3},{8,10},{9,13},{10,... | collective-permute-start | bytes 589832 | tf_op jit(solution)/shard_map/ppermute | solution.py:302
  19.5 0.0 collective-permute-done.rest_2_
  19.5 1.6 %shard_map.91 = (bf16[256,896]{1,0:T(8,128)(2,1)S(1)}, bf16[256,896]{1,0:T(8,128)(2,1)S(1)}, bf16[4,128,512]{2,1,0:T(8,128)(2,1)}) custom-call(bf16[256,128]{1,0:T(8,128)(2,1)S(1)} %get-tuple-element.35.shift, bf16[4,128,512]{2,1,0:T(8,128)(2,1)S(1)} %get-tuple-element.36.top, bf16[512,512]{1,0:T(8,128)(2,1)S(1)} %shard_map.86.h_t, ...), custom_call_target="tpu_custom_call" | custom-call | flops 99999997952 | bytes 6815744 | tf_op jit(solution)/shard_map/pallas_call | solution.py:25
  21.1 2.5 %collective-permute-done.4.refs_1_ = bf16[128,768]{1,0:T(8,128)(2,1)S(1)} collective-permute-done((bf16[128,768]{1,0:T(8,128)(2,1)S(1)}, bf16[128,768]{1,0:T(8,128)(2,1)S(1)}, u32[]{:S(2)}, u32[]{:S(2)}) %collective-permute-start.4) | collective-permute-done | bytes 196640 | tf_op jit(solution)/shard_map/ppermute | solution.py:302
  23.7 0.0 collective-permute-start.9
  23.7 1.6 %collective-permute-start.5 = (bf16[64,768]{1,0:T(8,128)(2,1)S(1)}, bf16[64,768]{1,0:T(8,128)(2,1)S(1)}, u32[]{:S(2)}, u32[]{:S(2)}) collective-permute-start(bf16[64,768]{1,0:T(8,128)(2,1)S(1)} %get-tuple-element.54), channel_id=1, source_target_pairs={{0,4},{1,3},{2,6},{3,1},{4,0},{5,7},{6,2},{7,5},{8,12},{9,11},{10,... | collective-permute-start | bytes 294920 | tf_op jit(solution)/shard_map/ppermute | solution.py:302
  25.4 0.1 collective-permute-done.9.refs_1_
  25.5 0.1 shard_map.94
  25.6 1.6 %collective-permute-start.10 = (bf16[128,896]{1,0:T(8,128)(2,1)S(1)}, bf16[128,896]{1,0:T(8,128)(2,1)S(1)}, u32[]{:S(2)}, u32[]{:S(2)}) collective-permute-start(bf16[128,896]{1,0:T(8,128)(2,1)S(1)} %get-tuple-element.59), channel_id=1, source_target_pairs={{0,2},{1,5},{2,0},{3,7},{4,6},{5,1},{6,4},{7,3},{8,10},{9,13},{10,... | collective-permute-start | bytes 688136 | tf_op jit(solution)/shard_map/ppermute | solution.py:302
  27.2 1.2 %collective-permute-done.5 = bf16[64,768]{1,0:T(8,128)(2,1)S(1)} collective-permute-done((bf16[64,768]{1,0:T(8,128)(2,1)S(1)}, bf16[64,768]{1,0:T(8,128)(2,1)S(1)}, u32[]{:S(2)}, u32[]{:S(2)}) %collective-permute-start.5) | collective-permute-done | bytes 98336 | tf_op jit(solution)/shard_map/ppermute | solution.py:302
  28.4 2.7 %collective-permute-start.6 = (bf16[64,768]{1,0:T(8,128)(2,1)S(1)}, bf16[64,768]{1,0:T(8,128)(2,1)S(1)}, u32[]{:S(2)}, u32[]{:S(2)}) collective-permute-start(bf16[64,768]{1,0:T(8,128)(2,1)S(1)} %add_convert_fusion.3), channel_id=1, source_target_pairs={{0,8},{1,9},{2,10},{3,11},{4,12},{5,13},{6,14},{7,15},{8,0},{9,1},... | collective-permute-start | bytes 294920 | tf_op jit(solution)/shard_map/ppermute | solution.py:302
  31.1 0.6 %collective-permute-done.10.refs_1_ = bf16[128,896]{1,0:T(8,128)(2,1)S(1)} collective-permute-done((bf16[128,896]{1,0:T(8,128)(2,1)S(1)}, bf16[128,896]{1,0:T(8,128)(2,1)S(1)}, u32[]{:S(2)}, u32[]{:S(2)}) %collective-permute-start.10) | collective-permute-done | bytes 229408 | tf_op jit(solution)/shard_map/ppermute | solution.py:302
  31.7 0.1 shard_map.95
  31.8 1.6 %collective-permute-start.11 = (bf16[64,896]{1,0:T(8,128)(2,1)S(1)}, bf16[64,896]{1,0:T(8,128)(2,1)S(1)}, u32[]{:S(2)}, u32[]{:S(2)}) collective-permute-start(bf16[64,896]{1,0:T(8,128)(2,1)S(1)} %get-tuple-element.61), channel_id=1, source_target_pairs={{0,4},{1,3},{2,6},{3,1},{4,0},{5,7},{6,2},{7,5},{8,12},{9,11},{10,... | collective-permute-start | bytes 344072 | tf_op jit(solution)/shard_map/ppermute | solution.py:302
  33.4 2.7 %collective-permute-done.6 = bf16[64,768]{1,0:T(8,128)(2,1)S(1)} collective-permute-done((bf16[64,768]{1,0:T(8,128)(2,1)S(1)}, bf16[64,768]{1,0:T(8,128)(2,1)S(1)}, u32[]{:S(2)}, u32[]{:S(2)}) %collective-permute-start.6) | collective-permute-done | bytes 98336 | tf_op jit(solution)/shard_map/ppermute | solution.py:302
  36.2 0.5 collective-permute-start.7
  36.6 0.7 %collective-permute-done.11 = bf16[64,896]{1,0:T(8,128)(2,1)S(1)} collective-permute-done((bf16[64,896]{1,0:T(8,128)(2,1)S(1)}, bf16[64,896]{1,0:T(8,128)(2,1)S(1)}, u32[]{:S(2)}, u32[]{:S(2)}) %collective-permute-start.11) | collective-permute-done | bytes 114720 | tf_op jit(solution)/shard_map/ppermute | solution.py:302
  37.3 2.8 %collective-permute-start.12 = (bf16[64,896]{1,0:T(8,128)(2,1)S(1)}, bf16[64,896]{1,0:T(8,128)(2,1)S(1)}, u32[]{:S(2)}, u32[]{:S(2)}) collective-permute-start(bf16[64,896]{1,0:T(8,128)(2,1)S(1)} %add_convert_fusion.1), channel_id=1, source_target_pairs={{0,8},{1,9},{2,10},{3,11},{4,12},{5,13},{6,14},{7,15},{8,0},{9,1},... | collective-permute-start | bytes 344072 | tf_op jit(solution)/shard_map/ppermute | solution.py:302
  40.2 0.8 %collective-permute-done.7.refs_1_ = bf16[64,768]{1,0:T(8,128)(2,1)S(1)} collective-permute-done((bf16[64,768]{1,0:T(8,128)(2,1)S(1)}, bf16[64,768]{1,0:T(8,128)(2,1)S(1)}, u32[]{:S(2)}, u32[]{:S(2)}) %collective-permute-start.7) | collective-permute-done | bytes 98336 | tf_op jit(solution)/shard_map/ppermute | solution.py:302
  40.9 1.6 %collective-permute-start.8 = (bf16[128,768]{1,0:T(8,128)(2,1)S(1)}, bf16[128,768]{1,0:T(8,128)(2,1)S(1)}, u32[]{:S(2)}, u32[]{:S(2)}) collective-permute-start(bf16[128,768]{1,0:T(8,128)(2,1)S(1)} %pad_maximum_fusion), channel_id=1, source_target_pairs={{0,2},{1,5},{2,0},{3,7},{4,6},{5,1},{6,4},{7,3},{8,10},{9,13},{10,... | collective-permute-start | bytes 589832 | tf_op jit(solution)/shard_map/ppermute | solution.py:302
  42.6 2.8 %collective-permute-done.12 = bf16[64,896]{1,0:T(8,128)(2,1)S(1)} collective-permute-done((bf16[64,896]{1,0:T(8,128)(2,1)S(1)}, bf16[64,896]{1,0:T(8,128)(2,1)S(1)}, u32[]{:S(2)}, u32[]{:S(2)}) %collective-permute-start.12) | collective-permute-done | bytes 114720 | tf_op jit(solution)/shard_map/ppermute | solution.py:302
  45.4 0.5 collective-permute-start.15
  45.9 1.9 %collective-permute-start.14 = (bf16[64,896]{1,0:T(8,128)(2,1)S(1)}, bf16[64,896]{1,0:T(8,128)(2,1)S(1)}, u32[]{:S(2)}, u32[]{:S(2)}) collective-permute-start(bf16[64,896]{1,0:T(8,128)(2,1)S(1)} %add_convert_fusion.refs_4_), channel_id=1, source_target_pairs={{0,4},{1,5},{2,6},{3,7},{4,0},{5,1},{6,2},{7,3},{8,12},{9,13},{10,... | collective-permute-start | bytes 344072 | tf_op jit(solution)/shard_map/ppermute | solution.py:302
  47.8 1.1 %collective-permute-start.13 = (bf16[64,896]{1,0:T(8,128)(2,1)S(1)}, bf16[64,896]{1,0:T(8,128)(2,1)S(1)}, u32[]{:S(2)}, u32[]{:S(2)}) collective-permute-start(bf16[64,896]{1,0:T(8,128)(2,1)S(1)} %add_convert_fusion.refs_4_), channel_id=1, source_target_pairs={{0,2},{1,3},{2,0},{3,1},{4,6},{5,7},{6,4},{7,5},{8,10},{9,11},{10,... | collective-permute-start | bytes 344072 | tf_op jit(solution)/shard_map/ppermute | solution.py:302
  48.9 0.0 collective-permute-done.8.refs_2_
  48.9 2.2 %collective-permute-done.15.refs_7_ = bf16[64,896]{1,0:T(8,128)(2,1)S(1)} collective-permute-done((bf16[64,896]{1,0:T(8,128)(2,1)S(1)}, bf16[64,896]{1,0:T(8,128)(2,1)S(1)}, u32[]{:S(2)}, u32[]{:S(2)}) %collective-permute-start.15) | collective-permute-done | bytes 114720 | tf_op jit(solution)/shard_map/ppermute | solution.py:302
  51.1 0.7 %collective-permute-done.14.refs_6_ = bf16[64,896]{1,0:T(8,128)(2,1)S(1)} collective-permute-done((bf16[64,896]{1,0:T(8,128)(2,1)S(1)}, bf16[64,896]{1,0:T(8,128)(2,1)S(1)}, u32[]{:S(2)}, u32[]{:S(2)}) %collective-permute-start.14) | collective-permute-done | bytes 114720 | tf_op jit(solution)/shard_map/ppermute | solution.py:302
  51.8 0.8 %collective-permute-done.13.refs_5_ = bf16[64,896]{1,0:T(8,128)(2,1)S(1)} collective-permute-done((bf16[64,896]{1,0:T(8,128)(2,1)S(1)}, bf16[64,896]{1,0:T(8,128)(2,1)S(1)}, u32[]{:S(2)}, u32[]{:S(2)}) %collective-permute-start.13) | collective-permute-done | bytes 114720 | tf_op jit(solution)/shard_map/ppermute | solution.py:302
  52.6 0.1 maximum_maximum_fusion
  52.6 0.1 collective-permute-start.16
  52.7 2.4 %collective-permute-done.16.refs_3_.refs_8_ = bf16[256,1664]{1,0:T(8,128)(2,1)S(1)} collective-permute-done((bf16[256,1664]{1,0:T(8,128)(2,1)S(1)}, bf16[256,1664]{1,0:T(8,128)(2,1)S(1)}, u32[]{:S(2)}, u32[]{:S(2)}) %collective-permute-start.16) | collective-permute-done | bytes 852000 | tf_op jit(solution)/shard_map/ppermute | solution.py:302
  55.1 1.3 %shard_map.96 = (bf16[3,512,512]{2,1,0:T(8,128)(2,1)}, bf16[50,512]{1,0:T(8,128)(2,1)}) custom-call(bf16[64,768]{1,0:T(8,128)(2,1)S(1)} %add_convert_fusion.2.refs_0_, bf16[64,768]{1,0:T(8,128)(2,1)S(1)} %collective-permute-done.7.refs_1_, bf16[128,768]{1,0:T(8,128)(2,1)S(1)} %collective-permute-done.8.refs_2_, ...), custom_call_target="tpu_custom_call" | custom-call | bytes 4179968 | tf_op jit(solution)/shard_map/pallas_call | solution.py:25
  (6 shorter events, 0.2 us)
Async XLA Ops:
  4.3 7.4 %collective-permute-start.1 = (bf16[256,256]{1,0:T(8,128)(2,1)S(1)}, bf16[256,256]{1,0:T(8,128)(2,1)S(1)}, u32[]{:S(2)}, u32[]{:S(2)}) collective-permute-start(bf16[256,256]{1,0:T(8,128)(2,1)S(1)} %get-tuple-element.44), channel_id=1, source_target_pairs={{16,0},{0,16},{17,1},{1,17},{18,2},{2,18},{19,3},{3,19},{20,4},{4,... | collective-permute-start | bytes 393224 | tf_op jit(solution)/shard_map/ppermute | solution.py:368
  8.8 6.5 %collective-permute-start.2 = (bf16[256,256]{1,0:T(8,128)(2,1)S(1)}, bf16[256,256]{1,0:T(8,128)(2,1)S(1)}, u32[]{:S(2)}, u32[]{:S(2)}) collective-permute-start(bf16[256,256]{1,0:T(8,128)(2,1)S(1)} %get-tuple-element.45), channel_id=1, source_target_pairs={{16,0},{0,16},{17,1},{1,17},{18,2},{2,18},{19,3},{3,19},{20,4},{4,... | collective-permute-start | bytes 393224 | tf_op jit(solution)/shard_map/ppermute | solution.py:368
  9.4 10.1 %collective-permute-start = (bf16[512,256]{1,0:T(8,128)(2,1)S(1)}, bf16[512,256]{1,0:T(8,128)(2,1)S(1)}, u32[]{:S(2)}, u32[]{:S(2)}) collective-permute-start(bf16[512,256]{1,0:T(8,128)(2,1)S(1)} %shard_map.88), channel_id=1, source_target_pairs={{16,0},{0,16},{17,1},{1,17},{18,2},{2,18},{19,3},{3,19},{20,4},{4,... | collective-permute-start | bytes 786440 | tf_op jit(solution)/shard_map/ppermute | solution.py:368
  16.1 1.8 %collective-permute-start.3 = (bf16[256,768]{1,0:T(8,128)(2,1)S(1)}, bf16[256,768]{1,0:T(8,128)(2,1)S(1)}, u32[]{:S(2)}, u32[]{:S(2)}) collective-permute-start(bf16[256,768]{1,0:T(8,128)(2,1)S(1)} %get-tuple-element.50), channel_id=1, source_target_pairs={{0,1},{1,0},{2,3},{3,2},{4,5},{5,4},{6,7},{7,6},{8,9},{9,8},{10,11... | collective-permute-start | bytes 1179656 | tf_op jit(solution)/shard_map/ppermute | solution.py:302
  17.9 5.7 %collective-permute-start.4 = (bf16[128,768]{1,0:T(8,128)(2,1)S(1)}, bf16[128,768]{1,0:T(8,128)(2,1)S(1)}, u32[]{:S(2)}, u32[]{:S(2)}) collective-permute-start(bf16[128,768]{1,0:T(8,128)(2,1)S(1)} %get-tuple-element.52), channel_id=1, source_target_pairs={{0,2},{1,5},{2,0},{3,7},{4,6},{5,1},{6,4},{7,3},{8,10},{9,13},{10,... | collective-permute-start | bytes 589832 | tf_op jit(solution)/shard_map/ppermute | solution.py:302
  23.7 1.8 %collective-permute-start.9 = (bf16[256,896]{1,0:T(8,128)(2,1)S(1)}, bf16[256,896]{1,0:T(8,128)(2,1)S(1)}, u32[]{:S(2)}, u32[]{:S(2)}) collective-permute-start(bf16[256,896]{1,0:T(8,128)(2,1)S(1)} %get-tuple-element.57), channel_id=1, source_target_pairs={{0,1},{1,0},{2,3},{3,2},{4,5},{5,4},{6,7},{7,6},{8,9},{9,8},{10,11... | collective-permute-start | bytes 1376264 | tf_op jit(solution)/shard_map/ppermute | solution.py:302
  23.7 4.7 %collective-permute-start.5 = (bf16[64,768]{1,0:T(8,128)(2,1)S(1)}, bf16[64,768]{1,0:T(8,128)(2,1)S(1)}, u32[]{:S(2)}, u32[]{:S(2)}) collective-permute-start(bf16[64,768]{1,0:T(8,128)(2,1)S(1)} %get-tuple-element.54), channel_id=1, source_target_pairs={{0,4},{1,3},{2,6},{3,1},{4,0},{5,7},{6,2},{7,5},{8,12},{9,11},{10,... | collective-permute-start | bytes 294920 | tf_op jit(solution)/shard_map/ppermute | solution.py:302
  25.6 6.1 %collective-permute-start.10 = (bf16[128,896]{1,0:T(8,128)(2,1)S(1)}, bf16[128,896]{1,0:T(8,128)(2,1)S(1)}, u32[]{:S(2)}, u32[]{:S(2)}) collective-permute-start(bf16[128,896]{1,0:T(8,128)(2,1)S(1)} %get-tuple-element.59), channel_id=1, source_target_pairs={{0,2},{1,5},{2,0},{3,7},{4,6},{5,1},{6,4},{7,3},{8,10},{9,13},{10,... | collective-permute-start | bytes 688136 | tf_op jit(solution)/shard_map/ppermute | solution.py:302
  28.4 7.7 %collective-permute-start.6 = (bf16[64,768]{1,0:T(8,128)(2,1)S(1)}, bf16[64,768]{1,0:T(8,128)(2,1)S(1)}, u32[]{:S(2)}, u32[]{:S(2)}) collective-permute-start(bf16[64,768]{1,0:T(8,128)(2,1)S(1)} %add_convert_fusion.3), channel_id=1, source_target_pairs={{0,8},{1,9},{2,10},{3,11},{4,12},{5,13},{6,14},{7,15},{8,0},{9,1},... | collective-permute-start | bytes 294920 | tf_op jit(solution)/shard_map/ppermute | solution.py:302
  31.8 5.5 %collective-permute-start.11 = (bf16[64,896]{1,0:T(8,128)(2,1)S(1)}, bf16[64,896]{1,0:T(8,128)(2,1)S(1)}, u32[]{:S(2)}, u32[]{:S(2)}) collective-permute-start(bf16[64,896]{1,0:T(8,128)(2,1)S(1)} %get-tuple-element.61), channel_id=1, source_target_pairs={{0,4},{1,3},{2,6},{3,1},{4,0},{5,7},{6,2},{7,5},{8,12},{9,11},{10,... | collective-permute-start | bytes 344072 | tf_op jit(solution)/shard_map/ppermute | solution.py:302
  36.2 4.8 %collective-permute-start.7 = (bf16[64,768]{1,0:T(8,128)(2,1)S(1)}, bf16[64,768]{1,0:T(8,128)(2,1)S(1)}, u32[]{:S(2)}, u32[]{:S(2)}) collective-permute-start(bf16[64,768]{1,0:T(8,128)(2,1)S(1)} %add_convert_fusion.2.refs_0_), channel_id=1, source_target_pairs={{0,4},{1,3},{2,6},{3,1},{4,0},{5,7},{6,2},{7,5},{8,12},{9,11},{10,... | collective-permute-start | bytes 294920 | tf_op jit(solution)/shard_map/ppermute | solution.py:302
  37.3 8.0 %collective-permute-start.12 = (bf16[64,896]{1,0:T(8,128)(2,1)S(1)}, bf16[64,896]{1,0:T(8,128)(2,1)S(1)}, u32[]{:S(2)}, u32[]{:S(2)}) collective-permute-start(bf16[64,896]{1,0:T(8,128)(2,1)S(1)} %add_convert_fusion.1), channel_id=1, source_target_pairs={{0,8},{1,9},{2,10},{3,11},{4,12},{5,13},{6,14},{7,15},{8,0},{9,1},... | collective-permute-start | bytes 344072 | tf_op jit(solution)/shard_map/ppermute | solution.py:302
  40.9 8.0 %collective-permute-start.8 = (bf16[128,768]{1,0:T(8,128)(2,1)S(1)}, bf16[128,768]{1,0:T(8,128)(2,1)S(1)}, u32[]{:S(2)}, u32[]{:S(2)}) collective-permute-start(bf16[128,768]{1,0:T(8,128)(2,1)S(1)} %pad_maximum_fusion), channel_id=1, source_target_pairs={{0,2},{1,5},{2,0},{3,7},{4,6},{5,1},{6,4},{7,3},{8,10},{9,13},{10,... | collective-permute-start | bytes 589832 | tf_op jit(solution)/shard_map/ppermute | solution.py:302
  45.4 5.8 %collective-permute-start.15 = (bf16[64,896]{1,0:T(8,128)(2,1)S(1)}, bf16[64,896]{1,0:T(8,128)(2,1)S(1)}, u32[]{:S(2)}, u32[]{:S(2)}) collective-permute-start(bf16[64,896]{1,0:T(8,128)(2,1)S(1)} %add_convert_fusion.refs_4_), channel_id=1, source_target_pairs={{0,6},{1,7},{2,4},{3,5},{4,2},{5,3},{6,0},{7,1},{8,14},{9,15},{10,... | collective-permute-start | bytes 344072 | tf_op jit(solution)/shard_map/ppermute | solution.py:302
  45.9 5.9 %collective-permute-start.14 = (bf16[64,896]{1,0:T(8,128)(2,1)S(1)}, bf16[64,896]{1,0:T(8,128)(2,1)S(1)}, u32[]{:S(2)}, u32[]{:S(2)}) collective-permute-start(bf16[64,896]{1,0:T(8,128)(2,1)S(1)} %add_convert_fusion.refs_4_), channel_id=1, source_target_pairs={{0,4},{1,5},{2,6},{3,7},{4,0},{5,1},{6,2},{7,3},{8,12},{9,13},{10,... | collective-permute-start | bytes 344072 | tf_op jit(solution)/shard_map/ppermute | solution.py:302
  47.8 4.8 %collective-permute-start.13 = (bf16[64,896]{1,0:T(8,128)(2,1)S(1)}, bf16[64,896]{1,0:T(8,128)(2,1)S(1)}, u32[]{:S(2)}, u32[]{:S(2)}) collective-permute-start(bf16[64,896]{1,0:T(8,128)(2,1)S(1)} %add_convert_fusion.refs_4_), channel_id=1, source_target_pairs={{0,2},{1,3},{2,0},{3,1},{4,6},{5,7},{6,4},{7,5},{8,10},{9,11},{10,... | collective-permute-start | bytes 344072 | tf_op jit(solution)/shard_map/ppermute | solution.py:302
  52.6 2.4 %collective-permute-start.16 = (bf16[256,1664]{1,0:T(8,128)(2,1)S(1)}, bf16[256,1664]{1,0:T(8,128)(2,1)S(1)}, u32[]{:S(2)}, u32[]{:S(2)}) collective-permute-start(bf16[256,1664]{1,0:T(8,128)(2,1)S(1)} %maximum_maximum_fusion), channel_id=1, source_target_pairs={{0,1},{1,0},{2,3},{3,2},{4,5},{5,4},{6,7},{7,6},{8,9},{9,8},{10,11... | collective-permute-start | bytes 2555912 | tf_op jit(solution)/shard_map/ppermute | solution.py:302

commit v8 on v7

--- a/solution.py
+++ b/solution.py
@@ -122,13 +122,24 @@
 
     for b in range(rows // bins):
         mix(b)
-    forward(
-        mixed[0:rows, :], forward_taps, shift, weight_v, slope, lambda k: copies[3 + k].wait()
-    )
-    copies[6].wait()
-    g = top_v[near].reshape(rows, chans)
-    backward(g.astype(F32), taps, shift, slope)
-    below_of(g, taps, weight_v, 0, g_out)
+
+    @pl.when(is_top())
+    def _():
+        def arrived(k):
+            copies[3 + k].wait()
+
+        forward(mixed[0:rows, :], forward_taps, shift, weight_v, slope, arrived)
+        copies[6].wait()
+        g = top_v[near].reshape(rows, chans)
+        backward(g.astype(F32), taps, shift, slope)
+        below_of(g, taps, weight_v, 0, g_out)
+
+    @pl.when(jnp.logical_not(is_top()))
+    def _():
+        for copy in copies[3:7]:
+            copy.wait()
+        g_out[...] = jnp.zeros(g_out.shape, BF16)
+
     steps = lax.broadcasted_iota(jnp.int32, hot.shape, 0)
     lanes = lax.broadcasted_iota(jnp.int32, hot.shape, 1)
     marks = jnp.zeros(hot.shape, F32)
@@ -142,24 +153,49 @@
 
 
 def other_kernel(start, shift, mixed, weight, top, slope, taps, g_out, forward_taps):
-    at = slice(start, start + slope.shape[0])
-    forward(mixed[at, :], forward_taps, shift, weight, slope)
-    g = top[...].reshape(mixed.shape)[at]
-    backward(g.astype(F32), taps, shift, slope)
-    below_of(g, taps, weight, 0, g_out)
+    @pl.when(is_top())
+    def _():
+        at = slice(start, start + slope.shape[0])
+        forward(mixed[at, :], forward_taps, shift, weight, slope)
+        g = top[...].reshape(mixed.shape)[at]
+        backward(g.astype(F32), taps, shift, slope)
+        below_of(g, taps, weight, 0, g_out)
+
+    @pl.when(jnp.logical_not(is_top()))
+    def _():
+        g_out[...] = jnp.zeros(g_out.shape, BF16)
 
 
 def rest_kernel(col, weight, top, *rest):
     taps, g_out = rest[:-1], rest[-1]
     part = taps[0].shape[0]
-    g = top[...].reshape(-1, top.shape[2])
-    for n, ref in enumerate(taps):
-        at = slice(n * part, (n + 1) * part)
-        below_of(g[at], ref, weight, col, g_out.at[at])
-
-
-def turn_kernel(mixed, h_t):
+
+    @pl.when(is_top())
+    def _():
+        g = top[...].reshape(-1, top.shape[2])
+        for n, ref in enumerate(taps):
+            at = slice(n * part, (n + 1) * part)
+            below_of(g[at], ref, weight, col, g_out.at[at])
+
+    @pl.when(jnp.logical_not(is_top()))
+    def _():
+        g_out[...] = jnp.zeros(g_out.shape, BF16)
+
+
+def prepare_kernel(shift, mixed, weight, *rest):
+    early, h_t, late, taps = rest[:PARTS], rest[PARTS], rest[PARTS + 1 : -1], rest[-1]
+    part = taps.shape[0]
     h_t[...] = mixed[...].T
+
+    @pl.when(is_top())
+    def _():
+        for n in range(PARTS):
+            late[n][...] = early[n][...]
+
+    @pl.when(jnp.logical_not(is_top()))
+    def _():
+        for n in range(PARTS):
+            forward(mixed[n * part : (n + 1) * part, :], taps, shift, weight, late[n])
 
 
 def layer_kernel(start, shift, slope, weight, top, *rest):
@@ -386,7 +422,13 @@
         flops=unit // 2,
     )[0]
     got = [[below(v[2]) for v in made], [below(late)]]
-    h_t = call(turn_kernel, [like((chans, rows), BF16)], (mixed,), flops=unit // 9)[0]
+    h_t, *slope = call(
+        prepare_kernel,
+        [like((chans, rows), BF16)] + [like((part, chans), F32)] * PARTS,
+        (shift, mixed, weight) + tuple(slope),
+        scratch=[room],
+        flops=unit // 9,
+    )
     for _ in range(section_count - 2):
         pieces = [
             call(

time: 56.6 us -> 55.8 us (0.986)
  Pallas kernels: 9.9 us -> 7.94 us
  starting transfers between devices: 22.9 us -> 24.8 us
  waiting for transfers between devices: 22.1 us -> 21.4 us
    pallas_call x12, Pallas kernels: 9.9 us -> 7.94 us  [call(): pl.pallas_call(kernel, out_shape=out_shape, in_specs=specs, out_specs=[VM...]
    ppermute x3, starting transfers between devices: 5.16 us -> 7.06 us  [below(): return lax.ppermute(value, 'section', pairs)]
  transfers between devices with their start and end apart: 17 -> 17, of which waited for: 14 -> 16; matrix products, arithmetic and copies ran while one was open for 0% -> 0% of each run, Pallas kernels for 10% -> 9%
where the time goes in v8:
time: 55.8 us; the launch traced here: 55.7 us
  starting transfers between devices  24.8 us (44%)
  waiting for transfers between devices  21.4 us (38%)
  Pallas kernels  7.94 us (14%)
  between operations  1.38 us (2%)
    ppermute x14, waiting for transfers between devices, swap(): lax.ppermute(value, 'dp', [(i, i ^ masks[i % 2]) for i in range(count)])  18 us
    ppermute x14, starting transfers between devices, swap(): lax.ppermute(value, 'dp', [(i, i ^ masks[i % 2]) for i in range(count)])  17.7 us
    pallas_call x12, Pallas kernels, call(): pl.pallas_call(kernel, out_shape=out_shape, in_specs=specs, out_specs=[VM...  7.94 us
    ppermute x3, starting transfers between devices, below(): return lax.ppermute(value, 'section', pairs)  7.06 us
    ppermute x3, waiting for transfers between devices, below(): return lax.ppermute(value, 'section', pairs)  3.37 us
  transfers between devices with their start and end apart: 17, of which 16 were waited for; matrix products, arithmetic and copies ran while one was open for 0% of the time, Pallas kernels for 9%

profile of v8, /device:TPU:0, one launch (start us, length us, event | category | flops | bytes accessed | tf_op | source)
XLA Modules:
  0.0 55.7 jit_solution(14044734033276456967)
XLA Ops:
  1.3 1.8 %shard_map.85 = (bf16[512,512]{1,0:T(8,128)(2,1)S(1)}, bf16[3,512,512]{2,1,0:T(8,128)(2,1)S(1)}, bf16[4,128,512]{2,1,0:T(8,128)(2,1)S(1)}, f32[128,128]{1,0:T(8,...) custom-call(s32[1]{0:T(128)S(6)} %copy.9.dil, ...), custom_call_target="tpu_custom_call" | custom-call | flops 805306368 | bytes 6866964 | tf_op jit(solution)/shard_map/pallas_call | solution.py:25
  3.1 4.3 %collective-permute-start.1 = (bf16[256,256]{1,0:T(8,128)(2,1)S(1)}, bf16[256,256]{1,0:T(8,128)(2,1)S(1)}, u32[]{:S(2)}, u32[]{:S(2)}) collective-permute-start(bf16[256,256]{1,0:T(8,128)(2,1)S(1)} %get-tuple-element.50), channel_id=1, source_target_pairs={{16,0},{0,16},{17,1},{1,17},{18,2},{2,18},{19,3},{3,19},{20,4},{4,... | collective-permute-start | bytes 393224 | tf_op jit(solution)/shard_map/ppermute | solution.py:404
  7.4 1.5 %collective-permute-start.2 = (bf16[256,256]{1,0:T(8,128)(2,1)S(1)}, bf16[256,256]{1,0:T(8,128)(2,1)S(1)}, u32[]{:S(2)}, u32[]{:S(2)}) collective-permute-start(bf16[256,256]{1,0:T(8,128)(2,1)S(1)} %get-tuple-element.51), channel_id=1, source_target_pairs={{16,0},{0,16},{17,1},{1,17},{18,2},{2,18},{19,3},{3,19},{20,4},{4,... | collective-permute-start | bytes 393224 | tf_op jit(solution)/shard_map/ppermute | solution.py:404
  8.9 1.2 %collective-permute-start = (bf16[512,256]{1,0:T(8,128)(2,1)S(1)}, bf16[512,256]{1,0:T(8,128)(2,1)S(1)}, u32[]{:S(2)}, u32[]{:S(2)}) collective-permute-start(bf16[512,256]{1,0:T(8,128)(2,1)S(1)} %shard_map.88), channel_id=1, source_target_pairs={{16,0},{0,16},{17,1},{1,17},{18,2},{2,18},{19,3},{3,19},{20,4},{4,... | collective-permute-start | bytes 786440 | tf_op jit(solution)/shard_map/ppermute | solution.py:404
  10.2 1.5 %shard_map.87 = (bf16[512,512]{1,0:T(8,128)(2,1)S(1)}, f32[256,512]{1,0:T(8,128)S(1)}, f32[256,512]{1,0:T(8,128)S(1)}) custom-call(bf16[256,128]{1,0:T(8,128)(2,1)S(1)} %get-tuple-element.38.shift, bf16[512,512]{1,0:T(8,128)(2,1)S(1)} %get-tuple-element.40.mixed, bf16[3,512,512]{2,1,0:T(8,128)(2,1)S(1)} %get-tuple-element.41.weight, ...), custom_call_target="tpu_custom_call" | custom-call | flops 89478488 | bytes 4784128 | tf_op jit(solution)/shard_map/pallas_call | solution.py:25
  11.6 0.1 collective-permute-done.1.rest_2_
  11.7 2.8 %collective-permute-done.2.rest_3_ = bf16[256,256]{1,0:T(8,128)(2,1)S(1)} collective-permute-done((bf16[256,256]{1,0:T(8,128)(2,1)S(1)}, bf16[256,256]{1,0:T(8,128)(2,1)S(1)}, u32[]{:S(2)}, u32[]{:S(2)}) %collective-permute-start.2) | collective-permute-done | bytes 131104 | tf_op jit(solution)/shard_map/ppermute | solution.py:404
  14.5 0.8 %shard_map.89 = (bf16[512,256]{1,0:T(8,128)(2,1)S(1)}, bf16[512,768]{1,0:T(8,128)(2,1)S(1)}, bf16[256,768]{1,0:T(8,128)(2,1)S(1)}, bf16[256,768]{1,0:T(8,128)(2,1)S(1)}) custom-call(bf16[256,128]{1,0:T(8,128)(2,1)S(1)} %get-tuple-element.38.shift, bf16[4,128,512]{2,1,0:T(8,128)(2,1)S(1)} %get-tuple-element.39.top, ...), custom_call_target="tpu_custom_call" | custom-call | flops 402653184 | bytes 4259840 | tf_op jit(solution)/shard_map/pallas_call | solution.py:25
  15.3 0.1 collective-permute-start.3
  15.4 0.6 %shard_map.90.rest_4_ = f32[512,512]{1,0:T(8,128)S(1)} custom-call(bf16[512,768]{1,0:T(8,128)(2,1)S(1)} %get-tuple-element.53.taps, bf16[3,512,512]{2,1,0:T(8,128)(2,1)S(1)} %get-tuple-element.41.weight), custom_call_target="tpu_custom_call" | custom-call | flops 99999997952 | bytes 3407872 | tf_op jit(solution)/shard_map/pallas_call | solution.py:25
  16.0 1.1 %collective-permute-done.3.refs_1_ = bf16[256,768]{1,0:T(8,128)(2,1)S(1)} collective-permute-done((bf16[256,768]{1,0:T(8,128)(2,1)S(1)}, bf16[256,768]{1,0:T(8,128)(2,1)S(1)}, u32[]{:S(2)}, u32[]{:S(2)}) %collective-permute-start.3) | collective-permute-done | bytes 393248 | tf_op jit(solution)/shard_map/ppermute | solution.py:338
  17.1 0.1 shard_map.92
  17.2 1.6 %collective-permute-start.4 = (bf16[128,768]{1,0:T(8,128)(2,1)S(1)}, bf16[128,768]{1,0:T(8,128)(2,1)S(1)}, u32[]{:S(2)}, u32[]{:S(2)}) collective-permute-start(bf16[128,768]{1,0:T(8,128)(2,1)S(1)} %get-tuple-element.58), channel_id=1, source_target_pairs={{0,2},{1,5},{2,0},{3,7},{4,6},{5,1},{6,4},{7,3},{8,10},{9,13},{10,... | collective-permute-start | bytes 589832 | tf_op jit(solution)/shard_map/ppermute | solution.py:338
  18.8 0.5 collective-permute-done.rest_2_
  19.3 1.6 %shard_map.91 = (bf16[256,896]{1,0:T(8,128)(2,1)S(1)}, bf16[256,896]{1,0:T(8,128)(2,1)S(1)}, bf16[4,128,512]{2,1,0:T(8,128)(2,1)}) custom-call(bf16[256,128]{1,0:T(8,128)(2,1)S(1)} %get-tuple-element.38.shift, bf16[4,128,512]{2,1,0:T(8,128)(2,1)S(1)} %get-tuple-element.39.top, bf16[512,512]{1,0:T(8,128)(2,1)S(1)} %get-tuple-element.44.h_t, ...), custom_call_target="tpu_custom_call" | custom-call | flops 99999997952 | bytes 6815744 | tf_op jit(solution)/shard_map/pallas_call | solution.py:25
  20.9 2.0 %collective-permute-done.4.refs_1_ = bf16[128,768]{1,0:T(8,128)(2,1)S(1)} collective-permute-done((bf16[128,768]{1,0:T(8,128)(2,1)S(1)}, bf16[128,768]{1,0:T(8,128)(2,1)S(1)}, u32[]{:S(2)}, u32[]{:S(2)}) %collective-permute-start.4) | collective-permute-done | bytes 196640 | tf_op jit(solution)/shard_map/ppermute | solution.py:338
  22.9 0.0 collective-permute-start.9
  23.0 1.6 %collective-permute-start.5 = (bf16[64,768]{1,0:T(8,128)(2,1)S(1)}, bf16[64,768]{1,0:T(8,128)(2,1)S(1)}, u32[]{:S(2)}, u32[]{:S(2)}) collective-permute-start(bf16[64,768]{1,0:T(8,128)(2,1)S(1)} %get-tuple-element.60), channel_id=1, source_target_pairs={{0,4},{1,3},{2,6},{3,1},{4,0},{5,7},{6,2},{7,5},{8,12},{9,11},{10,... | collective-permute-start | bytes 294920 | tf_op jit(solution)/shard_map/ppermute | solution.py:338
  24.6 0.1 collective-permute-done.9.refs_1_
  24.8 0.1 shard_map.94
  24.9 1.6 %collective-permute-start.10 = (bf16[128,896]{1,0:T(8,128)(2,1)S(1)}, bf16[128,896]{1,0:T(8,128)(2,1)S(1)}, u32[]{:S(2)}, u32[]{:S(2)}) collective-permute-start(bf16[128,896]{1,0:T(8,128)(2,1)S(1)} %get-tuple-element.65), channel_id=1, source_target_pairs={{0,2},{1,5},{2,0},{3,7},{4,6},{5,1},{6,4},{7,3},{8,10},{9,13},{10,... | collective-permute-start | bytes 688136 | tf_op jit(solution)/shard_map/ppermute | solution.py:338
  26.5 1.2 %collective-permute-done.5 = bf16[64,768]{1,0:T(8,128)(2,1)S(1)} collective-permute-done((bf16[64,768]{1,0:T(8,128)(2,1)S(1)}, bf16[64,768]{1,0:T(8,128)(2,1)S(1)}, u32[]{:S(2)}, u32[]{:S(2)}) %collective-permute-start.5) | collective-permute-done | bytes 98336 | tf_op jit(solution)/shard_map/ppermute | solution.py:338
  27.7 2.7 %collective-permute-start.6 = (bf16[64,768]{1,0:T(8,128)(2,1)S(1)}, bf16[64,768]{1,0:T(8,128)(2,1)S(1)}, u32[]{:S(2)}, u32[]{:S(2)}) collective-permute-start(bf16[64,768]{1,0:T(8,128)(2,1)S(1)} %add_convert_fusion.3), channel_id=1, source_target_pairs={{0,8},{1,9},{2,10},{3,11},{4,12},{5,13},{6,14},{7,15},{8,0},{9,1},... | collective-permute-start | bytes 294920 | tf_op jit(solution)/shard_map/ppermute | solution.py:338
  30.4 0.6 %collective-permute-done.10.refs_1_ = bf16[128,896]{1,0:T(8,128)(2,1)S(1)} collective-permute-done((bf16[128,896]{1,0:T(8,128)(2,1)S(1)}, bf16[128,896]{1,0:T(8,128)(2,1)S(1)}, u32[]{:S(2)}, u32[]{:S(2)}) %collective-permute-start.10) | collective-permute-done | bytes 229408 | tf_op jit(solution)/shard_map/ppermute | solution.py:338
  31.0 0.1 shard_map.95
  31.0 1.6 %collective-permute-start.11 = (bf16[64,896]{1,0:T(8,128)(2,1)S(1)}, bf16[64,896]{1,0:T(8,128)(2,1)S(1)}, u32[]{:S(2)}, u32[]{:S(2)}) collective-permute-start(bf16[64,896]{1,0:T(8,128)(2,1)S(1)} %get-tuple-element.67), channel_id=1, source_target_pairs={{0,4},{1,3},{2,6},{3,1},{4,0},{5,7},{6,2},{7,5},{8,12},{9,11},{10,... | collective-permute-start | bytes 344072 | tf_op jit(solution)/shard_map/ppermute | solution.py:338
  32.7 2.7 %collective-permute-done.6 = bf16[64,768]{1,0:T(8,128)(2,1)S(1)} collective-permute-done((bf16[64,768]{1,0:T(8,128)(2,1)S(1)}, bf16[64,768]{1,0:T(8,128)(2,1)S(1)}, u32[]{:S(2)}, u32[]{:S(2)}) %collective-permute-start.6) | collective-permute-done | bytes 98336 | tf_op jit(solution)/shard_map/ppermute | solution.py:338
  35.4 0.5 collective-permute-start.7
  35.9 0.7 %collective-permute-done.11 = bf16[64,896]{1,0:T(8,128)(2,1)S(1)} collective-permute-done((bf16[64,896]{1,0:T(8,128)(2,1)S(1)}, bf16[64,896]{1,0:T(8,128)(2,1)S(1)}, u32[]{:S(2)}, u32[]{:S(2)}) %collective-permute-start.11) | collective-permute-done | bytes 114720 | tf_op jit(solution)/shard_map/ppermute | solution.py:338
  36.6 2.8 %collective-permute-start.12 = (bf16[64,896]{1,0:T(8,128)(2,1)S(1)}, bf16[64,896]{1,0:T(8,128)(2,1)S(1)}, u32[]{:S(2)}, u32[]{:S(2)}) collective-permute-start(bf16[64,896]{1,0:T(8,128)(2,1)S(1)} %add_convert_fusion.1), channel_id=1, source_target_pairs={{0,8},{1,9},{2,10},{3,11},{4,12},{5,13},{6,14},{7,15},{8,0},{9,1},... | collective-permute-start | bytes 344072 | tf_op jit(solution)/shard_map/ppermute | solution.py:338
  39.4 0.8 %collective-permute-done.7.refs_1_ = bf16[64,768]{1,0:T(8,128)(2,1)S(1)} collective-permute-done((bf16[64,768]{1,0:T(8,128)(2,1)S(1)}, bf16[64,768]{1,0:T(8,128)(2,1)S(1)}, u32[]{:S(2)}, u32[]{:S(2)}) %collective-permute-start.7) | collective-permute-done | bytes 98336 | tf_op jit(solution)/shard_map/ppermute | solution.py:338
  40.2 1.6 %collective-permute-start.8 = (bf16[128,768]{1,0:T(8,128)(2,1)S(1)}, bf16[128,768]{1,0:T(8,128)(2,1)S(1)}, u32[]{:S(2)}, u32[]{:S(2)}) collective-permute-start(bf16[128,768]{1,0:T(8,128)(2,1)S(1)} %pad_maximum_fusion), channel_id=1, source_target_pairs={{0,2},{1,5},{2,0},{3,7},{4,6},{5,1},{6,4},{7,3},{8,10},{9,13},{10,... | collective-permute-start | bytes 589832 | tf_op jit(solution)/shard_map/ppermute | solution.py:338
  41.8 2.8 %collective-permute-done.12 = bf16[64,896]{1,0:T(8,128)(2,1)S(1)} collective-permute-done((bf16[64,896]{1,0:T(8,128)(2,1)S(1)}, bf16[64,896]{1,0:T(8,128)(2,1)S(1)}, u32[]{:S(2)}, u32[]{:S(2)}) %collective-permute-start.12) | collective-permute-done | bytes 114720 | tf_op jit(solution)/shard_map/ppermute | solution.py:338
  44.6 0.5 collective-permute-start.15
  45.1 1.9 %collective-permute-start.14 = (bf16[64,896]{1,0:T(8,128)(2,1)S(1)}, bf16[64,896]{1,0:T(8,128)(2,1)S(1)}, u32[]{:S(2)}, u32[]{:S(2)}) collective-permute-start(bf16[64,896]{1,0:T(8,128)(2,1)S(1)} %add_convert_fusion.refs_4_), channel_id=1, source_target_pairs={{0,4},{1,5},{2,6},{3,7},{4,0},{5,1},{6,2},{7,3},{8,12},{9,13},{10,... | collective-permute-start | bytes 344072 | tf_op jit(solution)/shard_map/ppermute | solution.py:338
  47.0 1.1 %collective-permute-start.13 = (bf16[64,896]{1,0:T(8,128)(2,1)S(1)}, bf16[64,896]{1,0:T(8,128)(2,1)S(1)}, u32[]{:S(2)}, u32[]{:S(2)}) collective-permute-start(bf16[64,896]{1,0:T(8,128)(2,1)S(1)} %add_convert_fusion.refs_4_), channel_id=1, source_target_pairs={{0,2},{1,3},{2,0},{3,1},{4,6},{5,7},{6,4},{7,5},{8,10},{9,11},{10,... | collective-permute-start | bytes 344072 | tf_op jit(solution)/shard_map/ppermute | solution.py:338
  48.2 0.0 collective-permute-done.8.refs_2_
  48.2 2.2 %collective-permute-done.15.refs_7_ = bf16[64,896]{1,0:T(8,128)(2,1)S(1)} collective-permute-done((bf16[64,896]{1,0:T(8,128)(2,1)S(1)}, bf16[64,896]{1,0:T(8,128)(2,1)S(1)}, u32[]{:S(2)}, u32[]{:S(2)}) %collective-permute-start.15) | collective-permute-done | bytes 114720 | tf_op jit(solution)/shard_map/ppermute | solution.py:338
  50.4 0.7 %collective-permute-done.14.refs_6_ = bf16[64,896]{1,0:T(8,128)(2,1)S(1)} collective-permute-done((bf16[64,896]{1,0:T(8,128)(2,1)S(1)}, bf16[64,896]{1,0:T(8,128)(2,1)S(1)}, u32[]{:S(2)}, u32[]{:S(2)}) %collective-permute-start.14) | collective-permute-done | bytes 114720 | tf_op jit(solution)/shard_map/ppermute | solution.py:338
  51.0 0.8 %collective-permute-done.13.refs_5_ = bf16[64,896]{1,0:T(8,128)(2,1)S(1)} collective-permute-done((bf16[64,896]{1,0:T(8,128)(2,1)S(1)}, bf16[64,896]{1,0:T(8,128)(2,1)S(1)}, u32[]{:S(2)}, u32[]{:S(2)}) %collective-permute-start.13) | collective-permute-done | bytes 114720 | tf_op jit(solution)/shard_map/ppermute | solution.py:338
  51.8 0.1 maximum_maximum_fusion
  51.9 0.1 collective-permute-start.16
  52.0 2.4 %collective-permute-done.16.refs_3_.refs_8_ = bf16[256,1664]{1,0:T(8,128)(2,1)S(1)} collective-permute-done((bf16[256,1664]{1,0:T(8,128)(2,1)S(1)}, bf16[256,1664]{1,0:T(8,128)(2,1)S(1)}, u32[]{:S(2)}, u32[]{:S(2)}) %collective-permute-start.16) | collective-permute-done | bytes 852000 | tf_op jit(solution)/shard_map/ppermute | solution.py:338
  54.4 1.3 %shard_map.96 = (bf16[3,512,512]{2,1,0:T(8,128)(2,1)}, bf16[50,512]{1,0:T(8,128)(2,1)}) custom-call(bf16[64,768]{1,0:T(8,128)(2,1)S(1)} %add_convert_fusion.2.refs_0_, bf16[64,768]{1,0:T(8,128)(2,1)S(1)} %collective-permute-done.7.refs_1_, bf16[128,768]{1,0:T(8,128)(2,1)S(1)} %collective-permute-done.8.refs_2_, ...), custom_call_target="tpu_custom_call" | custom-call | bytes 4179968 | tf_op jit(solution)/shard_map/pallas_call | solution.py:25
  (8 shorter events, 0.2 us)
Async XLA Ops:
  3.1 8.6 %collective-permute-start.1 = (bf16[256,256]{1,0:T(8,128)(2,1)S(1)}, bf16[256,256]{1,0:T(8,128)(2,1)S(1)}, u32[]{:S(2)}, u32[]{:S(2)}) collective-permute-start(bf16[256,256]{1,0:T(8,128)(2,1)S(1)} %get-tuple-element.50), channel_id=1, source_target_pairs={{16,0},{0,16},{17,1},{1,17},{18,2},{2,18},{19,3},{3,19},{20,4},{4,... | collective-permute-start | bytes 393224 | tf_op jit(solution)/shard_map/ppermute | solution.py:404
  7.4 7.1 %collective-permute-start.2 = (bf16[256,256]{1,0:T(8,128)(2,1)S(1)}, bf16[256,256]{1,0:T(8,128)(2,1)S(1)}, u32[]{:S(2)}, u32[]{:S(2)}) collective-permute-start(bf16[256,256]{1,0:T(8,128)(2,1)S(1)} %get-tuple-element.51), channel_id=1, source_target_pairs={{16,0},{0,16},{17,1},{1,17},{18,2},{2,18},{19,3},{3,19},{20,4},{4,... | collective-permute-start | bytes 393224 | tf_op jit(solution)/shard_map/ppermute | solution.py:404
  8.9 10.4 %collective-permute-start = (bf16[512,256]{1,0:T(8,128)(2,1)S(1)}, bf16[512,256]{1,0:T(8,128)(2,1)S(1)}, u32[]{:S(2)}, u32[]{:S(2)}) collective-permute-start(bf16[512,256]{1,0:T(8,128)(2,1)S(1)} %shard_map.88), channel_id=1, source_target_pairs={{16,0},{0,16},{17,1},{1,17},{18,2},{2,18},{19,3},{3,19},{20,4},{4,... | collective-permute-start | bytes 786440 | tf_op jit(solution)/shard_map/ppermute | solution.py:404
  15.3 1.8 %collective-permute-start.3 = (bf16[256,768]{1,0:T(8,128)(2,1)S(1)}, bf16[256,768]{1,0:T(8,128)(2,1)S(1)}, u32[]{:S(2)}, u32[]{:S(2)}) collective-permute-start(bf16[256,768]{1,0:T(8,128)(2,1)S(1)} %get-tuple-element.56), channel_id=1, source_target_pairs={{0,1},{1,0},{2,3},{3,2},{4,5},{5,4},{6,7},{7,6},{8,9},{9,8},{10,11... | collective-permute-start | bytes 1179656 | tf_op jit(solution)/shard_map/ppermute | solution.py:338
  17.2 5.7 %collective-permute-start.4 = (bf16[128,768]{1,0:T(8,128)(2,1)S(1)}, bf16[128,768]{1,0:T(8,128)(2,1)S(1)}, u32[]{:S(2)}, u32[]{:S(2)}) collective-permute-start(bf16[128,768]{1,0:T(8,128)(2,1)S(1)} %get-tuple-element.58), channel_id=1, source_target_pairs={{0,2},{1,5},{2,0},{3,7},{4,6},{5,1},{6,4},{7,3},{8,10},{9,13},{10,... | collective-permute-start | bytes 589832 | tf_op jit(solution)/shard_map/ppermute | solution.py:338
  22.9 1.8 %collective-permute-start.9 = (bf16[256,896]{1,0:T(8,128)(2,1)S(1)}, bf16[256,896]{1,0:T(8,128)(2,1)S(1)}, u32[]{:S(2)}, u32[]{:S(2)}) collective-permute-start(bf16[256,896]{1,0:T(8,128)(2,1)S(1)} %get-tuple-element.63), channel_id=1, source_target_pairs={{0,1},{1,0},{2,3},{3,2},{4,5},{5,4},{6,7},{7,6},{8,9},{9,8},{10,11... | collective-permute-start | bytes 1376264 | tf_op jit(solution)/shard_map/ppermute | solution.py:338
  23.0 4.7 %collective-permute-start.5 = (bf16[64,768]{1,0:T(8,128)(2,1)S(1)}, bf16[64,768]{1,0:T(8,128)(2,1)S(1)}, u32[]{:S(2)}, u32[]{:S(2)}) collective-permute-start(bf16[64,768]{1,0:T(8,128)(2,1)S(1)} %get-tuple-element.60), channel_id=1, source_target_pairs={{0,4},{1,3},{2,6},{3,1},{4,0},{5,7},{6,2},{7,5},{8,12},{9,11},{10,... | collective-permute-start | bytes 294920 | tf_op jit(solution)/shard_map/ppermute | solution.py:338
  24.9 6.1 %collective-permute-start.10 = (bf16[128,896]{1,0:T(8,128)(2,1)S(1)}, bf16[128,896]{1,0:T(8,128)(2,1)S(1)}, u32[]{:S(2)}, u32[]{:S(2)}) collective-permute-start(bf16[128,896]{1,0:T(8,128)(2,1)S(1)} %get-tuple-element.65), channel_id=1, source_target_pairs={{0,2},{1,5},{2,0},{3,7},{4,6},{5,1},{6,4},{7,3},{8,10},{9,13},{10,... | collective-permute-start | bytes 688136 | tf_op jit(solution)/shard_map/ppermute | solution.py:338
  27.7 7.7 %collective-permute-start.6 = (bf16[64,768]{1,0:T(8,128)(2,1)S(1)}, bf16[64,768]{1,0:T(8,128)(2,1)S(1)}, u32[]{:S(2)}, u32[]{:S(2)}) collective-permute-start(bf16[64,768]{1,0:T(8,128)(2,1)S(1)} %add_convert_fusion.3), channel_id=1, source_target_pairs={{0,8},{1,9},{2,10},{3,11},{4,12},{5,13},{6,14},{7,15},{8,0},{9,1},... | collective-permute-start | bytes 294920 | tf_op jit(solution)/shard_map/ppermute | solution.py:338
  31.0 5.5 %collective-permute-start.11 = (bf16[64,896]{1,0:T(8,128)(2,1)S(1)}, bf16[64,896]{1,0:T(8,128)(2,1)S(1)}, u32[]{:S(2)}, u32[]{:S(2)}) collective-permute-start(bf16[64,896]{1,0:T(8,128)(2,1)S(1)} %get-tuple-element.67), channel_id=1, source_target_pairs={{0,4},{1,3},{2,6},{3,1},{4,0},{5,7},{6,2},{7,5},{8,12},{9,11},{10,... | collective-permute-start | bytes 344072 | tf_op jit(solution)/shard_map/ppermute | solution.py:338
  35.4 4.8 %collective-permute-start.7 = (bf16[64,768]{1,0:T(8,128)(2,1)S(1)}, bf16[64,768]{1,0:T(8,128)(2,1)S(1)}, u32[]{:S(2)}, u32[]{:S(2)}) collective-permute-start(bf16[64,768]{1,0:T(8,128)(2,1)S(1)} %add_convert_fusion.2.refs_0_), channel_id=1, source_target_pairs={{0,4},{1,3},{2,6},{3,1},{4,0},{5,7},{6,2},{7,5},{8,12},{9,11},{10,... | collective-permute-start | bytes 294920 | tf_op jit(solution)/shard_map/ppermute | solution.py:338
  36.6 8.0 %collective-permute-start.12 = (bf16[64,896]{1,0:T(8,128)(2,1)S(1)}, bf16[64,896]{1,0:T(8,128)(2,1)S(1)}, u32[]{:S(2)}, u32[]{:S(2)}) collective-permute-start(bf16[64,896]{1,0:T(8,128)(2,1)S(1)} %add_convert_fusion.1), channel_id=1, source_target_pairs={{0,8},{1,9},{2,10},{3,11},{4,12},{5,13},{6,14},{7,15},{8,0},{9,1},... | collective-permute-start | bytes 344072 | tf_op jit(solution)/shard_map/ppermute | solution.py:338
  40.2 8.0 %collective-permute-start.8 = (bf16[128,768]{1,0:T(8,128)(2,1)S(1)}, bf16[128,768]{1,0:T(8,128)(2,1)S(1)}, u32[]{:S(2)}, u32[]{:S(2)}) collective-permute-start(bf16[128,768]{1,0:T(8,128)(2,1)S(1)} %pad_maximum_fusion), channel_id=1, source_target_pairs={{0,2},{1,5},{2,0},{3,7},{4,6},{5,1},{6,4},{7,3},{8,10},{9,13},{10,... | collective-permute-start | bytes 589832 | tf_op jit(solution)/shard_map/ppermute | solution.py:338
  44.6 5.8 %collective-permute-start.15 = (bf16[64,896]{1,0:T(8,128)(2,1)S(1)}, bf16[64,896]{1,0:T(8,128)(2,1)S(1)}, u32[]{:S(2)}, u32[]{:S(2)}) collective-permute-start(bf16[64,896]{1,0:T(8,128)(2,1)S(1)} %add_convert_fusion.refs_4_), channel_id=1, source_target_pairs={{0,6},{1,7},{2,4},{3,5},{4,2},{5,3},{6,0},{7,1},{8,14},{9,15},{10,... | collective-permute-start | bytes 344072 | tf_op jit(solution)/shard_map/ppermute | solution.py:338
  45.1 5.9 %collective-permute-start.14 = (bf16[64,896]{1,0:T(8,128)(2,1)S(1)}, bf16[64,896]{1,0:T(8,128)(2,1)S(1)}, u32[]{:S(2)}, u32[]{:S(2)}) collective-permute-start(bf16[64,896]{1,0:T(8,128)(2,1)S(1)} %add_convert_fusion.refs_4_), channel_id=1, source_target_pairs={{0,4},{1,5},{2,6},{3,7},{4,0},{5,1},{6,2},{7,3},{8,12},{9,13},{10,... | collective-permute-start | bytes 344072 | tf_op jit(solution)/shard_map/ppermute | solution.py:338
  47.0 4.8 %collective-permute-start.13 = (bf16[64,896]{1,0:T(8,128)(2,1)S(1)}, bf16[64,896]{1,0:T(8,128)(2,1)S(1)}, u32[]{:S(2)}, u32[]{:S(2)}) collective-permute-start(bf16[64,896]{1,0:T(8,128)(2,1)S(1)} %add_convert_fusion.refs_4_), channel_id=1, source_target_pairs={{0,2},{1,3},{2,0},{3,1},{4,6},{5,7},{6,4},{7,5},{8,10},{9,11},{10,... | collective-permute-start | bytes 344072 | tf_op jit(solution)/shard_map/ppermute | solution.py:338
  51.9 2.4 %collective-permute-start.16 = (bf16[256,1664]{1,0:T(8,128)(2,1)S(1)}, bf16[256,1664]{1,0:T(8,128)(2,1)S(1)}, u32[]{:S(2)}, u32[]{:S(2)}) collective-permute-start(bf16[256,1664]{1,0:T(8,128)(2,1)S(1)} %maximum_maximum_fusion), channel_id=1, source_target_pairs={{0,1},{1,0},{2,3},{3,2},{4,5},{5,4},{6,7},{7,6},{8,9},{9,8},{10,11... | collective-permute-start | bytes 2555912 | tf_op jit(solution)/shard_map/ppermute | solution.py:338

commit v9 on v8

--- a/solution.py
+++ b/solution.py
@@ -247,15 +247,25 @@
         ref[:, 0:cols] = (prod * scale).astype(BF16)
 
 
+def weight_half(h_t, taps, scale, part, out):
+    half = out.shape[0]
+    left = h_t[pl.ds(pl.multiple_of(part * half, half), half), :]
+    out[...] = (jnp.dot(left, taps[...], preferred_element_type=F32) * scale).astype(BF16)
+
+
+def keep_kernel(scale, h_t, taps, keep):
+    weight_half(h_t, taps, scale, dp_bit(0), keep)
+
+
 def weight_kernel(col, scale, shift, top, h_t, *rest):
-    slope, recv, out = rest[:PARTS], rest[PARTS:-4], rest[-4:]
-    g_used, taps, keep, send = out
+    slope, recv, out = rest[:PARTS], rest[PARTS:-3], rest[-3:]
+    g_used, taps, send = out
     width = g_used.shape[1]
     g = upstream(col, top, recv)
     g_used[...] = g.astype(BF16)
     delta = delta_of(g, slope, col)
     put_taps(delta, taps, shift, -1)
-    weight_blocks(h_t, taps, scale, keep, send, 3 * width)
+    weight_half(h_t, taps, scale, 1 - dp_bit(0), send)
 
 
 def back_kernel(col, taps, weight, acc):
@@ -455,13 +465,20 @@
             got[n], _ = lax.optimization_barrier((got[n], ahead))
         recv = tuple(slope) + tuple(got[n])
         if n < len(sent) - 1:
-            g_now, taps_now, *blocks = call(
+            g_now, taps_now, send = call(
                 functools.partial(weight_kernel, col, scale),
                 [like((rows, width), BF16), like((rows, 3 * width), BF16)]
-                + [like((chans // 2, 3 * width), BF16)] * 2,
+                + [like((chans // 2, 3 * width), BF16)],
                 (shift, top, h_t) + recv,
                     flops=unit * width // chans,
             )
+            keep = call(
+                functools.partial(keep_kernel, scale),
+                [like((chans // 2, 3 * width), BF16)],
+                (h_t, taps_now),
+                flops=unit * width // chans // 2,
+            )[0]
+            blocks = [keep, send]
             acc = call(
                 functools.partial(back_kernel, col),
                 [like((rows, chans), F32)],

time: 55.8 us -> 55.7 us (level)
    pallas_call x12 -> x13, Pallas kernels: 7.94 us -> 8.21 us  [call(): pl.pallas_call(kernel, out_shape=out_shape, in_specs=specs, out_specs=[VM...]
where the time goes in v9:
time: 55.7 us; the launch traced here: 55.6 us
  starting transfers between devices  24.8 us (45%)
  waiting for transfers between devices  21 us (38%)
  Pallas kernels  8.21 us (15%)
  between operations  1.39 us (2%)
    ppermute x14, starting transfers between devices, swap(): lax.ppermute(value, 'dp', [(i, i ^ masks[i % 2]) for i in range(count)])  17.7 us
    ppermute x14, waiting for transfers between devices, swap(): lax.ppermute(value, 'dp', [(i, i ^ masks[i % 2]) for i in range(count)])  17.5 us
    pallas_call x13, Pallas kernels, call(): pl.pallas_call(kernel, out_shape=out_shape, in_specs=specs, out_specs=[VM...  8.21 us
    ppermute x3, starting transfers between devices, below(): return lax.ppermute(value, 'section', pairs)  7.06 us
    ppermute x3, waiting for transfers between devices, below(): return lax.ppermute(value, 'section', pairs)  3.47 us
  transfers between devices with their start and end apart: 17, of which 16 were waited for; matrix products, arithmetic and copies ran while one was open for 0% of the time, Pallas kernels for 9%

profile of v9, /device:TPU:0, one launch (start us, length us, event | category | flops | bytes accessed | tf_op | source)
XLA Modules:
  0.0 55.6 jit_solution(18193393167765242741)
XLA Ops:
  1.3 1.8 %shard_map.85 = (bf16[512,512]{1,0:T(8,128)(2,1)S(1)}, bf16[3,512,512]{2,1,0:T(8,128)(2,1)S(1)}, bf16[4,128,512]{2,1,0:T(8,128)(2,1)S(1)}, f32[128,128]{1,0:T(8,...) custom-call(s32[1]{0:T(128)S(6)} %copy.9.dil, ...), custom_call_target="tpu_custom_call" | custom-call | flops 805306368 | bytes 6866964 | tf_op jit(solution)/shard_map/pallas_call | solution.py:25
  3.1 4.3 %collective-permute-start.1 = (bf16[256,256]{1,0:T(8,128)(2,1)S(1)}, bf16[256,256]{1,0:T(8,128)(2,1)S(1)}, u32[]{:S(2)}, u32[]{:S(2)}) collective-permute-start(bf16[256,256]{1,0:T(8,128)(2,1)S(1)} %get-tuple-element.49), channel_id=1, source_target_pairs={{16,0},{0,16},{17,1},{1,17},{18,2},{2,18},{19,3},{3,19},{20,4},{4,... | collective-permute-start | bytes 393224 | tf_op jit(solution)/shard_map/ppermute | solution.py:414
  7.4 1.5 %collective-permute-start.2 = (bf16[256,256]{1,0:T(8,128)(2,1)S(1)}, bf16[256,256]{1,0:T(8,128)(2,1)S(1)}, u32[]{:S(2)}, u32[]{:S(2)}) collective-permute-start(bf16[256,256]{1,0:T(8,128)(2,1)S(1)} %get-tuple-element.50), channel_id=1, source_target_pairs={{16,0},{0,16},{17,1},{1,17},{18,2},{2,18},{19,3},{3,19},{20,4},{4,... | collective-permute-start | bytes 393224 | tf_op jit(solution)/shard_map/ppermute | solution.py:414
  8.9 1.2 %collective-permute-start = (bf16[512,256]{1,0:T(8,128)(2,1)S(1)}, bf16[512,256]{1,0:T(8,128)(2,1)S(1)}, u32[]{:S(2)}, u32[]{:S(2)}) collective-permute-start(bf16[512,256]{1,0:T(8,128)(2,1)S(1)} %shard_map.88), channel_id=1, source_target_pairs={{16,0},{0,16},{17,1},{1,17},{18,2},{2,18},{19,3},{3,19},{20,4},{4,... | collective-permute-start | bytes 786440 | tf_op jit(solution)/shard_map/ppermute | solution.py:414
  10.2 1.5 %shard_map.87 = (bf16[512,512]{1,0:T(8,128)(2,1)S(1)}, f32[256,512]{1,0:T(8,128)S(1)}, f32[256,512]{1,0:T(8,128)S(1)}) custom-call(bf16[256,128]{1,0:T(8,128)(2,1)S(1)} %get-tuple-element.37.shift, bf16[512,512]{1,0:T(8,128)(2,1)S(1)} %get-tuple-element.39.mixed, bf16[3,512,512]{2,1,0:T(8,128)(2,1)S(1)} %get-tuple-element.40.weight, ...), custom_call_target="tpu_custom_call" | custom-call | flops 89478488 | bytes 4784128 | tf_op jit(solution)/shard_map/pallas_call | solution.py:25
  11.6 0.1 collective-permute-done.1.rest_2_
  11.7 2.8 %collective-permute-done.2.rest_3_ = bf16[256,256]{1,0:T(8,128)(2,1)S(1)} collective-permute-done((bf16[256,256]{1,0:T(8,128)(2,1)S(1)}, bf16[256,256]{1,0:T(8,128)(2,1)S(1)}, u32[]{:S(2)}, u32[]{:S(2)}) %collective-permute-start.2) | collective-permute-done | bytes 131104 | tf_op jit(solution)/shard_map/ppermute | solution.py:414
  14.5 0.7 %shard_map.89 = (bf16[512,256]{1,0:T(8,128)(2,1)S(1)}, bf16[512,768]{1,0:T(8,128)(2,1)S(1)}, bf16[256,768]{1,0:T(8,128)(2,1)S(1)}) custom-call(bf16[256,128]{1,0:T(8,128)(2,1)S(1)} %get-tuple-element.37.shift, bf16[4,128,512]{2,1,0:T(8,128)(2,1)S(1)} %get-tuple-element.38.top, bf16[512,512]{1,0:T(8,128)(2,1)S(1)} %get-tuple-element.43.h_t, ...), custom_call_target="tpu_custom_call" | custom-call | flops 402653184 | bytes 3866624 | tf_op jit(solution)/shard_map/pallas_call | solution.py:25
  15.2 0.1 collective-permute-start.3
  15.3 0.6 %shard_map.90.rest_4_ = f32[512,512]{1,0:T(8,128)S(1)} custom-call(bf16[512,768]{1,0:T(8,128)(2,1)S(1)} %get-tuple-element.52.taps, bf16[3,512,512]{2,1,0:T(8,128)(2,1)S(1)} %get-tuple-element.40.weight), custom_call_target="tpu_custom_call" | custom-call | flops 99999997952 | bytes 3407872 | tf_op jit(solution)/shard_map/pallas_call | solution.py:25
  15.9 0.4 shard_map.92.refs_0_
  16.3 0.7 %collective-permute-done.3.refs_1_ = bf16[256,768]{1,0:T(8,128)(2,1)S(1)} collective-permute-done((bf16[256,768]{1,0:T(8,128)(2,1)S(1)}, bf16[256,768]{1,0:T(8,128)(2,1)S(1)}, u32[]{:S(2)}, u32[]{:S(2)}) %collective-permute-start.3) | collective-permute-done | bytes 393248 | tf_op jit(solution)/shard_map/ppermute | solution.py:348
  17.0 0.1 shard_map.93
  17.1 1.6 %collective-permute-start.4 = (bf16[128,768]{1,0:T(8,128)(2,1)S(1)}, bf16[128,768]{1,0:T(8,128)(2,1)S(1)}, u32[]{:S(2)}, u32[]{:S(2)}) collective-permute-start(bf16[128,768]{1,0:T(8,128)(2,1)S(1)} %get-tuple-element.56), channel_id=1, source_target_pairs={{0,2},{1,5},{2,0},{3,7},{4,6},{5,1},{6,4},{7,3},{8,10},{9,13},{10,... | collective-permute-start | bytes 589832 | tf_op jit(solution)/shard_map/ppermute | solution.py:348
  18.7 0.6 %collective-permute-done.rest_2_ = bf16[512,256]{1,0:T(8,128)(2,1)S(1)} collective-permute-done((bf16[512,256]{1,0:T(8,128)(2,1)S(1)}, bf16[512,256]{1,0:T(8,128)(2,1)S(1)}, u32[]{:S(2)}, u32[]{:S(2)}) %collective-permute-start) | collective-permute-done | bytes 262176 | tf_op jit(solution)/shard_map/ppermute | solution.py:414
  19.3 1.6 %shard_map.91 = (bf16[256,896]{1,0:T(8,128)(2,1)S(1)}, bf16[256,896]{1,0:T(8,128)(2,1)S(1)}, bf16[4,128,512]{2,1,0:T(8,128)(2,1)}) custom-call(bf16[256,128]{1,0:T(8,128)(2,1)S(1)} %get-tuple-element.37.shift, bf16[4,128,512]{2,1,0:T(8,128)(2,1)S(1)} %get-tuple-element.38.top, bf16[512,512]{1,0:T(8,128)(2,1)S(1)} %get-tuple-element.43.h_t, ...), custom_call_target="tpu_custom_call" | custom-call | flops 99999997952 | bytes 6815744 | tf_op jit(solution)/shard_map/pallas_call | solution.py:25
  20.9 1.9 %collective-permute-done.4.refs_1_ = bf16[128,768]{1,0:T(8,128)(2,1)S(1)} collective-permute-done((bf16[128,768]{1,0:T(8,128)(2,1)S(1)}, bf16[128,768]{1,0:T(8,128)(2,1)S(1)}, u32[]{:S(2)}, u32[]{:S(2)}) %collective-permute-start.4) | collective-permute-done | bytes 196640 | tf_op jit(solution)/shard_map/ppermute | solution.py:348
  22.8 0.0 collective-permute-start.9
  22.9 1.6 %collective-permute-start.5 = (bf16[64,768]{1,0:T(8,128)(2,1)S(1)}, bf16[64,768]{1,0:T(8,128)(2,1)S(1)}, u32[]{:S(2)}, u32[]{:S(2)}) collective-permute-start(bf16[64,768]{1,0:T(8,128)(2,1)S(1)} %get-tuple-element.58), channel_id=1, source_target_pairs={{0,4},{1,3},{2,6},{3,1},{4,0},{5,7},{6,2},{7,5},{8,12},{9,11},{10,... | collective-permute-start | bytes 294920 | tf_op jit(solution)/shard_map/ppermute | solution.py:348
  24.5 0.1 collective-permute-done.9.refs_1_
  24.7 0.1 shard_map.95
  24.8 1.6 %collective-permute-start.10 = (bf16[128,896]{1,0:T(8,128)(2,1)S(1)}, bf16[128,896]{1,0:T(8,128)(2,1)S(1)}, u32[]{:S(2)}, u32[]{:S(2)}) collective-permute-start(bf16[128,896]{1,0:T(8,128)(2,1)S(1)} %get-tuple-element.63), channel_id=1, source_target_pairs={{0,2},{1,5},{2,0},{3,7},{4,6},{5,1},{6,4},{7,3},{8,10},{9,13},{10,... | collective-permute-start | bytes 688136 | tf_op jit(solution)/shard_map/ppermute | solution.py:348
  26.4 1.2 %collective-permute-done.5 = bf16[64,768]{1,0:T(8,128)(2,1)S(1)} collective-permute-done((bf16[64,768]{1,0:T(8,128)(2,1)S(1)}, bf16[64,768]{1,0:T(8,128)(2,1)S(1)}, u32[]{:S(2)}, u32[]{:S(2)}) %collective-permute-start.5) | collective-permute-done | bytes 98336 | tf_op jit(solution)/shard_map/ppermute | solution.py:348
  27.6 2.7 %collective-permute-start.6 = (bf16[64,768]{1,0:T(8,128)(2,1)S(1)}, bf16[64,768]{1,0:T(8,128)(2,1)S(1)}, u32[]{:S(2)}, u32[]{:S(2)}) collective-permute-start(bf16[64,768]{1,0:T(8,128)(2,1)S(1)} %add_convert_fusion.3), channel_id=1, source_target_pairs={{0,8},{1,9},{2,10},{3,11},{4,12},{5,13},{6,14},{7,15},{8,0},{9,1},... | collective-permute-start | bytes 294920 | tf_op jit(solution)/shard_map/ppermute | solution.py:348
  30.3 0.6 %collective-permute-done.10.refs_1_ = bf16[128,896]{1,0:T(8,128)(2,1)S(1)} collective-permute-done((bf16[128,896]{1,0:T(8,128)(2,1)S(1)}, bf16[128,896]{1,0:T(8,128)(2,1)S(1)}, u32[]{:S(2)}, u32[]{:S(2)}) %collective-permute-start.10) | collective-permute-done | bytes 229408 | tf_op jit(solution)/shard_map/ppermute | solution.py:348
  30.9 0.1 shard_map.96
  30.9 1.6 %collective-permute-start.11 = (bf16[64,896]{1,0:T(8,128)(2,1)S(1)}, bf16[64,896]{1,0:T(8,128)(2,1)S(1)}, u32[]{:S(2)}, u32[]{:S(2)}) collective-permute-start(bf16[64,896]{1,0:T(8,128)(2,1)S(1)} %get-tuple-element.65), channel_id=1, source_target_pairs={{0,4},{1,3},{2,6},{3,1},{4,0},{5,7},{6,2},{7,5},{8,12},{9,11},{10,... | collective-permute-start | bytes 344072 | tf_op jit(solution)/shard_map/ppermute | solution.py:348
  32.6 2.7 %collective-permute-done.6 = bf16[64,768]{1,0:T(8,128)(2,1)S(1)} collective-permute-done((bf16[64,768]{1,0:T(8,128)(2,1)S(1)}, bf16[64,768]{1,0:T(8,128)(2,1)S(1)}, u32[]{:S(2)}, u32[]{:S(2)}) %collective-permute-start.6) | collective-permute-done | bytes 98336 | tf_op jit(solution)/shard_map/ppermute | solution.py:348
  35.3 0.5 collective-permute-start.7
  35.8 0.7 %collective-permute-done.11 = bf16[64,896]{1,0:T(8,128)(2,1)S(1)} collective-permute-done((bf16[64,896]{1,0:T(8,128)(2,1)S(1)}, bf16[64,896]{1,0:T(8,128)(2,1)S(1)}, u32[]{:S(2)}, u32[]{:S(2)}) %collective-permute-start.11) | collective-permute-done | bytes 114720 | tf_op jit(solution)/shard_map/ppermute | solution.py:348
  36.5 2.8 %collective-permute-start.12 = (bf16[64,896]{1,0:T(8,128)(2,1)S(1)}, bf16[64,896]{1,0:T(8,128)(2,1)S(1)}, u32[]{:S(2)}, u32[]{:S(2)}) collective-permute-start(bf16[64,896]{1,0:T(8,128)(2,1)S(1)} %add_convert_fusion.1), channel_id=1, source_target_pairs={{0,8},{1,9},{2,10},{3,11},{4,12},{5,13},{6,14},{7,15},{8,0},{9,1},... | collective-permute-start | bytes 344072 | tf_op jit(solution)/shard_map/ppermute | solution.py:348
  39.3 0.8 %collective-permute-done.7.refs_1_ = bf16[64,768]{1,0:T(8,128)(2,1)S(1)} collective-permute-done((bf16[64,768]{1,0:T(8,128)(2,1)S(1)}, bf16[64,768]{1,0:T(8,128)(2,1)S(1)}, u32[]{:S(2)}, u32[]{:S(2)}) %collective-permute-start.7) | collective-permute-done | bytes 98336 | tf_op jit(solution)/shard_map/ppermute | solution.py:348
  40.1 1.6 %collective-permute-start.8 = (bf16[128,768]{1,0:T(8,128)(2,1)S(1)}, bf16[128,768]{1,0:T(8,128)(2,1)S(1)}, u32[]{:S(2)}, u32[]{:S(2)}) collective-permute-start(bf16[128,768]{1,0:T(8,128)(2,1)S(1)} %pad_maximum_fusion), channel_id=1, source_target_pairs={{0,2},{1,5},{2,0},{3,7},{4,6},{5,1},{6,4},{7,3},{8,10},{9,13},{10,... | collective-permute-start | bytes 589832 | tf_op jit(solution)/shard_map/ppermute | solution.py:348
  41.7 2.8 %collective-permute-done.12 = bf16[64,896]{1,0:T(8,128)(2,1)S(1)} collective-permute-done((bf16[64,896]{1,0:T(8,128)(2,1)S(1)}, bf16[64,896]{1,0:T(8,128)(2,1)S(1)}, u32[]{:S(2)}, u32[]{:S(2)}) %collective-permute-start.12) | collective-permute-done | bytes 114720 | tf_op jit(solution)/shard_map/ppermute | solution.py:348
  44.5 0.5 collective-permute-start.15
  45.0 1.9 %collective-permute-start.14 = (bf16[64,896]{1,0:T(8,128)(2,1)S(1)}, bf16[64,896]{1,0:T(8,128)(2,1)S(1)}, u32[]{:S(2)}, u32[]{:S(2)}) collective-permute-start(bf16[64,896]{1,0:T(8,128)(2,1)S(1)} %add_convert_fusion.refs_4_), channel_id=1, source_target_pairs={{0,4},{1,5},{2,6},{3,7},{4,0},{5,1},{6,2},{7,3},{8,12},{9,13},{10,... | collective-permute-start | bytes 344072 | tf_op jit(solution)/shard_map/ppermute | solution.py:348
  46.9 1.1 %collective-permute-start.13 = (bf16[64,896]{1,0:T(8,128)(2,1)S(1)}, bf16[64,896]{1,0:T(8,128)(2,1)S(1)}, u32[]{:S(2)}, u32[]{:S(2)}) collective-permute-start(bf16[64,896]{1,0:T(8,128)(2,1)S(1)} %add_convert_fusion.refs_4_), channel_id=1, source_target_pairs={{0,2},{1,3},{2,0},{3,1},{4,6},{5,7},{6,4},{7,5},{8,10},{9,11},{10,... | collective-permute-start | bytes 344072 | tf_op jit(solution)/shard_map/ppermute | solution.py:348
  48.1 0.0 collective-permute-done.8.refs_2_
  48.1 2.2 %collective-permute-done.15.refs_7_ = bf16[64,896]{1,0:T(8,128)(2,1)S(1)} collective-permute-done((bf16[64,896]{1,0:T(8,128)(2,1)S(1)}, bf16[64,896]{1,0:T(8,128)(2,1)S(1)}, u32[]{:S(2)}, u32[]{:S(2)}) %collective-permute-start.15) | collective-permute-done | bytes 114720 | tf_op jit(solution)/shard_map/ppermute | solution.py:348
  50.3 0.7 %collective-permute-done.14.refs_6_ = bf16[64,896]{1,0:T(8,128)(2,1)S(1)} collective-permute-done((bf16[64,896]{1,0:T(8,128)(2,1)S(1)}, bf16[64,896]{1,0:T(8,128)(2,1)S(1)}, u32[]{:S(2)}, u32[]{:S(2)}) %collective-permute-start.14) | collective-permute-done | bytes 114720 | tf_op jit(solution)/shard_map/ppermute | solution.py:348
  50.9 0.8 %collective-permute-done.13.refs_5_ = bf16[64,896]{1,0:T(8,128)(2,1)S(1)} collective-permute-done((bf16[64,896]{1,0:T(8,128)(2,1)S(1)}, bf16[64,896]{1,0:T(8,128)(2,1)S(1)}, u32[]{:S(2)}, u32[]{:S(2)}) %collective-permute-start.13) | collective-permute-done | bytes 114720 | tf_op jit(solution)/shard_map/ppermute | solution.py:348
  51.7 0.1 maximum_maximum_fusion
  51.8 0.1 collective-permute-start.16
  51.9 2.4 %collective-permute-done.16.refs_3_.refs_8_ = bf16[256,1664]{1,0:T(8,128)(2,1)S(1)} collective-permute-done((bf16[256,1664]{1,0:T(8,128)(2,1)S(1)}, bf16[256,1664]{1,0:T(8,128)(2,1)S(1)}, u32[]{:S(2)}, u32[]{:S(2)}) %collective-permute-start.16) | collective-permute-done | bytes 852000 | tf_op jit(solution)/shard_map/ppermute | solution.py:348
  54.2 1.3 %shard_map.97 = (bf16[3,512,512]{2,1,0:T(8,128)(2,1)}, bf16[50,512]{1,0:T(8,128)(2,1)}) custom-call(bf16[64,768]{1,0:T(8,128)(2,1)S(1)} %add_convert_fusion.2.refs_0_, bf16[64,768]{1,0:T(8,128)(2,1)S(1)} %collective-permute-done.7.refs_1_, bf16[128,768]{1,0:T(8,128)(2,1)S(1)} %collective-permute-done.8.refs_2_, ...), custom_call_target="tpu_custom_call" | custom-call | bytes 4179968 | tf_op jit(solution)/shard_map/pallas_call | solution.py:25
  (8 shorter events, 0.2 us)
Async XLA Ops:
  3.1 8.6 %collective-permute-start.1 = (bf16[256,256]{1,0:T(8,128)(2,1)S(1)}, bf16[256,256]{1,0:T(8,128)(2,1)S(1)}, u32[]{:S(2)}, u32[]{:S(2)}) collective-permute-start(bf16[256,256]{1,0:T(8,128)(2,1)S(1)} %get-tuple-element.49), channel_id=1, source_target_pairs={{16,0},{0,16},{17,1},{1,17},{18,2},{2,18},{19,3},{3,19},{20,4},{4,... | collective-permute-start | bytes 393224 | tf_op jit(solution)/shard_map/ppermute | solution.py:414
  7.4 7.1 %collective-permute-start.2 = (bf16[256,256]{1,0:T(8,128)(2,1)S(1)}, bf16[256,256]{1,0:T(8,128)(2,1)S(1)}, u32[]{:S(2)}, u32[]{:S(2)}) collective-permute-start(bf16[256,256]{1,0:T(8,128)(2,1)S(1)} %get-tuple-element.50), channel_id=1, source_target_pairs={{16,0},{0,16},{17,1},{1,17},{18,2},{2,18},{19,3},{3,19},{20,4},{4,... | collective-permute-start | bytes 393224 | tf_op jit(solution)/shard_map/ppermute | solution.py:414
  8.9 10.4 %collective-permute-start = (bf16[512,256]{1,0:T(8,128)(2,1)S(1)}, bf16[512,256]{1,0:T(8,128)(2,1)S(1)}, u32[]{:S(2)}, u32[]{:S(2)}) collective-permute-start(bf16[512,256]{1,0:T(8,128)(2,1)S(1)} %shard_map.88), channel_id=1, source_target_pairs={{16,0},{0,16},{17,1},{1,17},{18,2},{2,18},{19,3},{3,19},{20,4},{4,... | collective-permute-start | bytes 786440 | tf_op jit(solution)/shard_map/ppermute | solution.py:414
  15.2 1.8 %collective-permute-start.3 = (bf16[256,768]{1,0:T(8,128)(2,1)S(1)}, bf16[256,768]{1,0:T(8,128)(2,1)S(1)}, u32[]{:S(2)}, u32[]{:S(2)}) collective-permute-start(bf16[256,768]{1,0:T(8,128)(2,1)S(1)} %get-tuple-element.54), channel_id=1, source_target_pairs={{0,1},{1,0},{2,3},{3,2},{4,5},{5,4},{6,7},{7,6},{8,9},{9,8},{10,11... | collective-permute-start | bytes 1179656 | tf_op jit(solution)/shard_map/ppermute | solution.py:348
  17.1 5.7 %collective-permute-start.4 = (bf16[128,768]{1,0:T(8,128)(2,1)S(1)}, bf16[128,768]{1,0:T(8,128)(2,1)S(1)}, u32[]{:S(2)}, u32[]{:S(2)}) collective-permute-start(bf16[128,768]{1,0:T(8,128)(2,1)S(1)} %get-tuple-element.56), channel_id=1, source_target_pairs={{0,2},{1,5},{2,0},{3,7},{4,6},{5,1},{6,4},{7,3},{8,10},{9,13},{10,... | collective-permute-start | bytes 589832 | tf_op jit(solution)/shard_map/ppermute | solution.py:348
  22.8 1.8 %collective-permute-start.9 = (bf16[256,896]{1,0:T(8,128)(2,1)S(1)}, bf16[256,896]{1,0:T(8,128)(2,1)S(1)}, u32[]{:S(2)}, u32[]{:S(2)}) collective-permute-start(bf16[256,896]{1,0:T(8,128)(2,1)S(1)} %get-tuple-element.61), channel_id=1, source_target_pairs={{0,1},{1,0},{2,3},{3,2},{4,5},{5,4},{6,7},{7,6},{8,9},{9,8},{10,11... | collective-permute-start | bytes 1376264 | tf_op jit(solution)/shard_map/ppermute | solution.py:348
  22.9 4.7 %collective-permute-start.5 = (bf16[64,768]{1,0:T(8,128)(2,1)S(1)}, bf16[64,768]{1,0:T(8,128)(2,1)S(1)}, u32[]{:S(2)}, u32[]{:S(2)}) collective-permute-start(bf16[64,768]{1,0:T(8,128)(2,1)S(1)} %get-tuple-element.58), channel_id=1, source_target_pairs={{0,4},{1,3},{2,6},{3,1},{4,0},{5,7},{6,2},{7,5},{8,12},{9,11},{10,... | collective-permute-start | bytes 294920 | tf_op jit(solution)/shard_map/ppermute | solution.py:348
  24.8 6.1 %collective-permute-start.10 = (bf16[128,896]{1,0:T(8,128)(2,1)S(1)}, bf16[128,896]{1,0:T(8,128)(2,1)S(1)}, u32[]{:S(2)}, u32[]{:S(2)}) collective-permute-start(bf16[128,896]{1,0:T(8,128)(2,1)S(1)} %get-tuple-element.63), channel_id=1, source_target_pairs={{0,2},{1,5},{2,0},{3,7},{4,6},{5,1},{6,4},{7,3},{8,10},{9,13},{10,... | collective-permute-start | bytes 688136 | tf_op jit(solution)/shard_map/ppermute | solution.py:348
  27.6 7.7 %collective-permute-start.6 = (bf16[64,768]{1,0:T(8,128)(2,1)S(1)}, bf16[64,768]{1,0:T(8,128)(2,1)S(1)}, u32[]{:S(2)}, u32[]{:S(2)}) collective-permute-start(bf16[64,768]{1,0:T(8,128)(2,1)S(1)} %add_convert_fusion.3), channel_id=1, source_target_pairs={{0,8},{1,9},{2,10},{3,11},{4,12},{5,13},{6,14},{7,15},{8,0},{9,1},... | collective-permute-start | bytes 294920 | tf_op jit(solution)/shard_map/ppermute | solution.py:348
  30.9 5.5 %collective-permute-start.11 = (bf16[64,896]{1,0:T(8,128)(2,1)S(1)}, bf16[64,896]{1,0:T(8,128)(2,1)S(1)}, u32[]{:S(2)}, u32[]{:S(2)}) collective-permute-start(bf16[64,896]{1,0:T(8,128)(2,1)S(1)} %get-tuple-element.65), channel_id=1, source_target_pairs={{0,4},{1,3},{2,6},{3,1},{4,0},{5,7},{6,2},{7,5},{8,12},{9,11},{10,... | collective-permute-start | bytes 344072 | tf_op jit(solution)/shard_map/ppermute | solution.py:348
  35.3 4.8 %collective-permute-start.7 = (bf16[64,768]{1,0:T(8,128)(2,1)S(1)}, bf16[64,768]{1,0:T(8,128)(2,1)S(1)}, u32[]{:S(2)}, u32[]{:S(2)}) collective-permute-start(bf16[64,768]{1,0:T(8,128)(2,1)S(1)} %add_convert_fusion.2.refs_0_), channel_id=1, source_target_pairs={{0,4},{1,3},{2,6},{3,1},{4,0},{5,7},{6,2},{7,5},{8,12},{9,11},{10,... | collective-permute-start | bytes 294920 | tf_op jit(solution)/shard_map/ppermute | solution.py:348
  36.5 8.0 %collective-permute-start.12 = (bf16[64,896]{1,0:T(8,128)(2,1)S(1)}, bf16[64,896]{1,0:T(8,128)(2,1)S(1)}, u32[]{:S(2)}, u32[]{:S(2)}) collective-permute-start(bf16[64,896]{1,0:T(8,128)(2,1)S(1)} %add_convert_fusion.1), channel_id=1, source_target_pairs={{0,8},{1,9},{2,10},{3,11},{4,12},{5,13},{6,14},{7,15},{8,0},{9,1},... | collective-permute-start | bytes 344072 | tf_op jit(solution)/shard_map/ppermute | solution.py:348
  40.1 8.0 %collective-permute-start.8 = (bf16[128,768]{1,0:T(8,128)(2,1)S(1)}, bf16[128,768]{1,0:T(8,128)(2,1)S(1)}, u32[]{:S(2)}, u32[]{:S(2)}) collective-permute-start(bf16[128,768]{1,0:T(8,128)(2,1)S(1)} %pad_maximum_fusion), channel_id=1, source_target_pairs={{0,2},{1,5},{2,0},{3,7},{4,6},{5,1},{6,4},{7,3},{8,10},{9,13},{10,... | collective-permute-start | bytes 589832 | tf_op jit(solution)/shard_map/ppermute | solution.py:348
  44.5 5.8 %collective-permute-start.15 = (bf16[64,896]{1,0:T(8,128)(2,1)S(1)}, bf16[64,896]{1,0:T(8,128)(2,1)S(1)}, u32[]{:S(2)}, u32[]{:S(2)}) collective-permute-start(bf16[64,896]{1,0:T(8,128)(2,1)S(1)} %add_convert_fusion.refs_4_), channel_id=1, source_target_pairs={{0,6},{1,7},{2,4},{3,5},{4,2},{5,3},{6,0},{7,1},{8,14},{9,15},{10,... | collective-permute-start | bytes 344072 | tf_op jit(solution)/shard_map/ppermute | solution.py:348
  45.0 5.9 %collective-permute-start.14 = (bf16[64,896]{1,0:T(8,128)(2,1)S(1)}, bf16[64,896]{1,0:T(8,128)(2,1)S(1)}, u32[]{:S(2)}, u32[]{:S(2)}) collective-permute-start(bf16[64,896]{1,0:T(8,128)(2,1)S(1)} %add_convert_fusion.refs_4_), channel_id=1, source_target_pairs={{0,4},{1,5},{2,6},{3,7},{4,0},{5,1},{6,2},{7,3},{8,12},{9,13},{10,... | collective-permute-start | bytes 344072 | tf_op jit(solution)/shard_map/ppermute | solution.py:348
  46.9 4.8 %collective-permute-start.13 = (bf16[64,896]{1,0:T(8,128)(2,1)S(1)}, bf16[64,896]{1,0:T(8,128)(2,1)S(1)}, u32[]{:S(2)}, u32[]{:S(2)}) collective-permute-start(bf16[64,896]{1,0:T(8,128)(2,1)S(1)} %add_convert_fusion.refs_4_), channel_id=1, source_target_pairs={{0,2},{1,3},{2,0},{3,1},{4,6},{5,7},{6,4},{7,5},{8,10},{9,11},{10,... | collective-permute-start | bytes 344072 | tf_op jit(solution)/shard_map/ppermute | solution.py:348
  51.8 2.4 %collective-permute-start.16 = (bf16[256,1664]{1,0:T(8,128)(2,1)S(1)}, bf16[256,1664]{1,0:T(8,128)(2,1)S(1)}, u32[]{:S(2)}, u32[]{:S(2)}) collective-permute-start(bf16[256,1664]{1,0:T(8,128)(2,1)S(1)} %maximum_maximum_fusion), channel_id=1, source_target_pairs={{0,1},{1,0},{2,3},{3,2},{4,5},{5,4},{6,7},{7,6},{8,9},{9,8},{10,11... | collective-permute-start | bytes 2555912 | tf_op jit(solution)/shard_map/ppermute | solution.py:348
